TPU v7x, 512 devices: a whole 4x4x16 slice. The times are simulated.
512 devices in a mesh: seq: 128 (over y, z, core), chan: 4 (over x).
Axes of the slice: x: 4, y: 4, z: 16, core: 2. Of those that a mesh axis runs over, the one named last changes fastest.
Arguments:
- stream: bfloat16 [32768, 4096], P('seq', 'chan'), may hold values from -60 to 60
- norm_gain: float32 [4096], P('chan'), may hold values from 0.1 to 1.9
- gate_query: bfloat16 [32768, 4096], P('seq', 'chan'), may hold values from -6 to 6
- gate_key: bfloat16 [32768, 4096], P('seq', 'chan'), may hold values from -6 to 6
- gate_out: bfloat16 [32768, 4096], P('seq', 'chan'), may hold values from -6 to 6
- cotangent: bfloat16 [32768, 4096], P('seq', 'chan'), may hold values from -6 to 6
- medium_filter: float32 [128, 4096], P(None, 'chan'), may hold values from -0.53033009 to 0.53033009
- long_residue: float32 [4096], P('chan'), may hold values from 0.5 to 1.5
- long_rate: float32 [4096], P('chan'), may hold values from 9.1552734e-06 to 0.0333333333
Outputs:
- grad_query: bfloat16 [32768, 4096], P('seq', 'chan')
- grad_stream: bfloat16 [32768, 4096], P('seq', 'chan')
- grad_filter: float32 [128, 4096], P(None, 'chan')
- grad_residue: float32 [4096], P('chan')
All inputs are finite; a program needn't handle non-finite values.
Results may differ from a plain program's by a relative error of at most 0.008.
Values sent between devices are 32-bit elements; how exact they have to be, the bound alone decides.
No kernel may reach another device: no remote copies, remote signals or barrier semaphores. Data moves between devices by JAX's collectives and lax.ppermute only.
A program may use at most 64 MiB of HBM per device.

v0:
```python
import jax
import jax.numpy as jnp
from jax import lax
from jax.sharding import PartitionSpec as P

EPSILON = 1e-05


def passed_along(block, axis, distance):
    devices = range(lax.axis_size(axis))
    route = [(i - distance, i) for i in devices if i - distance in devices]
    return lax.ppermute(block, axis, route)


def prefix(value, axis, join, neutral):
    count, mine = (lax.axis_size(axis), lax.axis_index(axis))
    pieces = jax.tree.map(lambda part: lax.all_gather(part, axis), value)
    pieces = jax.tree.map(lambda part: part[::-1], pieces)
    mine = count - 1 - mine
    subtotal = jax.tree.map(
        lambda part, zero: jnp.full_like(part, 0) + jnp.asarray(zero, part.dtype), value, neutral
    )

    def hop(position, subtotal):
        longer = join(subtotal, jax.tree.map(lambda part: part[position], pieces))
        return jax.tree.map(lambda new, old: jnp.where(position < mine, new, old), longer, subtotal)

    return lax.fori_loop(0, count - 1, hop, subtotal)


def linked(first_pair, second_pair):
    return (first_pair[0] * second_pair[0], first_pair[1] * second_pair[0] + second_pair[1])


def running(values, decay_row):
    factors = jnp.broadcast_to(decay_row, values.shape)
    return lax.associative_scan(linked, (factors, values), reverse=True, axis=0)[1]


def depthwise(extended, kernel):
    result = lax.conv_general_dilated(
        extended[None],
        kernel[:, None, :],
        (1,),
        "VALID",
        dimension_numbers=("NWC", "WIO", "NWC"),
        feature_group_count=extended.shape[1],
        precision=lax.Precision.HIGHEST,
    )
    return result[0]


def body(
    stream,
    norm_gain,
    gate_query,
    gate_key,
    gate_out,
    cotangent,
    medium_filter,
    long_residue,
    long_rate,
):
    row_count, chan_count = stream.shape
    tap_count = medium_filter.shape[0]
    rim_width = tap_count - 1
    token_count = row_count * lax.axis_size("seq")
    channel_total = chan_count * lax.axis_size("chan")
    grad_scale = token_count ** (-0.5)
    inputs = stream.astype(jnp.float32)
    squares = lax.psum(jnp.sum(inputs * inputs, axis=1), "chan")
    inv_rms = lax.rsqrt(squares / channel_total + EPSILON)[:, None]
    normed = inputs * inv_rms * norm_gain
    key_rows = gate_key.astype(jnp.float32)
    query_rows = gate_query.astype(jnp.float32)
    product = key_rows * normed
    before_rim = passed_along(product[row_count - rim_width :], "seq", 1)
    product_ext = jnp.concatenate([before_rim, product], axis=0)
    mixed_rows = depthwise(product_ext, medium_filter[::-1])
    stored = (query_rows * mixed_rows).astype(jnp.bfloat16)
    normalizer = jnp.sqrt(-jnp.expm1(-2.0 * long_rate))
    step_decay = jnp.exp(-long_rate)
    block_decay = jnp.exp(-long_rate * row_count)
    grad_source = gate_out.astype(jnp.float32) * cotangent.astype(jnp.float32)
    local_reverse = running(grad_source, step_decay)
    position = jnp.arange(row_count, dtype=jnp.float32)[:, None]
    identity = (jnp.ones_like(block_decay), jnp.zeros_like(block_decay))
    later_state = prefix((block_decay, local_reverse[0]), "seq", linked, identity)[1]
    reverse_state = local_reverse + jnp.exp(-long_rate * (row_count - position)) * later_state
    grad_stored = long_residue * normalizer * reverse_state
    grad_query = (mixed_rows * grad_stored).astype(jnp.bfloat16)
    grad_mixed = query_rows * grad_stored
    after_rim = passed_along(grad_mixed[:rim_width], "seq", -1)
    grad_product = depthwise(jnp.concatenate([grad_mixed, after_rim], axis=0), medium_filter)
    weighted = norm_gain * key_rows * grad_product
    row_dots = lax.psum(jnp.sum(weighted * inputs, axis=1), "chan")
    grad_stream = (
        inv_rms * (weighted - inputs * inv_rms * inv_rms * (row_dots / channel_total)[:, None])
    ).astype(jnp.bfloat16)
    filter_local = depthwise(product_ext, grad_mixed)[::-1]
    residue_local = normalizer * jnp.sum(stored.astype(jnp.float32) * reverse_state, axis=0)
    filter_sum, residue_sum = lax.psum((filter_local, residue_local), "seq")
    return (grad_query, grad_stream, filter_sum * grad_scale, residue_sum * grad_scale)


def solution(mesh):
    in_specs = (
        P("seq", "chan"),
        P("chan"),
        P("seq", "chan"),
        P("seq", "chan"),
        P("seq", "chan"),
        P("seq", "chan"),
        P(None, "chan"),
        P("chan"),
        P("chan"),
    )
    out_specs = (P("seq", "chan"), P("seq", "chan"), P(None, "chan"), P("chan"))
    return jax.shard_map(body, mesh=mesh, in_specs=in_specs, out_specs=out_specs, check_vma=False)
```

profile of v0, /device:TPU:1, one launch (start us, length us, event | category | flops | bytes accessed | tf_op | source)
XLA Modules:
  0.0 602.5 jit_solution(791053334205475690)
XLA Ops:
  7.2 1.4 convert_multiply_fusion.7
  9.7 2.6 slice.215
  12.4 1.2 multiply_add_fusion.1
  17.4 1.5 slice.270
  20.3 3.5 slice.271
  24.5 91.3 %all-gather.1 = f32[128,1,1024]{2,1,0:T(1,128)S(1)} all-gather(f32[1,1,1024]{2,1,0:T(1,128)S(1)} %add_bitcast_fusion), channel_id=1, replica_groups=mesh['seq'=128,'chan'=4] {'seq'}, dimensions={0}, use_global_device_ids=true | all-gather | bytes 528384 | tf_op jit(solution)/shard_map/all_gather | solution.py:17
  116.1 81.9 %all-gather = f32[131072]{0:T(1024)S(1)} all-gather(f32[1024]{0:T(1024)S(1)} %get-tuple-element.155), channel_id=2, replica_groups=mesh['seq'=128,'chan'=4] {'seq'}, dimensions={0}, use_global_device_ids=true | all-gather | bytes 528384 | tf_op jit(solution)/shard_map/all_gather | solution.py:17
  198.4 7.6 %while.14 = (s32[]{:T(128)}, f32[1024]{0:T(1024)S(1)}, s32[]{:T(128)}, f32[128,1024]{1,0:T(8,128)S(1)}, f32[128,1024]{1,0:T(8,128)S(1)}, /*index=5*/s32[]{:T(128)}, s32[]{:T(128)}) while((s32[]{:T(128)}, f32[1024]{0:T(1024)S(1)}, s32[]{:T(128)}, f32[128,1024]{1,0:T(8,128)S(1)}, f32[128,1024]{1,0:T(8,128)S(1)}, ...), condition=%wide.region_3.4_spmd.clone, body=%wide.region_2.3_spmd.clone.sunk | while | flops 4100 | bytes 32869 | solution.py:28
  206.9 2.4 collective-permute-start.1
  209.3 8.2 %collective-permute-done.1 = f32[127,1024]{1,0:T(8,128)S(1)} collective-permute-done((f32[127,1024]{1,0:T(8,128)S(1)}, f32[127,1024]{1,0:T(8,128)S(1)}, u32[]{:S(2)}, u32[]{:S(2)}) %collective-permute-start.1) | collective-permute-done | bytes 520224 | tf_op jit(solution)/shard_map/ppermute | solution.py:12
  217.8 10.6 %fusion = f32[1,256,1024]{2,0,1:T(1,128)S(1)} fusion(f32[1,383,1024]{2,1,0:T(8,128)S(1)} %maximum_bitcast_fusion, f32[128,1,1024]{2,0,1:T(8,128)S(1)} %bitcast.37), kind=kOutput, calls=%fused_computation.8 | convolution fusion | flops 402653184 | bytes 3141632 | tf_op jit(solution)/shard_map/conv_general_dilated | solution.py:41
  229.8 8.5 %all-reduce.16 = (f32[256]{0:T(256)S(1)}, f32[256]{0:T(256)S(1)}) all-reduce(f32[256]{0:T(256)S(1)} %get-tuple-element.118, f32[256]{0:T(256)S(1)} %get-tuple-element.117), channel_id=1, replica_groups=mesh['seq'=128,'chan'=4] {'chan'}, use_global_device_ids=true, to_apply=%region_1.0 | all-reduce | flops 512 | bytes 4096 | tf_op jit(solution)/shard_map/psum | solution.py:71
  238.3 2.8 fusion.7
  241.9 3.8 collective-permute-start
  245.6 4.7 rev.17
  250.4 1.7 collective-permute-done
  252.1 1.2 pad_maximum_fusion
  254.4 10.5 %fusion.13 = f32[1,128,1024]{2,0,1:T(1,128)S(1)} fusion(f32[1,383,1024]{2,0,1:T(1,128)S(1)} %broadcast_in_dim.12, f32[256,1,1024]{2,0,1:T(8,128)S(1)} %bitcast.34), kind=kOutput, calls=%fused_computation.26 | convolution fusion | flops 402653184 | bytes 3141632 | tf_op jit(solution)/shard_map/conv_general_dilated | solution.py:41
  265.1 2.6 rev.21
  267.7 11.3 %fusion.17 = f32[1,256,1024]{2,0,1:T(1,128)S(1)} fusion(f32[1,383,1024]{2,0,1:T(1,128)S(1)} %copy-done.6, f32[128,1,1024]{2,0,1:T(8,128)} %bitcast.38), kind=kOutput, calls=%fused_computation.37 | convolution fusion | flops 402653184 | bytes 3141632 | tf_op jit(solution)/shard_map/conv_general_dilated | solution.py:41
  279.0 1.3 multiply_reduce_fusion
  280.4 244.9 %psum.31 = f32[1024]{0:T(1024)S(1)} all-reduce(f32[1024]{0:T(1024)S(1)} %fusion.27), channel_id=1, replica_groups=mesh['seq'=128,'chan'=4] {'seq'}, use_global_device_ids=true, to_apply=%region_8.9 | all-reduce | flops 1024 | bytes 8192 | tf_op jit(solution)/shard_map/psum | solution.py:102
  525.9 67.9 %all-reduce.19.cloned.1.call-done = f32[128,1024]{1,0:T(8,128)} async-done(((f32[128,1024]{1,0:T(8,128)}), f32[128,1024]{1,0:T(8,128)}) %all-reduce.19.cloned.1.call-update) | async-done | bytes 524304 | tf_op jit(solution)/shard_map/psum | solution.py:102
  593.7 1.9 broadcast_multiply_fusion
  (387 shorter events, 15.2 us)
Async XLA Ops:
  7.2 2.0 copy-start.10
  7.2 2.0 copy-start.8
  7.2 586.6 %all-reduce.19.cloned.1.call-start = ((), (), s32[]{:S(2)}) async-start(), calls=%async_computation | async-start | bytes 1048576 | tf_op jit(solution)/shard_map/psum | solution.py:102
  198.1 8.4 %copy-start.3 = (bf16[256,1024]{1,0:T(8,128)(2,1)S(1)}, bf16[256,1024]{1,0:T(8,128)(2,1)}, u32[]{:S(2)}) copy-start(bf16[256,1024]{1,0:T(8,128)(2,1)} %param.13) | copy-start | bytes 1572868
  206.9 10.8 %copy-start.7 = (f32[128,1024]{1,0:T(8,128)S(1)}, f32[128,1024]{1,0:T(8,128)}, u32[]{:S(2)}) copy-start(f32[128,1024]{1,0:T(8,128)} %param.17) | copy-start | bytes 1572868
  206.9 10.6 %collective-permute-start.1 = (f32[127,1024]{1,0:T(8,128)S(1)}, f32[127,1024]{1,0:T(8,128)S(1)}, u32[]{:S(2)}, u32[]{:S(2)}) collective-permute-start(f32[127,1024]{1,0:T(8,128)S(1)} %slice.304), channel_id=1, source_target_pairs={{4,0},{8,4},{12,8},{16,12},{20,16},{24,20},{28,24},{32,28},{36,32}... | collective-permute-start | bytes 1560584 | tf_op jit(solution)/shard_map/ppermute | solution.py:12
  217.7 11.6 %copy-start.1 = (bf16[256,1024]{1,0:T(8,128)(2,1)S(1)}, bf16[256,1024]{1,0:T(8,128)(2,1)}, u32[]{:S(2)}) copy-start(bf16[256,1024]{1,0:T(8,128)(2,1)} %param.11) | copy-start | bytes 1572868
  217.7 11.6 %copy-start.2 = (bf16[256,1024]{1,0:T(8,128)(2,1)S(1)}, bf16[256,1024]{1,0:T(8,128)(2,1)}, u32[]{:S(2)}) copy-start(bf16[256,1024]{1,0:T(8,128)(2,1)} %param.14) | copy-start | bytes 1572868
  217.8 11.6 %copy-start.9 = (f32[1024]{0:T(1024)S(1)}, f32[1024]{0:T(1024)}, u32[]{:S(2)}) copy-start(f32[1024]{0:T(1024)} %param.12) | copy-start | bytes 12292
  228.4 1.0 copy-start
  241.9 10.2 %collective-permute-start = (f32[127,1024]{1,0:T(8,128)}, f32[127,1024]{1,0:T(8,128)}, u32[]{:S(2)}, u32[]{:S(2)}) collective-permute-start(f32[127,1024]{1,0:T(8,128)} %slice.274), channel_id=1, source_target_pairs={{0,4},{4,8},{8,12},{12,16},{16,20},{20,24},{24,28},{28,32},{32,36}... | collective-permute-start | bytes 1560584 | tf_op jit(solution)/shard_map/ppermute | solution.py:12
  254.4 10.5 %copy-start.5 = (f32[1,383,1024]{2,0,1:T(1,128)}, f32[1,383,1024]{2,0,1:T(1,128)S(1)}, u32[]{:S(2)}) copy-start(f32[1,383,1024]{2,0,1:T(1,128)S(1)} %broadcast_in_dim.12) | copy-start | bytes 4706308
  265.0 2.7 copy-start.6
  267.7 11.3 %copy-start.4 = (bf16[256,1024]{1,0:T(8,128)(2,1)S(1)}, bf16[256,1024]{1,0:T(8,128)(2,1)}, u32[]{:S(2)}) copy-start(bf16[256,1024]{1,0:T(8,128)(2,1)} %param.13) | copy-start | bytes 1572868
Sparse Core Ops, SparseCore 0:
  267.8 325.8 all-reduce.18
where the time goes:
time: 603 us; the launch traced here: 602 us
  blocking collectives  427 us (71%)
  waiting for transfers between devices  77.8 us (13%)
  matrix products  32.4 us (5%)
  local copies, waits for them, and re-layouts  25.6 us (4%)
  between operations  14.9 us (2%)
  other arithmetic  14.3 us (2%)
  starting transfers between devices  6.19 us (1%)
    psum x1, blocking collectives, body(): filter_sum, residue_sum = lax.psum((filter_local, residue_local), 'seq')  245 us
    all_gather x2, blocking collectives, prefix(): pieces = jax.tree.map(lambda part: lax.all_gather(part, axis), value)  173 us
    psum x1, waiting for transfers between devices, body(): filter_sum, residue_sum = lax.psum((filter_local, residue_local), 'seq')  67.9 us
    conv_general_dilated x3, matrix products, depthwise(): lax.conv_general_dilated(extended[None], kernel[:, None, :], (1,), 'VALID...  32.4 us
  transfers between devices with their start and end apart: 3, of which 3 were waited for; matrix products, arithmetic and copies ran while one was open for 3% of the time, Pallas kernels for 0%

commit v1 on v0

v1 whole, which is shorter than its diff:
```python
import jax
import jax.numpy as jnp
import numpy as np
from jax import lax
from jax.experimental import pallas as pl
from jax.experimental.pallas import tpu as pltpu
from jax.sharding import Mesh, PartitionSpec as P

EPSILON = 1e-05
ROWS = 256
TAPS = 128
CHANS = 1024
TOKENS = 32768
CHANNEL_TOTAL = 4096
LANES = 128
TILES = CHANS // LANES
POINTS = ROWS + TAPS
HALF = POINTS // 2
Y, Z = (4, 16)
PLANE = Y * Z
F32 = jnp.float32
BF16 = jnp.bfloat16


def transform_tables():
    k = np.arange(HALF, dtype=np.int64)[:, None]
    n = np.arange(POINTS, dtype=np.int64)[None, :]
    angle = np.pi * (((2 * k + 1) * n) % (2 * POINTS)).astype(np.float64) / POINTS
    table = np.concatenate([np.cos(angle), -np.sin(angle)], axis=0)
    forward = table.astype(BF16)
    inverse = np.ascontiguousarray(table.T).astype(BF16)
    lags = np.ascontiguousarray(table.T[TAPS:0:-1]).astype(BF16)
    return forward, inverse, lags


def call(kernel, outs, *args, specs=None, flops=0):
    vmem = pl.BlockSpec(memory_space=pltpu.VMEM)
    sizes = [a.size * a.dtype.itemsize for a in args]
    sizes += [int(np.prod(o.shape)) * o.dtype.itemsize for o in outs]
    result = pl.pallas_call(
        kernel,
        out_shape=tuple(outs),
        in_specs=[vmem] * len(args) if specs is None else specs,
        out_specs=tuple([vmem] * len(outs)),
        compiler_params=pltpu.CompilerParams(vmem_limit_bytes=40 * 1024 * 1024),
        cost_estimate=pl.CostEstimate(
            flops=flops, bytes_accessed=sum(sizes), transcendentals=0
        ),
    )(*args)
    return result


def shape(dims, dtype=F32):
    return jax.ShapeDtypeStruct(dims, dtype)


SMEM = pl.BlockSpec(memory_space=pltpu.SMEM)
VMEM = pl.BlockSpec(memory_space=pltpu.VMEM)


def dot(a, b):
    return lax.dot_general(
        a, b, (((1,), (0,)), ((), ())), preferred_element_type=F32
    )


def lane_tile(tile):
    return slice(tile * LANES, (tile + 1) * LANES)


def row_scale(total):
    inv = lax.rsqrt(total / CHANNEL_TOTAL + EPSILON)
    return jnp.broadcast_to(inv, (LANES, ROWS)).T


def head_kernel(out_ref, cot_ref, rate_ref, first_ref):
    rank = lax.broadcasted_iota(jnp.int32, (8, LANES), 0).astype(F32)
    for tile in range(TILES):
        cols = lane_tile(tile)
        rate = rate_ref[tile : tile + 1, :]
        source = out_ref[:, cols].astype(F32) * cot_ref[:, cols].astype(F32)
        eight = jnp.exp(-8.0 * rate)
        total = source[ROWS - 8 :, :]
        for group in range(ROWS // 8 - 2, -1, -1):
            total = total * eight + source[group * 8 : group * 8 + 8, :]
        total = total * jnp.exp(-rate * rank)
        first_ref[tile : tile + 1, :] = jnp.sum(total, axis=0, keepdims=True)


def pair_kernel(core_ref, own_ref, other_ref, rate_ref, spread_ref):
    decay = jnp.exp(-ROWS * rate_ref[...])
    own, other = (own_ref[...], other_ref[...])
    is_first = core_ref[0] == 0
    low = jnp.where(is_first, own, other)
    high = jnp.where(is_first, other, own)
    spread_ref[...] = jnp.broadcast_to(low + decay * high, spread_ref.shape)


def squares_kernel(stream_ref, total_ref):
    acc = jnp.zeros((ROWS, LANES), F32)
    for tile in range(TILES):
        value = stream_ref[:, lane_tile(tile)].astype(F32)
        acc = acc + value * value
    total_ref[...] = jnp.sum(acc.T, axis=0, keepdims=True)


def product_kernel(total_ref, stream_ref, key_ref, gain_ref, product_ref, rim_ref):
    inv = row_scale(total_ref[...])
    for tile in range(TILES):
        cols = lane_tile(tile)
        normed = stream_ref[:, cols].astype(F32) * inv * gain_ref[tile : tile + 1, :]
        product = key_ref[:, cols].astype(F32) * normed
        product_ref[:, cols] = product.astype(BF16)
        rim_ref[:, cols] = product[ROWS - TAPS :, :]


def scan_kernel(out_ref, cot_ref, rate_ref, local_ref):
    rank = lax.broadcasted_iota(jnp.int32, (8, LANES), 0)
    for tile in range(TILES):
        cols = lane_tile(tile)
        rate = rate_ref[tile : tile + 1, :]
        source = out_ref[:, cols].astype(F32) * cot_ref[:, cols].astype(F32)
        coefs = [
            (s, jnp.where(rank < 8 - s, jnp.exp(-float(s) * rate), 0.0)) for s in (1, 2, 4)
        ]
        power = jnp.exp(-rate * (8 - rank).astype(F32))
        carry = jnp.zeros((1, LANES), F32)
        for group in range(ROWS // 8 - 1, -1, -1):
            value = source[group * 8 : group * 8 + 8, :]
            for s, coef in coefs:
                value = value + coef * pltpu.roll(value, 8 - s, 0)
            value = value + power * carry
            local_ref[group * 8 : group * 8 + 8, cols] = value
            carry = value[0:1, :]


def mul_conj(a, b):
    ar, ai = (a[:HALF], a[HALF:])
    br, bi = (b[:HALF], b[HALF:])
    return jnp.concatenate([ar * br + ai * bi, ar * bi - ai * br], axis=0).astype(BF16)


def mul(a, b):
    ar, ai = (a[:HALF], a[HALF:])
    br, bi = (b[:HALF], b[HALF:])
    return jnp.concatenate([ar * br - ai * bi, ar * bi + ai * br], axis=0).astype(BF16)


def tail_decay(rate):
    rows = lax.broadcasted_iota(jnp.int32, (8, LANES), 0)
    power = jnp.exp(-rate * (8 - rows).astype(F32))
    groups = []
    for group in range(ROWS // 8):
        groups.append(power * jnp.exp(-rate * float(ROWS - 8 - 8 * group)))
    return jnp.concatenate(groups, axis=0)


def filter_kernel(
    fwd_ref, lag_ref, product_ref, rim_ref, local_ref, query_ref, rate_ref, residue_ref, a_ref, b_ref
):
    for tile in range(TILES):
        cols = lane_tile(tile)
        rate = rate_ref[tile : tile + 1, :]
        scale = residue_ref[tile : tile + 1, :]
        ext = jnp.concatenate([rim_ref[:, cols].astype(BF16), product_ref[:, cols]], axis=0)
        product = dot(fwd_ref[...], ext)
        query = query_ref[:, cols].astype(F32) * scale
        first = (query * local_ref[:, cols]).astype(BF16)
        second = (query * tail_decay(rate)).astype(BF16)
        for part, ref in ((first, a_ref), (second, b_ref)):
            spectrum = dot(fwd_ref[:, :ROWS], part)
            taps = dot(lag_ref[...], mul_conj(spectrum, product))
            for group in range(TAPS // 8):
                ref[group * TILES + tile] = taps[group * 8 : group * 8 + 8, :]


def carry_kernel(place_ref, pairs_ref, own_ref, other_ref, rate_ref, carry_ref):
    chip, core = (place_ref[0], place_ref[1])
    rate = rate_ref[...]
    carry = jnp.zeros_like(rate)
    for later in range(1, PLANE):
        gap = later - chip - 1
        weight = jnp.exp(-rate * (2.0 * ROWS) * jnp.maximum(gap, 0).astype(F32))
        carry = carry + jnp.where(gap >= 0, weight, 0.0) * pairs_ref[later]
    below = other_ref[...] + jnp.exp(-ROWS * rate) * carry
    carry_ref[...] = jnp.where(core == 0, below, carry)


def join_kernel(core_ref, carry_ref, a_ref, b_ref, keep_ref, send_ref):
    carry = carry_ref[...]
    count = keep_ref.shape[0]
    mine = core_ref[0] * count
    theirs = count - mine
    for group in range(count // TILES):
        for tile in range(TILES):
            at = group * TILES + tile
            row = carry[tile : tile + 1, :]
            send_ref[at] = a_ref[theirs + at] + row * b_ref[theirs + at]
            keep_ref[at] = a_ref[mine + at] + row * b_ref[mine + at]


def add_kernel(a_ref, b_ref, out_ref):
    out_ref[...] = a_ref[...] + b_ref[...]


def spread_sum_kernel(parts_ref, spread_ref):
    total = jnp.sum(parts_ref[...], axis=0)
    spread_ref[...] = jnp.broadcast_to(total, spread_ref.shape)


def finish_kernel(core_ref, own_ref, other_ref, filter_ref, residue_ref, filter_out, residue_out):
    scale = TOKENS ** (-0.5) * 2.0 / POINTS
    count = own_ref.shape[0]
    is_first = core_ref[0] == 0
    for tile in range(TILES):
        cols = lane_tile(tile)
        total = jnp.zeros((8, LANES), F32)
        for group in range(TAPS // 8):
            at = (group * TILES + tile) % count
            low = group * TILES + tile < count
            own, other = (own_ref[at], other_ref[at])
            value = jnp.where(is_first, own, other) if low else jnp.where(is_first, other, own)
            value = value * scale
            rows = slice(group * 8, group * 8 + 8)
            filter_out[rows, cols] = value
            total = total + filter_ref[rows, cols] * value
        total = jnp.sum(total, axis=0, keepdims=True)
        residue_out[tile : tile + 1, :] = total / residue_ref[tile : tile + 1, :]


def query_kernel(
    fwd_ref, inv_ref, product_ref, rim_ref, local_ref, carry_ref, query_ref, filter_ref, rate_ref,
    scale_ref, grad_ref, mixed_grad_ref, head_ref,
):
    for tile in range(TILES):
        cols = lane_tile(tile)
        rate = rate_ref[tile : tile + 1, :]
        ext = jnp.concatenate([rim_ref[:, cols].astype(BF16), product_ref[:, cols]], axis=0)
        product = dot(fwd_ref[...], ext)
        taps = dot(fwd_ref[:, :TAPS], filter_ref[:, cols].astype(BF16))
        mixed = dot(inv_ref[TAPS:, :], mul(product, taps)) * (2.0 / POINTS)
        state = local_ref[:, cols] + tail_decay(rate) * carry_ref[tile : tile + 1, :]
        stored = state * scale_ref[tile : tile + 1, :]
        grad_ref[:, cols] = (mixed * stored).astype(BF16)
        grad_mixed = query_ref[:, cols].astype(F32) * stored
        mixed_grad_ref[:, cols] = grad_mixed.astype(BF16)
        head_ref[:, cols] = grad_mixed[:TAPS]


def weighted_kernel(
    fwd_ref, inv_ref, grad_ref, after_ref, filter_ref, key_ref, stream_ref, gain_ref, weighted_ref, dots_ref
):
    acc = jnp.zeros((ROWS, LANES), F32)
    for tile in range(TILES):
        cols = lane_tile(tile)
        ext = jnp.concatenate([grad_ref[:, cols], after_ref[:, cols].astype(BF16)], axis=0)
        grad = dot(fwd_ref[...], ext)
        taps = dot(fwd_ref[:, :TAPS], filter_ref[:, cols].astype(BF16))
        back = dot(inv_ref[:ROWS, :], mul_conj(taps, grad)) * (2.0 / POINTS)
        weighted = gain_ref[tile : tile + 1, :] * key_ref[:, cols].astype(F32) * back
        weighted_ref[:, cols] = weighted
        acc = acc + weighted * stream_ref[:, cols].astype(F32)
    dots_ref[...] = jnp.sum(acc.T, axis=0, keepdims=True)


def stream_kernel(total_ref, dots_ref, weighted_ref, stream_ref, out_ref):
    inv = row_scale(total_ref[...])
    dots = jnp.broadcast_to(dots_ref[...] / CHANNEL_TOTAL, (LANES, ROWS)).T
    factor = inv * inv * dots
    for tile in range(TILES):
        cols = lane_tile(tile)
        value = weighted_ref[:, cols] - stream_ref[:, cols].astype(F32) * factor
        out_ref[:, cols] = (inv * value).astype(BF16)


def body(
    stream, norm_gain, gate_query, gate_key, gate_out, cotangent, medium_filter, long_residue, long_rate
):
    forward, inverse, lags = (jnp.asarray(t) for t in transform_tables())
    gain = norm_gain.reshape(TILES, LANES)
    rate = long_rate.reshape(TILES, LANES)
    residue = long_residue.reshape(TILES, LANES)
    scale = residue * jnp.sqrt(-jnp.expm1(-2.0 * rate))
    core = lax.axis_index("core").astype(jnp.int32)
    chip = (lax.axis_index("y") * Z + lax.axis_index("z")).astype(jnp.int32)
    core_at = core.reshape(1)
    place = jnp.stack([chip, core])
    plane = ("y", "z")
    seq = ("y", "z", "core")
    swap = [(0, 1), (1, 0)]
    dense = (TILES, LANES)
    full = (ROWS, CHANS)

    (first,) = call(head_kernel, [shape(dense)], gate_out, cotangent, rate)
    other = lax.ppermute(first, "core", swap)
    (spread,) = call(
        pair_kernel, [shape((PLANE,) + dense)], core_at, first, other, rate, specs=[SMEM, VMEM, VMEM, VMEM]
    )
    pairs = lax.all_to_all(spread, plane, 0, 0, tiled=True)

    (squares,) = call(squares_kernel, [shape((1, ROWS))], stream)
    squares = lax.psum(squares, "chan")
    product, rim = call(
        product_kernel, [shape(full, BF16), shape((TAPS, CHANS))], squares, stream, gate_key, gain
    )
    count = 2 * PLANE
    before = lax.ppermute(rim, seq, [(i, i + 1) for i in range(count - 1)])
    (local,) = call(scan_kernel, [shape(full)], gate_out, cotangent, rate)
    tiles = (TAPS // 8 * TILES, 8, LANES)
    part_a, part_b = call(
        filter_kernel, [shape(tiles), shape(tiles)], forward, lags, product, before, local, gate_query,
        rate, scale, flops=2 * CHANS * POINTS * (POINTS + 2 * ROWS + 2 * TAPS),
    )

    (carry,) = call(
        carry_kernel, [shape(dense)], place, pairs, first, other, rate, specs=[SMEM] + [VMEM] * 4
    )

    half = (tiles[0] // 2, 8, LANES)
    keep, send = call(
        join_kernel, [shape(half), shape(half)], core_at, carry, part_a, part_b, specs=[SMEM] + [VMEM] * 3
    )
    got = lax.ppermute(send, "core", swap)
    (chip_sum,) = call(add_kernel, [shape(half)], keep, got)
    parts = lax.all_to_all(chip_sum, plane, 0, 0, tiled=True)
    (spread_sum,) = call(spread_sum_kernel, [shape(half)], parts)
    own_half = lax.all_to_all(spread_sum, plane, 0, 0, tiled=True)
    other_half = lax.ppermute(own_half, "core", swap)
    grad_filter, grad_residue = call(
        finish_kernel, [shape((TAPS, CHANS)), shape(dense)], core_at, own_half, other_half, medium_filter,
        residue, specs=[SMEM] + [VMEM] * 4,
    )

    grad_query, grad_mixed, head = call(
        query_kernel, [shape(full, BF16), shape(full, BF16), shape((TAPS, CHANS))], forward, inverse, product,
        before, local, carry, gate_query, medium_filter, rate, scale,
        flops=2 * CHANS * POINTS * (POINTS + ROWS + TAPS),
    )
    after = lax.ppermute(head, seq, [(i + 1, i) for i in range(count - 1)])
    weighted, dots = call(
        weighted_kernel, [shape(full), shape((1, ROWS))], forward, inverse, grad_mixed, after, medium_filter,
        gate_key, stream, gain, flops=2 * CHANS * POINTS * (POINTS + ROWS + TAPS),
    )
    dots = lax.psum(dots, "chan")
    (grad_stream,) = call(stream_kernel, [shape(full, BF16)], squares, dots, weighted, stream)
    return (grad_query, grad_stream, grad_filter, grad_residue.reshape(CHANS))


def solution(mesh):
    devices = mesh.devices.reshape(Y, Z, 2, mesh.devices.shape[1])
    fine = Mesh(devices, ("y", "z", "core", "chan"))
    seq = ("y", "z", "core")
    rows, chans = (P(seq, "chan"), P("chan"))
    in_specs = (rows, chans, rows, rows, rows, rows, P(None, "chan"), chans, chans)
    out_specs = (rows, rows, P(None, "chan"), chans)
    return jax.shard_map(body, mesh=fine, in_specs=in_specs, out_specs=out_specs, check_vma=False)
```

time: 603 us -> 149 us (0.25)
  blocking collectives: 427 us -> 51.7 us
  waiting for transfers between devices: 77.8 us -> 14.5 us
  starting transfers between devices: 6.19 us -> 45.8 us
  matrix products: 32.4 us -> 0 us
  Pallas kernels: 0 us -> 20.6 us
  other arithmetic: 14.3 us -> 0.09 us
  between operations: 14.9 us -> 0.86 us
  local copies, waits for them, and re-layouts: 25.6 us -> 13.8 us
    psum x2, blocking collectives: 253 us -> 15.1 us  [the longest x1 9.06 us: body(): squares = lax.psum(squares, 'chan')]
    all_gather x2 -> x0, blocking collectives: 173 us -> none  [prefix(): pieces = jax.tree.map(lambda part: lax.all_gather(part, axis), value)]
    psum x1 -> x0, waiting for transfers between devices: 67.9 us -> none  [body(): filter_sum, residue_sum = lax.psum((filter_local, residue_local), 'seq')]
    all_to_all x0 -> x1, blocking collectives: none -> 36.6 us  [body(): parts = lax.all_to_all(chip_sum, plane, 0, 0, tiled=True)]
    conv_general_dilated x3 -> x0, matrix products: 32.4 us -> none  [depthwise(): lax.conv_general_dilated(extended[None], kernel[:, None, :], (1,), 'VALID...]
    pallas_call x0 -> x14, Pallas kernels: none -> 20.6 us  [call(): pl.pallas_call(kernel, out_shape=tuple(outs), in_specs=[vmem] * len(args)...]
    all_to_all x0 -> x2, starting transfers between devices: none -> 20.3 us  [the longest x1 13.2 us: body(): pairs = lax.all_to_all(spread, plane, 0, 0, tiled=True)]
    ppermute x2 -> x5, starting transfers between devices: 6.15 us -> 25.5 us  [the longest x1 8.92 us: body(): other = lax.ppermute(first, 'core', swap)]
  transfers between devices with their start and end apart: 3 -> 7, of which waited for: 3 -> 4; matrix products, arithmetic and copies ran while one was open for 3% -> 0% of each run, Pallas kernels for 0% -> 11%
where the time goes in v1:
time: 149 us; the launch traced here: 147 us
  blocking collectives  51.7 us (35%)
  starting transfers between devices  45.8 us (31%)
  Pallas kernels  20.6 us (14%)
  waiting for transfers between devices  14.5 us (10%)
  local copies, waits for them, and re-layouts  13.8 us (9%)
    all_to_all x1, blocking collectives, body(): parts = lax.all_to_all(chip_sum, plane, 0, 0, tiled=True)  36.6 us
    pallas_call x14, Pallas kernels, call(): pl.pallas_call(kernel, out_shape=tuple(outs), in_specs=[vmem] * len(args)...  20.6 us
    unnamed x50, local copies, waits for them, and re-layouts  13.8 us
    all_to_all x1, starting transfers between devices, body(): pairs = lax.all_to_all(spread, plane, 0, 0, tiled=True)  13.2 us
    psum x1, blocking collectives, body(): squares = lax.psum(squares, 'chan')  9.06 us
    ppermute x1, starting transfers between devices, body(): other = lax.ppermute(first, 'core', swap)  8.92 us
    all_to_all x1, starting transfers between devices, body(): own_half = lax.all_to_all(spread_sum, plane, 0, 0, tiled=True)  7.13 us
    all_to_all x1, waiting for transfers between devices, body(): own_half = lax.all_to_all(spread_sum, plane, 0, 0, tiled=True)  7.09 us
  transfers between devices with their start and end apart: 7, of which 4 were waited for; matrix products, arithmetic and copies ran while one was open for 0% of the time, Pallas kernels for 11%

profile of v1, /device:TPU:1, one launch (start us, length us, event | category | flops | bytes accessed | tf_op | source)
XLA Modules:
  0.0 147.3 jit_solution(9939145802152763129)
XLA Ops:
  1.7 1.0 copy-done.5
  3.7 8.9 %collective-permute-start.1 = (f32[8,128]{1,0:T(8,128)S(1)}, f32[8,128]{1,0:T(8,128)S(1)}, u32[]{:S(2)}, u32[]{:S(2)}) collective-permute-start(f32[8,128]{1,0:T(8,128)S(1)} %shard_map.150.own_ref), channel_id=1, source_target_pairs={{0,4},{4,0},{1,5},{5,1},{2,6},{6,2},{3,7},{7,3},{8,12},{12,8},{9,1... | collective-permute-start | bytes 12296 | tf_op jit(solution)/shard_map/ppermute | solution.py:295
  14.1 13.2 %all-to-all-start = ((f32[64,8,128]{2,1,0:T(8,128)}), f32[64,8,128]{2,1,0:T(8,128)S(1)}, u32[]{:S(2)}, u32[]{:S(2)}) async-start(f32[64,8,128]{2,1,0:T(8,128)} %shard_map.151), calls=%async_computation | async-start | bytes 524288 | tf_op jit(solution)/shard_map/all_to_all | solution.py:299
  27.5 9.1 %psum.14.total_ref = f32[1,256]{1,0:T(1,128)S(1)} all-reduce(f32[1,256]{1,0:T(1,128)S(1)} %shard_map.147), channel_id=1, replica_groups=mesh['y'=4,'z'=16,'core'=2,'chan'=4] {'chan'}, use_global_device_ids=true, to_apply=%region_0.0 | all-reduce | flops 256 | bytes 2048 | tf_op jit(solution)/shard_map/psum | solution.py:302
  36.6 1.1 shard_map.148
  38.5 5.3 %collective-permute-start = (f32[128,1024]{1,0:T(8,128)}, f32[128,1024]{1,0:T(8,128)}, u32[]{:S(2)}, u32[]{:S(2)}) collective-permute-start(f32[128,1024]{1,0:T(8,128)} %get-tuple-element.18), channel_id=1, source_target_pairs={{0,4},{4,8},{8,12},{12,16},{16,20},{20,24},{24,28},{28,32},{32,36}... | collective-permute-start | bytes 1572872 | tf_op jit(solution)/shard_map/ppermute | solution.py:307
  45.0 5.1 %collective-permute-done.rim_ref = f32[128,1024]{1,0:T(8,128)} collective-permute-done((f32[128,1024]{1,0:T(8,128)}, f32[128,1024]{1,0:T(8,128)}, u32[]{:S(2)}, u32[]{:S(2)}) %collective-permute-start) | collective-permute-done | bytes 524320 | tf_op jit(solution)/shard_map/ppermute | solution.py:307
  50.2 1.0 copy-done.15
  51.2 1.0 copy-done.18
  52.3 5.9 %shard_map.156 = (f32[128,8,128]{2,1,0:T(8,128)S(1)}, f32[128,8,128]{2,1,0:T(8,128)S(1)}) custom-call(bf16[384,384]{1,0:T(8,128)(2,1)S(1)} %copy-done.7, bf16[128,384]{1,0:T(8,128)(2,1)S(1)} %copy-done.24, bf16[256,1024]{1,0:T(8,128)(2,1)S(1)} %copy-done.18, f32[128,1024]{1,0:T(8,128)} %collective-permute-done.rim_ref, ...), custom_call_target="tpu_custom_call" | custom-call | flops 905969664 | bytes 4071424 | tf_op jit(solution)/shard_map/pallas_call | solution.py:40
  60.8 1.9 %collective-permute-start.3 = (f32[64,8,128]{2,1,0:T(8,128)S(1)}, f32[64,8,128]{2,1,0:T(8,128)S(1)}, u32[]{:S(2)}, u32[]{:S(2)}) collective-permute-start(f32[64,8,128]{2,1,0:T(8,128)S(1)} %get-tuple-element.27), channel_id=1, source_target_pairs={{0,4},{4,0},{1,5},{5,1},{2,6},{6,2},{3,7},{7,3},{8,12},{12,8},{9,1... | collective-permute-start | bytes 786440 | tf_op jit(solution)/shard_map/ppermute | solution.py:323
  62.7 1.5 %collective-permute-done.3.b_ref = f32[64,8,128]{2,1,0:T(8,128)S(1)} collective-permute-done((f32[64,8,128]{2,1,0:T(8,128)S(1)}, f32[64,8,128]{2,1,0:T(8,128)S(1)}, u32[]{:S(2)}, u32[]{:S(2)}) %collective-permute-start.3) | collective-permute-done | bytes 262176 | tf_op jit(solution)/shard_map/ppermute | solution.py:323
  64.2 36.6 %all_to_all.15.parts_ref = f32[64,8,128]{2,1,0:T(8,128)S(1)} all-to-all(f32[64,8,128]{2,1,0:T(8,128)S(1)} %shard_map.158), channel_id=1, replica_groups=mesh['y'=4,'z'=16,'core'=2,'chan'=4] {'y','z'}, dimensions={0} | all-to-all | bytes 524288 | tf_op jit(solution)/shard_map/all_to_all | solution.py:325
  101.6 7.1 %all-to-all-start.2 = ((f32[64,8,128]{2,1,0:T(8,128)}), f32[64,8,128]{2,1,0:T(8,128)S(1)}, u32[]{:S(2)}, u32[]{:S(2)}) async-start(f32[64,8,128]{2,1,0:T(8,128)} %shard_map.159), calls=%async_computation.2 | async-start | bytes 524288 | tf_op jit(solution)/shard_map/all_to_all | solution.py:327
  109.8 1.0 copy-done.19
  110.8 4.7 %shard_map.153 = (bf16[256,1024]{1,0:T(8,128)(2,1)}, bf16[256,1024]{1,0:T(8,128)(2,1)S(1)}, f32[128,1024]{1,0:T(8,128)}) custom-call(bf16[384,384]{1,0:T(8,128)(2,1)S(1)} %copy-done.7, bf16[384,384]{1,0:T(8,128)(2,1)S(1)} %copy-done.8, bf16[256,1024]{1,0:T(8,128)(2,1)S(1)} %copy-done.19, f32[128,1024]{1,0:T(8,128)} %collective-permute-done.rim_ref, ...), custom_call_target="tpu_custom_call" | custom-call | flops 603979776 | bytes 5320704 | tf_op jit(solution)/shard_map/pallas_call | solution.py:40
  116.3 3.5 %collective-permute-start.2 = (f32[128,1024]{1,0:T(8,128)}, f32[128,1024]{1,0:T(8,128)S(1)}, u32[]{:S(2)}, u32[]{:S(2)}) collective-permute-start(f32[128,1024]{1,0:T(8,128)} %get-tuple-element.21), channel_id=1, source_target_pairs={{4,0},{8,4},{12,8},{16,12},{20,16},{24,20},{28,24},{32,28},{36,32}... | collective-permute-start | bytes 1572872 | tf_op jit(solution)/shard_map/ppermute | solution.py:339
  119.8 7.1 %all-to-all-done.2.own_ref = f32[64,8,128]{2,1,0:T(8,128)S(1)} async-done(((f32[64,8,128]{2,1,0:T(8,128)}), f32[64,8,128]{2,1,0:T(8,128)S(1)}, u32[]{:S(2)}, u32[]{:S(2)}) %all-to-all-start.2) | async-done | bytes 262176 | tf_op jit(solution)/shard_map/all_to_all | solution.py:327
  126.9 5.9 %collective-permute-start.4 = (f32[64,8,128]{2,1,0:T(8,128)S(1)}, f32[64,8,128]{2,1,0:T(8,128)}, u32[]{:S(2)}, u32[]{:S(2)}) collective-permute-start(f32[64,8,128]{2,1,0:T(8,128)S(1)} %all-to-all-done.2.own_ref), channel_id=1, source_target_pairs={{0,4},{4,0},{1,5},{5,1},{2,6},{6,2},{3,7},{7,3},{8,12},{12,8},{9,1... | collective-permute-start | bytes 786440 | tf_op jit(solution)/shard_map/ppermute | solution.py:328
  133.6 1.0 copy-done.10
  135.7 2.7 %shard_map.154 = (f32[256,1024]{1,0:T(8,128)S(1)}, f32[1,256]{1,0:T(1,128)S(1)}) custom-call(bf16[384,384]{1,0:T(8,128)(2,1)S(1)} %copy-done.7, bf16[384,384]{1,0:T(8,128)(2,1)S(1)} %copy-done.8, bf16[256,1024]{1,0:T(8,128)(2,1)S(1)} %copy-done.10, f32[128,1024]{1,0:T(8,128)S(1)} %copy-done.12, f32[128,1024]{1,0:T(8,128)S(1)} %copy-done.1, ...), custom_call_target="tpu_custom_call" | custom-call | flops 603979776 | bytes 4264960 | tf_op jit(solution)/shard_map/pallas_call | solution.py:40
  138.4 6.0 %psum.15.dots_ref = f32[1,256]{1,0:T(1,128)S(1)} all-reduce(f32[1,256]{1,0:T(1,128)S(1)} %get-tuple-element.22), channel_id=1, replica_groups=mesh['y'=4,'z'=16,'core'=2,'chan'=4] {'chan'}, use_global_device_ids=true, to_apply=%region_1.0 | all-reduce | flops 256 | bytes 2048 | tf_op jit(solution)/shard_map/psum | solution.py:344
  144.4 1.1 shard_map.155
  145.5 1.8 %shard_map.160 = (f32[128,1024]{1,0:T(8,128)}, f32[8,128]{1,0:T(8,128)}) custom-call(s32[1]{0:T(128)} %bitcast.3.core_ref, f32[64,8,128]{2,1,0:T(8,128)S(1)} %all-to-all-done.2.own_ref, f32[64,8,128]{2,1,0:T(8,128)} %collective-permute-done.4.other_ref, f32[128,1024]{1,0:T(8,128)S(1)} %copy-done.1, f32[8,128]{1,0:T(8,128)S(1)} %bitcast.16), custom_call_target="tpu_custom_call" | custom-call | bytes 1581060 | tf_op jit(solution)/shard_map/pallas_call | solution.py:40
  (59 shorter events, 12.9 us)
Async XLA Ops:
  0.6 1.0 copy-start.3
  1.7 1.0 copy-start.5
  3.4 10.0 %copy-start.21 = (f32[1024]{0:T(1024)S(1)}, f32[1024]{0:T(1024)}, u32[]{:S(2)}) copy-start(f32[1024]{0:T(1024)} %param.20) | copy-start | bytes 12292
  3.6 23.7 %copy-start = (bf16[256,1024]{1,0:T(8,128)(2,1)S(1)}, bf16[256,1024]{1,0:T(8,128)(2,1)}, u32[]{:S(2)}) copy-start(bf16[256,1024]{1,0:T(8,128)(2,1)} %stream_ref.7) | copy-start | bytes 1572868
  3.7 9.7 %collective-permute-start.1 = (f32[8,128]{1,0:T(8,128)S(1)}, f32[8,128]{1,0:T(8,128)S(1)}, u32[]{:S(2)}, u32[]{:S(2)}) collective-permute-start(f32[8,128]{1,0:T(8,128)S(1)} %shard_map.150.own_ref), channel_id=1, source_target_pairs={{0,4},{4,0},{1,5},{5,1},{2,6},{6,2},{3,7},{7,3},{8,12},{12,8},{9,1... | collective-permute-start | bytes 12296 | tf_op jit(solution)/shard_map/ppermute | solution.py:295
  14.1 22.5 %copy-start.2 = (bf16[256,1024]{1,0:T(8,128)(2,1)S(1)}, bf16[256,1024]{1,0:T(8,128)(2,1)}, u32[]{:S(2)}) copy-start(bf16[256,1024]{1,0:T(8,128)(2,1)} %key_ref.3) | copy-start | bytes 1572868
  14.1 44.8 %all-to-all-start = ((f32[64,8,128]{2,1,0:T(8,128)}), f32[64,8,128]{2,1,0:T(8,128)S(1)}, u32[]{:S(2)}, u32[]{:S(2)}) async-start(f32[64,8,128]{2,1,0:T(8,128)} %shard_map.151), calls=%async_computation | async-start | bytes 524288 | tf_op jit(solution)/shard_map/all_to_all | solution.py:299
  27.3 9.3 %copy-start.22 = (f32[1024]{0:T(1024)S(1)}, f32[1024]{0:T(1024)}, u32[]{:S(2)}) copy-start(f32[1024]{0:T(1024)} %param.13) | copy-start | bytes 12292
  36.6 7.2 %copy-start.4 = (bf16[256,1024]{1,0:T(8,128)(2,1)S(1)}, bf16[256,1024]{1,0:T(8,128)(2,1)}, u32[]{:S(2)}) copy-start(bf16[256,1024]{1,0:T(8,128)(2,1)} %out_ref.3) | copy-start | bytes 1572868
  36.6 7.2 %copy-start.6 = (bf16[256,1024]{1,0:T(8,128)(2,1)S(1)}, bf16[256,1024]{1,0:T(8,128)(2,1)}, u32[]{:S(2)}) copy-start(bf16[256,1024]{1,0:T(8,128)(2,1)} %cot_ref.3) | copy-start | bytes 1572868
  38.5 11.7 %copy-start.7 = (bf16[384,384]{1,0:T(8,128)(2,1)S(1)}, bf16[384,384]{1,0:T(8,128)(2,1)}, u32[]{:S(2)}) copy-start(bf16[384,384]{1,0:T(8,128)(2,1)} %constant.26.clone.fwd_ref) | copy-start | bytes 884740
  38.5 11.7 %copy-start.24 = (bf16[128,384]{1,0:T(8,128)(2,1)S(1)}, bf16[128,384]{1,0:T(8,128)(2,1)}, u32[]{:S(2)}) copy-start(bf16[128,384]{1,0:T(8,128)(2,1)} %constant.28.clone.lag_ref) | copy-start | bytes 294916
  38.5 11.7 %collective-permute-start = (f32[128,1024]{1,0:T(8,128)}, f32[128,1024]{1,0:T(8,128)}, u32[]{:S(2)}, u32[]{:S(2)}) collective-permute-start(f32[128,1024]{1,0:T(8,128)} %get-tuple-element.18), channel_id=1, source_target_pairs={{0,4},{4,8},{8,12},{12,16},{16,20},{20,24},{24,28},{28,32},{32,36}... | collective-permute-start | bytes 1572872 | tf_op jit(solution)/shard_map/ppermute | solution.py:307
  50.2 1.0 copy-start.15
  51.2 1.0 copy-start.18
  59.6 1.0 copy-start.14
  60.8 3.4 %collective-permute-start.3 = (f32[64,8,128]{2,1,0:T(8,128)S(1)}, f32[64,8,128]{2,1,0:T(8,128)S(1)}, u32[]{:S(2)}, u32[]{:S(2)}) collective-permute-start(f32[64,8,128]{2,1,0:T(8,128)S(1)} %get-tuple-element.27), channel_id=1, source_target_pairs={{0,4},{4,0},{1,5},{5,1},{2,6},{6,2},{3,7},{7,3},{8,12},{12,8},{9,1... | collective-permute-start | bytes 786440 | tf_op jit(solution)/shard_map/ppermute | solution.py:323
  100.8 7.9 %copy-start.1 = (f32[128,1024]{1,0:T(8,128)S(1)}, f32[128,1024]{1,0:T(8,128)}, u32[]{:S(2)}) copy-start(f32[128,1024]{1,0:T(8,128)} %filter_ref.5) | copy-start | bytes 1572868
  101.6 7.2 %copy-start.8 = (bf16[384,384]{1,0:T(8,128)(2,1)S(1)}, bf16[384,384]{1,0:T(8,128)(2,1)}, u32[]{:S(2)}) copy-start(bf16[384,384]{1,0:T(8,128)(2,1)} %constant.27.clone.inv_ref) | copy-start | bytes 884740
  101.6 25.3 %all-to-all-start.2 = ((f32[64,8,128]{2,1,0:T(8,128)}), f32[64,8,128]{2,1,0:T(8,128)S(1)}, u32[]{:S(2)}, u32[]{:S(2)}) async-start(f32[64,8,128]{2,1,0:T(8,128)} %shard_map.159), calls=%async_computation.2 | async-start | bytes 524288 | tf_op jit(solution)/shard_map/all_to_all | solution.py:327
  108.8 1.0 copy-start.16
  109.8 1.0 copy-start.19
  116.3 16.5 %collective-permute-start.2 = (f32[128,1024]{1,0:T(8,128)}, f32[128,1024]{1,0:T(8,128)S(1)}, u32[]{:S(2)}, u32[]{:S(2)}) collective-permute-start(f32[128,1024]{1,0:T(8,128)} %get-tuple-element.21), channel_id=1, source_target_pairs={{4,0},{8,4},{12,8},{16,12},{20,16},{24,20},{28,24},{32,28},{36,32}... | collective-permute-start | bytes 1572872 | tf_op jit(solution)/shard_map/ppermute | solution.py:339
  126.9 18.6 %collective-permute-start.4 = (f32[64,8,128]{2,1,0:T(8,128)S(1)}, f32[64,8,128]{2,1,0:T(8,128)}, u32[]{:S(2)}, u32[]{:S(2)}) collective-permute-start(f32[64,8,128]{2,1,0:T(8,128)S(1)} %all-to-all-done.2.own_ref), channel_id=1, source_target_pairs={{0,4},{4,0},{1,5},{5,1},{2,6},{6,2},{3,7},{7,3},{8,12},{12,8},{9,1... | collective-permute-start | bytes 786440 | tf_op jit(solution)/shard_map/ppermute | solution.py:328
  (8 other events, 6.6 us)

commit v2 on v0

v2 whole, which is shorter than its diff:
```python
import jax
import jax.numpy as jnp
import numpy as np
from jax import lax
from jax.experimental import pallas as pl
from jax.experimental.pallas import tpu as pltpu
from jax.sharding import Mesh, PartitionSpec as P

EPSILON = 1e-05
ROWS = 256
TAPS = 128
CHANS = 1024
TOKENS = 32768
CHANNEL_TOTAL = 4096
LANES = 128
TILES = CHANS // LANES
WIDTH = 256
PER = WIDTH // LANES
STEPS = CHANS // WIDTH
GROUPS = TAPS // 8
POINTS = ROWS + TAPS
HALF = POINTS // 2
X, Y, Z, ZL = (4, 4, 16, 4)
ZH = Z // ZL
PLANE = Y * Z
LARGE = 60 * 1024 * 1024
SMALL = 8 * 1024 * 1024
F32 = jnp.float32
BF16 = jnp.bfloat16
DENSE = (TILES, LANES)
FULL = (ROWS, CHANS)


def transform_tables():
    k = np.arange(HALF, dtype=np.int64)[:, None]
    n = np.arange(POINTS, dtype=np.int64)[None, :]
    angle = np.pi * (((2 * k + 1) * n) % (2 * POINTS)).astype(np.float64) / POINTS
    table = np.concatenate([np.cos(angle), -np.sin(angle)], axis=0)
    forward = table.astype(BF16)
    inverse = np.ascontiguousarray(table.T).astype(BF16)
    lags = np.ascontiguousarray(table.T[TAPS:0:-1]).astype(BF16)
    return forward, inverse, lags


SMEM = pl.BlockSpec(memory_space=pltpu.SMEM)
VMEM = pl.BlockSpec(memory_space=pltpu.VMEM)


def shape(dims, dtype=F32):
    return jax.ShapeDtypeStruct(dims, dtype)


def cols(rows):
    return pl.BlockSpec((rows, WIDTH), lambda j: (0, j))


def whole(*dims):
    return pl.BlockSpec(dims, lambda j: (0,) * len(dims))


def cost(args, outs, flops):
    sizes = [a.size * a.dtype.itemsize for a in args]
    sizes += [int(np.prod(o.shape)) * o.dtype.itemsize for o in outs]
    return pl.CostEstimate(flops=flops, bytes_accessed=sum(sizes), transcendentals=0)


def small(kernel, outs, *args, specs=None):
    return pl.pallas_call(
        kernel,
        out_shape=tuple(outs),
        in_specs=[VMEM] * len(args) if specs is None else specs,
        out_specs=tuple([VMEM] * len(outs)),
        compiler_params=pltpu.CompilerParams(vmem_limit_bytes=SMALL),
        cost_estimate=cost(args, outs, 0),
    )(*args)


def large(kernel, outs, out_specs, args, in_specs, scratch=(), flops=0):
    return pl.pallas_call(
        kernel,
        grid=(STEPS,),
        out_shape=tuple(outs),
        in_specs=in_specs,
        out_specs=tuple(out_specs),
        scratch_shapes=list(scratch),
        compiler_params=pltpu.CompilerParams(vmem_limit_bytes=LARGE),
        cost_estimate=cost(args, outs, flops),
    )(*args)


def dot(a, b):
    return lax.dot_general(
        a, b, (((1,), (0,)), ((), ())), preferred_element_type=F32
    )


def row(ref):
    at = pl.program_id(0) * PER
    return jnp.concatenate([ref[pl.ds(at + i, 1), :] for i in range(PER)], axis=1)


def put_row(ref, value):
    at = pl.program_id(0) * PER
    for i in range(PER):
        ref[pl.ds(at + i, 1), :] = value[:, i * LANES : (i + 1) * LANES]


def fold(value):
    return sum(value[:, i * LANES : (i + 1) * LANES] for i in range(PER))


def row_mean(parts_ref):
    packed = jnp.sum(parts_ref[...], axis=0) / CHANNEL_TOTAL
    return jnp.concatenate(
        [jnp.broadcast_to(packed[i : i + 1], (LANES, LANES)).T for i in range(ROWS // LANES)], axis=0
    )


def widen(value):
    return jnp.concatenate([value] * PER, axis=1)


def spread_rows(acc, out_ref):
    total = jnp.sum(acc.T, axis=0, keepdims=True)
    packed = jnp.concatenate([total[:, :LANES], total[:, LANES:], jnp.zeros((6, LANES), F32)], axis=0)
    out_ref[...] = jnp.broadcast_to(packed, out_ref.shape)


def start_kernel(stream_ref, out_ref, cot_ref, rate_ref, squares_ref, spread_ref, local_ref, acc_ref, first_ref):
    step = pl.program_id(0)
    value = stream_ref[...].astype(F32)
    squares = fold(value * value)

    @pl.when(step == 0)
    def _():
        acc_ref[...] = squares

    @pl.when(step > 0)
    def _():
        acc_ref[...] += squares

    rank = lax.broadcasted_iota(jnp.int32, (8, WIDTH), 0)
    rate = row(rate_ref)
    source = out_ref[...].astype(F32) * cot_ref[...].astype(F32)
    coefs = [(s, jnp.where(rank < 8 - s, jnp.exp(-float(s) * rate), 0.0)) for s in (1, 2, 4)]
    power = jnp.exp(-rate * (8 - rank).astype(F32))
    carry = jnp.zeros((1, WIDTH), F32)
    for group in range(ROWS // 8 - 1, -1, -1):
        value = source[group * 8 : group * 8 + 8, :]
        for s, coef in coefs:
            value = value + coef * pltpu.roll(value, 8 - s, 0)
        value = value + power * carry
        local_ref[group * 8 : group * 8 + 8, :] = value
        carry = value[0:1, :]
    put_row(first_ref, carry)

    @pl.when(step == STEPS - 1)
    def _():
        spread_rows(acc_ref[...], squares_ref)
        spread_ref[...] = jnp.broadcast_to(first_ref[...], spread_ref.shape)


def column_kernel(place_ref, parts_ref, first_ref, rate_ref, out_ref):
    z = place_ref[1]
    pace = rate_ref[...] * (-2.0 * ROWS)
    ahead = jnp.zeros(DENSE, F32)
    total = jnp.zeros(DENSE, F32)
    for other in range(Z):
        value = parts_ref[other]
        gap = other - z - 1
        weight = jnp.exp(pace * jnp.maximum(gap, 0).astype(F32))
        ahead = ahead + jnp.where(gap >= 0, weight, 0.0) * value
        total = total + jnp.exp(pace * float(other)) * value
    count = out_ref.shape[0]
    out_ref[:, 0] = jnp.broadcast_to(total, (count,) + DENSE)
    out_ref[:, 1] = jnp.broadcast_to(ahead, (count,) + DENSE)
    out_ref[:, 2] = jnp.broadcast_to(first_ref[0], (count,) + DENSE)


def carry_kernel(place_ref, parts_ref, rate_ref, carry_ref):
    y, z, core = (place_ref[0], place_ref[1], place_ref[2])
    rate = rate_ref[...]
    decay = jnp.exp(-ROWS * rate)
    rest = jnp.exp(rate * (-2.0 * ROWS) * (Z - 1 - z).astype(F32))
    both = []
    for parity in range(2):
        planes = jnp.zeros(DENSE, F32)
        for later in range(1, Y):
            gap = later - y - 1
            weight = jnp.exp(rate * (-2.0 * ROWS * Z) * jnp.maximum(gap, 0).astype(F32))
            planes = planes + jnp.where(gap >= 0, weight, 0.0) * parts_ref[later * 2 + parity, 0]
        both.append(parts_ref[y * 2 + parity, 1] + rest * planes)
    last = both[0] + decay * both[1]
    carry_ref[...] = jnp.where(core == 0, parts_ref[y * 2 + 1, 2] + decay * last, last)


def norm_kernel(total_ref, after_ref, inv_ref):
    inv_ref[...] = lax.rsqrt(row_mean(total_ref) + EPSILON)


def product_kernel(inv_ref, stream_ref, key_ref, gain_ref, product_ref, rim_ref):
    normed = stream_ref[...].astype(F32) * widen(inv_ref[...]) * row(gain_ref)
    product = key_ref[...].astype(F32) * normed
    product_ref[...] = product.astype(BF16)
    rim_ref[...] = product[ROWS - TAPS :, :]


def mul_conj(a, b):
    ar, ai = (a[:HALF], a[HALF:])
    br, bi = (b[:HALF], b[HALF:])
    return jnp.concatenate([ar * br + ai * bi, ar * bi - ai * br], axis=0).astype(BF16)


def mul(a, b):
    ar, ai = (a[:HALF], a[HALF:])
    br, bi = (b[:HALF], b[HALF:])
    return jnp.concatenate([ar * br - ai * bi, ar * bi + ai * br], axis=0).astype(BF16)


def grad_stored(local_ref, rate_ref, scale_ref, carry_ref):
    rate = row(rate_ref)
    rank = lax.broadcasted_iota(jnp.int32, (8, WIDTH), 0)
    power = jnp.exp(-rate * (8 - rank).astype(F32)) * row(carry_ref)
    groups = []
    for group in range(ROWS // 8):
        far = power * jnp.exp(-rate * float(ROWS - 8 - 8 * group))
        groups.append(local_ref[group * 8 : group * 8 + 8, :] + far)
    return jnp.concatenate(groups, axis=0) * row(scale_ref)


def filter_kernel(
    place_ref, fwd_ref, lag_ref, product_ref, rim_ref, local_ref, query_ref, rate_ref, scale_ref, carry_ref,
    keep_ref, send_ref, mixed_grad_ref, head_ref,
):
    ext = jnp.concatenate([rim_ref[...].astype(BF16), product_ref[...]], axis=0)
    product = dot(fwd_ref[...], ext)
    grad_mixed = query_ref[...].astype(F32) * grad_stored(local_ref, rate_ref, scale_ref, carry_ref)
    head_ref[...] = grad_mixed[:TAPS]
    grad_mixed = grad_mixed.astype(BF16)
    mixed_grad_ref[...] = grad_mixed
    spectrum = dot(fwd_ref[:, :ROWS], grad_mixed)
    taps = dot(lag_ref[...], mul_conj(spectrum, product))
    is_first = place_ref[2] == 0
    for group in range(GROUPS // 2):
        low = taps[group * 8 : group * 8 + 8, :]
        high = taps[TAPS // 2 + group * 8 : TAPS // 2 + group * 8 + 8, :]
        keep = jnp.where(is_first, low, high)
        send = jnp.where(is_first, high, low)
        for i in range(PER):
            keep_ref[group, i] = keep[:, i * LANES : (i + 1) * LANES]
            send_ref[group, i] = send[:, i * LANES : (i + 1) * LANES]


def query_kernel(
    fwd_ref, inv_ref, product_ref, rim_ref, local_ref, filter_ref, rate_ref, scale_ref, carry_ref, grad_ref, token_ref
):
    ext = jnp.concatenate([rim_ref[...].astype(BF16), product_ref[...]], axis=0)
    product = dot(fwd_ref[...], ext)
    taps = dot(fwd_ref[:, :TAPS], filter_ref[...].astype(BF16))
    mixed = dot(inv_ref[TAPS:, :], mul(product, taps)) * (2.0 / POINTS)
    grad_ref[...] = (mixed * grad_stored(local_ref, rate_ref, scale_ref, carry_ref)).astype(BF16)
    token_ref[...] = carry_ref[...]


def weighted_kernel(
    fwd_ref, inv_ref, grad_ref, after_ref, filter_ref, key_ref, stream_ref, gain_ref, weighted_ref, dots_ref, acc_ref
):
    step = pl.program_id(0)
    ext = jnp.concatenate([grad_ref[...], after_ref[...].astype(BF16)], axis=0)
    grad = dot(fwd_ref[...], ext)
    taps = dot(fwd_ref[:, :TAPS], filter_ref[...].astype(BF16))
    back = dot(inv_ref[:ROWS, :], mul_conj(taps, grad)) * (2.0 / POINTS)
    weighted = row(gain_ref) * key_ref[...].astype(F32) * back
    weighted_ref[...] = weighted
    dots = fold(weighted * stream_ref[...].astype(F32))

    @pl.when(step == 0)
    def _():
        acc_ref[...] = dots

    @pl.when(step > 0)
    def _():
        acc_ref[...] += dots

    @pl.when(step == STEPS - 1)
    def _():
        spread_rows(acc_ref[...], dots_ref)


def stream_kernel(inv_ref, dots_ref, weighted_ref, stream_ref, out_ref, token_ref, factor_ref):
    inv = inv_ref[...]

    @pl.when(pl.program_id(0) == 0)
    def _():
        factor_ref[...] = inv * inv * row_mean(dots_ref)

    value = weighted_ref[...] - stream_ref[...].astype(F32) * widen(factor_ref[...])
    out_ref[...] = (widen(inv) * value).astype(BF16)
    token_ref[...] = factor_ref[0:8, :]


def add_kernel(a_ref, b_ref, out_ref):
    out_ref[...] = a_ref[...] + b_ref[...]


def spread_sum_kernel(parts_ref, after_ref, spread_ref):
    total = jnp.sum(parts_ref[...], axis=0)
    spread_ref[...] = jnp.broadcast_to(total, spread_ref.shape)


def fence_kernel(value_ref, after_ref, out_ref):
    out_ref[...] = value_ref[...]


def finish_kernel(place_ref, own_ref, other_ref, filter_ref, residue_ref, filter_out, residue_out):
    scale = TOKENS ** (-0.5) * 2.0 / POINTS
    count = own_ref.shape[0]
    is_first = place_ref[2] == 0
    for tile in range(TILES):
        lanes = slice(tile * LANES, (tile + 1) * LANES)
        total = jnp.zeros((8, LANES), F32)
        for group in range(GROUPS):
            at = (group * TILES + tile) % count
            low = group * TILES + tile < count
            own, other = (own_ref[at], other_ref[at])
            value = jnp.where(is_first, own, other) if low else jnp.where(is_first, other, own)
            value = value * scale
            rows = slice(group * 8, group * 8 + 8)
            filter_out[rows, lanes] = value
            total = total + filter_ref[rows, lanes] * value
        total = jnp.sum(total, axis=0, keepdims=True)
        residue_out[tile : tile + 1, :] = total / residue_ref[tile : tile + 1, :]


def body(
    stream, norm_gain, gate_query, gate_key, gate_out, cotangent, medium_filter, long_residue, long_rate
):
    forward, inverse, lags = (jnp.asarray(t) for t in transform_tables())
    gain, rate, residue = (v.reshape(DENSE) for v in (norm_gain, long_rate, long_residue))
    scale = residue * jnp.sqrt(-jnp.expm1(-2.0 * rate))
    z_at = lax.axis_index(("zh", "zl"))
    place = jnp.stack([lax.axis_index("y"), z_at, lax.axis_index("core")]).astype(jnp.int32)
    swap = [(0, 1), (1, 0)]
    seq = ("y", "zh", "zl", "core")
    count = 2 * PLANE
    dense, table = (whole(*DENSE), whole(POINTS, POINTS))

    shares = (X,) + DENSE
    squares, spread, local = large(
        start_kernel, [shape(shares), shape((Z,) + DENSE), shape(FULL)],
        [whole(*shares), whole(Z, *DENSE), cols(ROWS)],
        (stream, gate_out, cotangent, rate), [cols(ROWS)] * 3 + [dense],
        scratch=[pltpu.VMEM((ROWS, LANES), F32), pltpu.VMEM(DENSE, F32)],
    )
    squares = lax.all_to_all(squares, "chan", 0, 0, tiled=True)
    column = lax.all_to_all(spread, ("zh", "zl"), 0, 0, tiled=True)
    thin = whole(ROWS, LANES)
    (inv,) = small(norm_kernel, [shape((ROWS, LANES))], squares, column)
    product, rim = large(
        product_kernel, [shape(FULL, BF16), shape((TAPS, CHANS))], [cols(ROWS), cols(TAPS)],
        (inv, stream, gate_key, gain), [thin, cols(ROWS), cols(ROWS), dense],
    )
    before = lax.ppermute(rim, seq, [(i, i + 1) for i in range(count - 1)])
    (sums,) = small(
        column_kernel, [shape((2 * Y, 3) + DENSE)], place, column, spread, rate, specs=[SMEM] + [VMEM] * 3
    )
    sums = lax.all_to_all(sums, ("y", "core"), 0, 0, tiled=True)
    (carry,) = small(carry_kernel, [shape(DENSE)], place, sums, rate, specs=[SMEM] + [VMEM] * 2)

    half = (GROUPS // 2, TILES, 8, LANES)
    blocks = pl.BlockSpec((GROUPS // 2, PER, 8, LANES), lambda j: (0, j, 0, 0))
    keep, send, grad_mixed, head = large(
        filter_kernel, [shape(half), shape(half), shape(FULL, BF16), shape((TAPS, CHANS))],
        [blocks, blocks, cols(ROWS), cols(TAPS)],
        (place, forward, lags, product, before, local, gate_query, rate, scale, carry),
        [SMEM, table, whole(TAPS, POINTS), cols(ROWS), cols(TAPS), cols(ROWS), cols(ROWS), dense, dense, dense],
        flops=2 * CHANS * POINTS * (POINTS + ROWS + TAPS),
    )

    got = lax.ppermute(send, "core", swap)
    (chip_sum,) = small(add_kernel, [shape(half)], keep, got)
    after = lax.ppermute(head, seq, [(i + 1, i) for i in range(count - 1)])
    parts = lax.all_to_all(chip_sum.reshape(PLANE, 8, LANES), ("y", "zl"), 0, 0, tiled=True)
    grad_query, token = large(
        query_kernel, [shape(FULL, BF16), shape(DENSE)], [cols(ROWS), dense],
        (forward, inverse, product, before, local, medium_filter, rate, scale, carry),
        [table, table, cols(ROWS), cols(TAPS), cols(ROWS), cols(TAPS), dense, dense, dense],
        flops=2 * CHANS * POINTS * (POINTS + ROWS + TAPS),
    )
    mine = (ZH, 8, LANES)
    (spread,) = small(
        spread_sum_kernel, [shape((ZH,) + mine)], parts.reshape((Y * ZL,) + mine), token
    )
    parts = lax.all_to_all(spread, "zh", 0, 0, tiled=True)
    weighted, dots = large(
        weighted_kernel, [shape(FULL), shape(shares)], [cols(ROWS), whole(*shares)],
        (forward, inverse, grad_mixed, after, medium_filter, gate_key, stream, gain),
        [table, table, cols(ROWS), cols(TAPS), cols(TAPS), cols(ROWS), cols(ROWS), dense],
        scratch=[pltpu.VMEM((ROWS, LANES), F32)],
        flops=2 * CHANS * POINTS * (POINTS + ROWS + TAPS),
    )
    (spread,) = small(spread_sum_kernel, [shape((Y * ZL,) + mine)], parts, dots)
    dots = lax.all_to_all(dots, "chan", 0, 0, tiled=True)
    own_half = lax.all_to_all(spread, ("y", "zl"), 0, 0, tiled=True).reshape(PLANE, 8, LANES)
    grad_stream, token = large(
        stream_kernel, [shape(FULL, BF16), shape(DENSE)], [cols(ROWS), dense],
        (inv, dots, weighted, stream), [thin, whole(*shares)] + [cols(ROWS)] * 2,
        scratch=[pltpu.VMEM((ROWS, LANES), F32)],
    )
    (own_half,) = small(fence_kernel, [shape(own_half.shape)], own_half, token)
    other_half = lax.ppermute(own_half, "core", swap)
    grad_filter, grad_residue = small(
        finish_kernel, [shape((TAPS, CHANS)), shape(DENSE)], place, own_half, other_half, medium_filter,
        residue, specs=[SMEM] + [VMEM] * 4,
    )
    return (grad_query, grad_stream, grad_filter, grad_residue.reshape(CHANS))


def solution(mesh):
    devices = mesh.devices.reshape(Y, ZH, ZL, 2, mesh.devices.shape[1])
    fine = Mesh(devices, ("y", "zh", "zl", "core", "chan"))
    seq = ("y", "zh", "zl", "core")
    rows, chans = (P(seq, "chan"), P("chan"))
    in_specs = (rows, chans, rows, rows, rows, rows, P(None, "chan"), chans, chans)
    out_specs = (rows, rows, P(None, "chan"), chans)
    return jax.shard_map(body, mesh=fine, in_specs=in_specs, out_specs=out_specs, check_vma=False)
```

time: 603 us -> 140 us (0.23)
  blocking collectives: 427 us -> 35.6 us
  waiting for transfers between devices: 77.8 us -> 24.2 us
  Pallas kernels: 0 us -> 32.7 us
  matrix products: 32.4 us -> 0 us
  starting transfers between devices: 6.19 us -> 37.7 us
  local copies, waits for them, and re-layouts: 25.6 us -> 6.36 us
  between operations: 14.9 us -> 0.78 us
  other arithmetic: 14.3 us -> 0.69 us
    psum x2 -> x0, blocking collectives: 253 us -> none  [the longest x1 245 us: body(): filter_sum, residue_sum = lax.psum((filter_local, residue_local), 'seq')]
    all_gather x2 -> x0, blocking collectives: 173 us -> none  [prefix(): pieces = jax.tree.map(lambda part: lax.all_gather(part, axis), value)]
    psum x1 -> x0, waiting for transfers between devices: 67.9 us -> none  [body(): filter_sum, residue_sum = lax.psum((filter_local, residue_local), 'seq')]
    all_to_all x0 -> x2, blocking collectives: none -> 35.6 us  [the longest x1 26.6 us: body(): column = lax.all_to_all(spread, ('zh', 'zl'), 0, 0, tiled=True)]
    pallas_call x0 -> x14, Pallas kernels: none -> 32.7 us  [the longest x6 27.3 us: large(): pl.pallas_call(kernel, grid=(STEPS,), out_shape=tuple(outs), in_specs=in_...]
    conv_general_dilated x3 -> x0, matrix products: 32.4 us -> none  [depthwise(): lax.conv_general_dilated(extended[None], kernel[:, None, :], (1,), 'VALID...]
    all_to_all x0 -> x5, waiting for transfers between devices: none -> 21.7 us  [the longest x1 6.32 us: body(): sums = lax.all_to_all(sums, ('y', 'core'), 0, 0, tiled=True)]
    all_to_all x0 -> x5, starting transfers between devices: none -> 21.1 us  [the longest x1 5.45 us: body(): lax.all_to_all(spread, ('y', 'zl'), 0, 0, tiled=True)]
  transfers between devices with their start and end apart: 3 -> 9, of which waited for: 3 -> 7; matrix products, arithmetic and copies ran while one was open for 3% -> 0% of each run, Pallas kernels for 0% -> 13%
where the time goes in v2:
time: 140 us; the launch traced here: 138 us
  starting transfers between devices  37.7 us (27%)
  blocking collectives  35.6 us (25%)
  Pallas kernels  32.7 us (23%)
  waiting for transfers between devices  24.2 us (17%)
  local copies, waits for them, and re-layouts  6.36 us (5%)
    pallas_call x6, Pallas kernels, large(): pl.pallas_call(kernel, grid=(STEPS,), out_shape=tuple(outs), in_specs=in_...  27.3 us
    all_to_all x1, blocking collectives, body(): column = lax.all_to_all(spread, ('zh', 'zl'), 0, 0, tiled=True)  26.6 us
    all_to_all x1, blocking collectives, body(): squares = lax.all_to_all(squares, 'chan', 0, 0, tiled=True)  9.05 us
    unnamed x32, local copies, waits for them, and re-layouts  6.36 us
    all_to_all x1, waiting for transfers between devices, body(): sums = lax.all_to_all(sums, ('y', 'core'), 0, 0, tiled=True)  6.32 us
    ppermute x1, starting transfers between devices, body(): other_half = lax.ppermute(own_half, 'core', swap)  6.23 us
    ppermute x1, starting transfers between devices, body(): before = lax.ppermute(rim, seq, [(i, i + 1) for i in range(count - 1)])  5.82 us
    pallas_call x8, Pallas kernels, small(): pl.pallas_call(kernel, out_shape=tuple(outs), in_specs=[VMEM] * len(args)...  5.47 us
  transfers between devices with their start and end apart: 9, of which 7 were waited for; matrix products, arithmetic and copies ran while one was open for 0% of the time, Pallas kernels for 13%

profile of v2, /device:TPU:1, one launch (start us, length us, event | category | flops | bytes accessed | tf_op | source)
XLA Modules:
  0.0 138.2 jit_solution(12290250652424758066)
XLA Ops:
  0.6 4.0 %shard_map.147 = (f32[4,8,128]{2,1,0:T(8,128)}, f32[16,8,128]{2,1,0:T(8,128)}, f32[256,1024]{1,0:T(8,128)}) custom-call(bf16[256,1024]{1,0:T(8,128)(2,1)} %stream_ref.7, bf16[256,1024]{1,0:T(8,128)(2,1)} %out_ref.1, bf16[256,1024]{1,0:T(8,128)(2,1)} %cot_ref.1, f32[8,128]{1,0:T(8,128)} %bitcast.14), custom_call_target="tpu_custom_call" | custom-call | bytes 2707456 | tf_op jit(solution)/shard_map/pallas_call | solution.py:79
  4.7 9.1 %all_to_all.35.total_ref = f32[4,8,128]{2,1,0:T(8,128)S(1)} all-to-all(f32[4,8,128]{2,1,0:T(8,128)} %get-tuple-element.21), channel_id=1, replica_groups=mesh['y'=4,'zh'=4,'zl'=4,'core'=2,'chan'=4] {'chan'}, dimensions={0} | all-to-all | bytes 32768 | tf_op jit(solution)/shard_map/all_to_all | solution.py:355
  13.7 26.6 %all_to_all.36.after_ref.parts_ref = f32[16,8,128]{2,1,0:T(8,128)S(1)} all-to-all(f32[16,8,128]{2,1,0:T(8,128)} %get-tuple-element.22.first_ref), channel_id=1, replica_groups=mesh['y'=4,'zh'=4,'zl'=4,'core'=2,'chan'=4] {'zh','zl'}, dimensions={0} | all-to-all | bytes 131072 | tf_op jit(solution)/shard_map/all_to_all | solution.py:356
  41.1 3.6 %shard_map.149 = (bf16[256,1024]{1,0:T(8,128)(2,1)}, f32[128,1024]{1,0:T(8,128)}) custom-call(f32[256,128]{1,0:T(8,128)} %copy-done.1, bf16[256,1024]{1,0:T(8,128)(2,1)} %stream_ref.7, bf16[256,1024]{1,0:T(8,128)(2,1)} %key_ref.3, f32[8,128]{1,0:T(8,128)} %bitcast.20), custom_call_target="tpu_custom_call" | custom-call | bytes 2232320 | tf_op jit(solution)/shard_map/pallas_call | solution.py:79
  44.6 5.8 %collective-permute-start = (f32[128,1024]{1,0:T(8,128)}, f32[128,1024]{1,0:T(8,128)S(1)}, u32[]{:S(2)}, u32[]{:S(2)}) collective-permute-start(f32[128,1024]{1,0:T(8,128)} %get-tuple-element.24), channel_id=1, source_target_pairs={{0,4},{4,8},{8,12},{12,16},{16,20},{20,24},{24,28},{28,32},{32,36}... | collective-permute-start | bytes 1572872 | tf_op jit(solution)/shard_map/ppermute | solution.py:363
  52.4 4.7 %all-to-all-start.2 = ((f32[8,3,8,128]{3,2,1,0:T(8,128)}), f32[8,3,8,128]{3,2,1,0:T(8,128)S(1)}, u32[]{:S(2)}, u32[]{:S(2)}) async-start(f32[8,3,8,128]{3,2,1,0:T(8,128)} %shard_map.150), calls=%async_computation.2 | async-start | bytes 196608 | tf_op jit(solution)/shard_map/all_to_all | solution.py:367
  57.7 6.3 %all-to-all-done.2.parts_ref = f32[8,3,8,128]{3,2,1,0:T(8,128)S(1)} async-done(((f32[8,3,8,128]{3,2,1,0:T(8,128)}), f32[8,3,8,128]{3,2,1,0:T(8,128)S(1)}, u32[]{:S(2)}, u32[]{:S(2)}) %all-to-all-start.2) | async-done | bytes 98336 | tf_op jit(solution)/shard_map/all_to_all | solution.py:367
  66.0 5.1 %shard_map.153 = (f32[8,8,8,128]{3,2,1,0:T(8,128)}, f32[8,8,8,128]{3,2,1,0:T(8,128)}, bf16[256,1024]{1,0:T(8,128)(2,1)}, f32[128,1024]{1,0:T(8,128)}) custom-call(s32[3]{0:T(128)} %copy-done.8, bf16[384,384]{1,0:T(8,128)(2,1)} %constant.28.clone.fwd_ref, bf16[128,384]{1,0:T(8,128)(2,1)} %constant.30.clone.lag_ref, ...), custom_call_target="tpu_custom_call" | custom-call | flops 603979776 | bytes 4599820 | tf_op jit(solution)/shard_map/pallas_call | solution.py:79
  71.1 2.3 %collective-permute-start.2 = (f32[8,8,8,128]{3,2,1,0:T(8,128)}, f32[8,8,8,128]{3,2,1,0:T(8,128)S(1)}, u32[]{:S(2)}, u32[]{:S(2)}) collective-permute-start(f32[8,8,8,128]{3,2,1,0:T(8,128)} %get-tuple-element.33), channel_id=1, source_target_pairs={{0,4},{4,0},{1,5},{5,1},{2,6},{6,2},{3,7},{7,3},{8,12},{12,8},{9,1... | collective-permute-start | bytes 786440 | tf_op jit(solution)/shard_map/ppermute | solution.py:380
  73.5 1.4 collective-permute-done.2.b_ref
  76.5 3.5 %all-to-all-start.4 = ((f32[64,8,128]{2,1,0:T(8,128)}), f32[64,8,128]{2,1,0:T(8,128)S(1)}, u32[]{:S(2)}, u32[]{:S(2)}) async-start(f32[64,8,128]{2,1,0:T(8,128)} %bitcast.6), calls=%async_computation.4 | async-start | bytes 524288 | tf_op jit(solution)/shard_map/all_to_all | solution.py:383
  80.1 2.3 %collective-permute-start.1 = (f32[128,1024]{1,0:T(8,128)S(1)}, f32[128,1024]{1,0:T(8,128)S(1)}, u32[]{:S(2)}, u32[]{:S(2)}) collective-permute-start(f32[128,1024]{1,0:T(8,128)S(1)} %copy-done.15), channel_id=1, source_target_pairs={{4,0},{8,4},{12,8},{16,12},{20,16},{24,20},{28,24},{32,28},{36,32}... | collective-permute-start | bytes 1572872 | tf_op jit(solution)/shard_map/ppermute | solution.py:382
  82.3 5.3 %shard_map.152 = (bf16[256,1024]{1,0:T(8,128)(2,1)}, f32[8,128]{1,0:T(8,128)}) custom-call(bf16[384,384]{1,0:T(8,128)(2,1)} %constant.28.clone.fwd_ref, bf16[384,384]{1,0:T(8,128)(2,1)} %constant.29.clone.inv_ref, bf16[256,1024]{1,0:T(8,128)(2,1)} %get-tuple-element.23.product_ref, f32[128,1024]{1,0:T(8,128)} %copy-done.12, ...), custom_call_target="tpu_custom_call" | custom-call | flops 603979776 | bytes 3751936 | tf_op jit(solution)/shard_map/pallas_call | solution.py:79
  87.6 2.4 %all-to-all-done.4 = f32[64,8,128]{2,1,0:T(8,128)S(1)} async-done(((f32[64,8,128]{2,1,0:T(8,128)}), f32[64,8,128]{2,1,0:T(8,128)S(1)}, u32[]{:S(2)}, u32[]{:S(2)}) %all-to-all-start.4) | async-done | bytes 262176 | tf_op jit(solution)/shard_map/all_to_all | solution.py:383
  91.3 4.0 %all-to-all-start.5 = ((f32[4,4,8,128]{3,2,1,0:T(8,128)}), f32[4,4,8,128]{3,2,1,0:T(8,128)S(1)}, u32[]{:S(2)}, u32[]{:S(2)}) async-start(f32[4,4,8,128]{3,2,1,0:T(8,128)} %shard_map.157), calls=%async_computation.5 | async-start | bytes 131072 | tf_op jit(solution)/shard_map/all_to_all | solution.py:394
  96.1 5.7 %shard_map.154 = (f32[256,1024]{1,0:T(8,128)}, f32[4,8,128]{2,1,0:T(8,128)}) custom-call(bf16[384,384]{1,0:T(8,128)(2,1)} %constant.28.clone.fwd_ref, bf16[384,384]{1,0:T(8,128)(2,1)} %constant.29.clone.inv_ref, bf16[256,1024]{1,0:T(8,128)(2,1)} %get-tuple-element.27.grad_ref, f32[128,1024]{1,0:T(8,128)} %copy-done.13, f32[128,1024]{1,0:T(8,128)} %filter_ref.5, ...), custom_call_target="tpu_custom_call" | custom-call | flops 603979776 | bytes 4280320 | tf_op jit(solution)/shard_map/pallas_call | solution.py:79
  101.8 5.2 %all-to-all-done.5.parts_ref = f32[4,4,8,128]{3,2,1,0:T(8,128)S(1)} async-done(((f32[4,4,8,128]{3,2,1,0:T(8,128)}), f32[4,4,8,128]{3,2,1,0:T(8,128)S(1)}, u32[]{:S(2)}, u32[]{:S(2)}) %all-to-all-start.5) | async-done | bytes 65568 | tf_op jit(solution)/shard_map/all_to_all | solution.py:394
  107.0 3.4 %all-to-all-start.3 = ((f32[4,8,128]{2,1,0:T(8,128)}), f32[4,8,128]{2,1,0:T(8,128)S(1)}, u32[]{:S(2)}, u32[]{:S(2)}) async-start(f32[4,8,128]{2,1,0:T(8,128)} %get-tuple-element.29.after_ref), calls=%async_computation.3 | async-start | bytes 32768 | tf_op jit(solution)/shard_map/all_to_all | solution.py:403
  111.2 3.4 %all-to-all-done.3.dots_ref = f32[4,8,128]{2,1,0:T(8,128)S(1)} async-done(((f32[4,8,128]{2,1,0:T(8,128)}), f32[4,8,128]{2,1,0:T(8,128)S(1)}, u32[]{:S(2)}, u32[]{:S(2)}) %all-to-all-start.3) | async-done | bytes 16416 | tf_op jit(solution)/shard_map/all_to_all | solution.py:403
  115.2 5.4 %all-to-all-start.6 = ((f32[16,4,8,128]{3,2,1,0:T(8,128)}), f32[16,4,8,128]{3,2,1,0:T(8,128)S(1)}, u32[]{:S(2)}, u32[]{:S(2)}) async-start(f32[16,4,8,128]{3,2,1,0:T(8,128)} %shard_map.158), calls=%async_computation.6 | async-start | bytes 524288 | tf_op jit(solution)/shard_map/all_to_all | solution.py:404
  120.6 3.6 %shard_map.155 = (bf16[256,1024]{1,0:T(8,128)(2,1)}, f32[8,128]{1,0:T(8,128)}) custom-call(f32[256,128]{1,0:T(8,128)} %copy-done.1, f32[4,8,128]{2,1,0:T(8,128)} %copy-done.14, f32[256,1024]{1,0:T(8,128)} %get-tuple-element.30.weighted_ref, bf16[256,1024]{1,0:T(8,128)(2,1)} %stream_ref.7), custom_call_target="tpu_custom_call" | custom-call | bytes 2248704 | tf_op jit(solution)/shard_map/pallas_call | solution.py:79
  124.3 4.4 %all-to-all-done.6 = f32[16,4,8,128]{3,2,1,0:T(8,128)S(1)} async-done(((f32[16,4,8,128]{3,2,1,0:T(8,128)}), f32[16,4,8,128]{3,2,1,0:T(8,128)S(1)}, u32[]{:S(2)}, u32[]{:S(2)}) %all-to-all-start.6) | async-done | bytes 262176 | tf_op jit(solution)/shard_map/all_to_all | solution.py:404
  129.4 6.2 %collective-permute-start.3 = (f32[64,8,128]{2,1,0:T(8,128)S(1)}, f32[64,8,128]{2,1,0:T(8,128)S(1)}, u32[]{:S(2)}, u32[]{:S(2)}) collective-permute-start(f32[64,8,128]{2,1,0:T(8,128)S(1)} %shard_map.159.own_ref), channel_id=1, source_target_pairs={{0,4},{4,0},{1,5},{5,1},{2,6},{6,2},{3,7},{7,3},{8,12},{12,8},{9,1... | collective-permute-start | bytes 786440 | tf_op jit(solution)/shard_map/ppermute | solution.py:411
  136.7 1.4 %shard_map.160 = (f32[128,1024]{1,0:T(8,128)}, f32[8,128]{1,0:T(8,128)}) custom-call(s32[3]{0:T(128)S(1)} %copy-done.9, f32[64,8,128]{2,1,0:T(8,128)S(1)} %shard_map.159.own_ref, f32[64,8,128]{2,1,0:T(8,128)S(1)} %collective-permute-done.3.other_ref, f32[128,1024]{1,0:T(8,128)S(1)} %copy-done, f32[8,128]{1,0:T(8,128)S(1)} %bitcast.19), custom_call_target="tpu_custom_call" | custom-call | bytes 1581068 | tf_op jit(solution)/shard_map/pallas_call | solution.py:68
  (44 shorter events, 12.2 us)
Async XLA Ops:
  40.4 0.7 copy-start.1
  41.1 9.5 %copy-start.3 = (f32[16,8,128]{2,1,0:T(8,128)S(1)}, f32[16,8,128]{2,1,0:T(8,128)}, u32[]{:S(2)}) copy-start(f32[16,8,128]{2,1,0:T(8,128)} %get-tuple-element.22.first_ref) | copy-start | bytes 196612
  44.6 20.6 %collective-permute-start = (f32[128,1024]{1,0:T(8,128)}, f32[128,1024]{1,0:T(8,128)S(1)}, u32[]{:S(2)}, u32[]{:S(2)}) collective-permute-start(f32[128,1024]{1,0:T(8,128)} %get-tuple-element.24), channel_id=1, source_target_pairs={{0,4},{4,8},{8,12},{12,16},{16,20},{20,24},{24,28},{28,32},{32,36}... | collective-permute-start | bytes 1572872 | tf_op jit(solution)/shard_map/ppermute | solution.py:363
  50.5 0.7 copy-start.4
  51.2 12.9 %copy-start.8 = (s32[3]{0:T(128)}, s32[3]{0:T(128)S(1)}, u32[]{:S(2)}) copy-start(s32[3]{0:T(128)S(1)} %pad_add_fusion.place_ref) | copy-start | bytes 40
  52.4 4.7 %copy-start.7 = (f32[1024]{0:T(1024)S(1)}, f32[1024]{0:T(1024)}, u32[]{:S(2)}) copy-start(f32[1024]{0:T(1024)} %param.19) | copy-start | bytes 12292
  52.4 11.7 %all-to-all-start.2 = ((f32[8,3,8,128]{3,2,1,0:T(8,128)}), f32[8,3,8,128]{3,2,1,0:T(8,128)S(1)}, u32[]{:S(2)}, u32[]{:S(2)}) async-start(f32[8,3,8,128]{3,2,1,0:T(8,128)} %shard_map.150), calls=%async_computation.2 | async-start | bytes 196608 | tf_op jit(solution)/shard_map/all_to_all | solution.py:367
  65.2 0.8 copy-start.12
  71.1 3.7 %collective-permute-start.2 = (f32[8,8,8,128]{3,2,1,0:T(8,128)}, f32[8,8,8,128]{3,2,1,0:T(8,128)S(1)}, u32[]{:S(2)}, u32[]{:S(2)}) collective-permute-start(f32[8,8,8,128]{3,2,1,0:T(8,128)} %get-tuple-element.33), channel_id=1, source_target_pairs={{0,4},{4,0},{1,5},{5,1},{2,6},{6,2},{3,7},{7,3},{8,12},{12,8},{9,1... | collective-permute-start | bytes 786440 | tf_op jit(solution)/shard_map/ppermute | solution.py:380
  74.8 0.9 copy-start.2
  75.8 4.3 %copy-start.15 = (f32[128,1024]{1,0:T(8,128)S(1)}, f32[128,1024]{1,0:T(8,128)}, u32[]{:S(2)}) copy-start(f32[128,1024]{1,0:T(8,128)} %get-tuple-element.28) | copy-start | bytes 1572868
  76.5 13.5 %all-to-all-start.4 = ((f32[64,8,128]{2,1,0:T(8,128)}), f32[64,8,128]{2,1,0:T(8,128)S(1)}, u32[]{:S(2)}, u32[]{:S(2)}) async-start(f32[64,8,128]{2,1,0:T(8,128)} %bitcast.6), calls=%async_computation.4 | async-start | bytes 524288 | tf_op jit(solution)/shard_map/all_to_all | solution.py:383
  80.1 15.3 %collective-permute-start.1 = (f32[128,1024]{1,0:T(8,128)S(1)}, f32[128,1024]{1,0:T(8,128)S(1)}, u32[]{:S(2)}, u32[]{:S(2)}) collective-permute-start(f32[128,1024]{1,0:T(8,128)S(1)} %copy-done.15), channel_id=1, source_target_pairs={{4,0},{8,4},{12,8},{16,12},{20,16},{24,20},{28,24},{32,28},{36,32}... | collective-permute-start | bytes 1572872 | tf_op jit(solution)/shard_map/ppermute | solution.py:382
  90.0 0.7 copy-start.11
  91.3 15.7 %all-to-all-start.5 = ((f32[4,4,8,128]{3,2,1,0:T(8,128)}), f32[4,4,8,128]{3,2,1,0:T(8,128)S(1)}, u32[]{:S(2)}, u32[]{:S(2)}) async-start(f32[4,4,8,128]{3,2,1,0:T(8,128)} %shard_map.157), calls=%async_computation.5 | async-start | bytes 131072 | tf_op jit(solution)/shard_map/all_to_all | solution.py:394
  95.3 0.8 copy-start.13
  107.0 3.4 %copy-start.5 = (f32[4,8,128]{2,1,0:T(8,128)S(1)}, f32[4,8,128]{2,1,0:T(8,128)}, u32[]{:S(2)}) copy-start(f32[4,8,128]{2,1,0:T(8,128)} %get-tuple-element.29.after_ref) | copy-start | bytes 49156
  107.0 7.6 %all-to-all-start.3 = ((f32[4,8,128]{2,1,0:T(8,128)}), f32[4,8,128]{2,1,0:T(8,128)S(1)}, u32[]{:S(2)}, u32[]{:S(2)}) async-start(f32[4,8,128]{2,1,0:T(8,128)} %get-tuple-element.29.after_ref), calls=%async_computation.3 | async-start | bytes 32768 | tf_op jit(solution)/shard_map/all_to_all | solution.py:403
  114.6 0.6 copy-start.14
  115.2 13.5 %all-to-all-start.6 = ((f32[16,4,8,128]{3,2,1,0:T(8,128)}), f32[16,4,8,128]{3,2,1,0:T(8,128)S(1)}, u32[]{:S(2)}, u32[]{:S(2)}) async-start(f32[16,4,8,128]{3,2,1,0:T(8,128)} %shard_map.158), calls=%async_computation.6 | async-start | bytes 524288 | tf_op jit(solution)/shard_map/all_to_all | solution.py:404
  124.3 12.5 %copy-start = (f32[128,1024]{1,0:T(8,128)S(1)}, f32[128,1024]{1,0:T(8,128)}, u32[]{:S(2)}) copy-start(f32[128,1024]{1,0:T(8,128)} %filter_ref.5) | copy-start | bytes 1572868
  128.6 0.7 copy-start.10
  129.3 7.4 %copy-start.9 = (s32[3]{0:T(128)S(1)}, s32[3]{0:T(128)}, u32[]{:S(2)}) copy-start(s32[3]{0:T(128)} %copy-done.8) | copy-start | bytes 40
  129.4 7.4 %collective-permute-start.3 = (f32[64,8,128]{2,1,0:T(8,128)S(1)}, f32[64,8,128]{2,1,0:T(8,128)S(1)}, u32[]{:S(2)}, u32[]{:S(2)}) collective-permute-start(f32[64,8,128]{2,1,0:T(8,128)S(1)} %shard_map.159.own_ref), channel_id=1, source_target_pairs={{0,4},{4,0},{1,5},{5,1},{2,6},{6,2},{3,7},{7,3},{8,12},{12,8},{9,1... | collective-permute-start | bytes 786440 | tf_op jit(solution)/shard_map/ppermute | solution.py:411
  (1 other events, 0.6 us)

commit v3 on v2

--- a/solution.py
+++ b/solution.py
@@ -23,7 +23,7 @@
 X, Y, Z, ZL = (4, 4, 16, 4)
 ZH = Z // ZL
 PLANE = Y * Z
-LARGE = 60 * 1024 * 1024
+LARGE = 16 * 1024 * 1024
 SMALL = 8 * 1024 * 1024
 F32 = jnp.float32
 BF16 = jnp.bfloat16
@@ -42,6 +42,7 @@
     return forward, inverse, lags
 
 
+ANY = pl.BlockSpec(memory_space=pl.ANY)
 SMEM = pl.BlockSpec(memory_space=pltpu.SMEM)
 VMEM = pl.BlockSpec(memory_space=pltpu.VMEM)
 
@@ -50,12 +51,12 @@
     return jax.ShapeDtypeStruct(dims, dtype)
 
 
-def cols(rows):
-    return pl.BlockSpec((rows, WIDTH), lambda j: (0, j))
-
-
-def whole(*dims):
-    return pl.BlockSpec(dims, lambda j: (0,) * len(dims))
+def cols(ref, step):
+    return ref.at[:, pl.ds(step * WIDTH, WIDTH)]
+
+
+def blocks(ref, step):
+    return ref.at[:, pl.ds(step * PER, PER)]
 
 
 def cost(args, outs, flops):
@@ -75,16 +76,51 @@
     )(*args)
 
 
-def large(kernel, outs, out_specs, args, in_specs, scratch=(), flops=0):
+def large(kernel, outs, out_cuts, args, in_cuts, scratch=(), flops=0):
+    cuts = list(in_cuts) + list(out_cuts)
+    cut_at = [i for i, cut in enumerate(cuts) if cut in (cols, blocks)]
+    like = list(args) + list(outs)
+
+    def stepped(*refs):
+        count = len(cuts)
+        far = list(refs[:count])
+        extra = refs[count : count + len(scratch)]
+        near = dict(zip(cut_at, refs[count + len(scratch) :]))
+        sems = refs[-1]
+
+        def copy(i, step):
+            ends = [cuts[i](ref, step) for ref in (far[i], near[i])]
+            if i >= len(args):
+                ends.reverse()
+            return pltpu.make_async_copy(*ends, sems.at[cut_at.index(i) * STEPS + step])
+
+        loads = [[copy(i, step) for i in cut_at if i < len(args)] for step in range(STEPS)]
+        stores = [[copy(i, step) for i in cut_at if i >= len(args)] for step in range(STEPS)]
+        for step in range(STEPS):
+            for load in loads[step]:
+                load.start()
+        for step in range(STEPS):
+            for load in loads[step]:
+                load.wait()
+            views = [cuts[i](near[i], step) if i in near else far[i] for i in range(count)]
+            kernel(step, *views, *extra)
+            for store in stores[step]:
+                store.start()
+        for step in range(STEPS):
+            for store in stores[step]:
+                store.wait()
+
+    specs = [ANY if i in cut_at else (VMEM if cuts[i] is None else cuts[i]) for i in range(len(cuts))]
     return pl.pallas_call(
-        kernel,
-        grid=(STEPS,),
+        stepped,
         out_shape=tuple(outs),
-        in_specs=in_specs,
-        out_specs=tuple(out_specs),
-        scratch_shapes=list(scratch),
+        in_specs=specs[: len(args)],
+        out_specs=tuple(specs[len(args) :]),
+        scratch_shapes=list(scratch)
+        + [pltpu.VMEM(like[i].shape, like[i].dtype) for i in cut_at]
+        + [pltpu.SemaphoreType.DMA((len(cut_at) * STEPS,))],
         compiler_params=pltpu.CompilerParams(vmem_limit_bytes=LARGE),
-        cost_estimate=cost(args, outs, flops),
+        cost_estimate=pl.CostEstimate(flops=flops, bytes_accessed=1024, transcendentals=0),
     )(*args)
 
 
@@ -94,23 +130,23 @@
     )
 
 
-def row(ref):
-    at = pl.program_id(0) * PER
-    return jnp.concatenate([ref[pl.ds(at + i, 1), :] for i in range(PER)], axis=1)
-
-
-def put_row(ref, value):
-    at = pl.program_id(0) * PER
+def row(ref, step):
+    at = step * PER
+    return jnp.concatenate([ref[at + i : at + i + 1, :] for i in range(PER)], axis=1)
+
+
+def put_row(ref, step, value):
+    at = step * PER
     for i in range(PER):
-        ref[pl.ds(at + i, 1), :] = value[:, i * LANES : (i + 1) * LANES]
+        ref[at + i : at + i + 1, :] = value[:, i * LANES : (i + 1) * LANES]
 
 
 def fold(value):
     return sum(value[:, i * LANES : (i + 1) * LANES] for i in range(PER))
 
 
-def row_mean(parts_ref):
-    packed = jnp.sum(parts_ref[...], axis=0) / CHANNEL_TOTAL
+def row_mean(total_ref):
+    packed = total_ref[...] / CHANNEL_TOTAL
     return jnp.concatenate(
         [jnp.broadcast_to(packed[i : i + 1], (LANES, LANES)).T for i in range(ROWS // LANES)], axis=0
     )
@@ -120,27 +156,22 @@
     return jnp.concatenate([value] * PER, axis=1)
 
 
-def spread_rows(acc, out_ref):
+def pack_rows(acc, out_ref):
     total = jnp.sum(acc.T, axis=0, keepdims=True)
-    packed = jnp.concatenate([total[:, :LANES], total[:, LANES:], jnp.zeros((6, LANES), F32)], axis=0)
-    out_ref[...] = jnp.broadcast_to(packed, out_ref.shape)
-
-
-def start_kernel(stream_ref, out_ref, cot_ref, rate_ref, squares_ref, spread_ref, local_ref, acc_ref, first_ref):
-    step = pl.program_id(0)
+    out_ref[...] = jnp.concatenate([total[:, :LANES], total[:, LANES:]], axis=0)
+
+
+def squares_kernel(step, stream_ref, squares_ref, acc_ref):
     value = stream_ref[...].astype(F32)
     squares = fold(value * value)
-
-    @pl.when(step == 0)
-    def _():
-        acc_ref[...] = squares
-
-    @pl.when(step > 0)
-    def _():
-        acc_ref[...] += squares
-
+    acc_ref[...] = squares if step == 0 else acc_ref[...] + squares
+    if step == STEPS - 1:
+        pack_rows(acc_ref[...], squares_ref)
+
+
+def scan_kernel(step, out_ref, cot_ref, rate_ref, spread_ref, local_ref, first_ref):
     rank = lax.broadcasted_iota(jnp.int32, (8, WIDTH), 0)
-    rate = row(rate_ref)
+    rate = row(rate_ref, step)
     source = out_ref[...].astype(F32) * cot_ref[...].astype(F32)
     coefs = [(s, jnp.where(rank < 8 - s, jnp.exp(-float(s) * rate), 0.0)) for s in (1, 2, 4)]
     power = jnp.exp(-rate * (8 - rank).astype(F32))
@@ -152,11 +183,8 @@
         value = value + power * carry
         local_ref[group * 8 : group * 8 + 8, :] = value
         carry = value[0:1, :]
-    put_row(first_ref, carry)
-
-    @pl.when(step == STEPS - 1)
-    def _():
-        spread_rows(acc_ref[...], squares_ref)
+    put_row(first_ref, step, carry)
+    if step == STEPS - 1:
         spread_ref[...] = jnp.broadcast_to(first_ref[...], spread_ref.shape)
 
 
@@ -194,12 +222,11 @@
     carry_ref[...] = jnp.where(core == 0, parts_ref[y * 2 + 1, 2] + decay * last, last)
 
 
-def norm_kernel(total_ref, after_ref, inv_ref):
-    inv_ref[...] = lax.rsqrt(row_mean(total_ref) + EPSILON)
-
-
-def product_kernel(inv_ref, stream_ref, key_ref, gain_ref, product_ref, rim_ref):
-    normed = stream_ref[...].astype(F32) * widen(inv_ref[...]) * row(gain_ref)
+def product_kernel(step, total_ref, stream_ref, key_ref, gain_ref, product_ref, rim_ref, inv_ref):
+    if step == 0:
+        inv_ref[...] = lax.rsqrt(row_mean(total_ref) + EPSILON)
+
+    normed = stream_ref[...].astype(F32) * widen(inv_ref[...]) * row(gain_ref, step)
     product = key_ref[...].astype(F32) * normed
     product_ref[...] = product.astype(BF16)
     rim_ref[...] = product[ROWS - TAPS :, :]
@@ -217,24 +244,24 @@
     return jnp.concatenate([ar * br - ai * bi, ar * bi + ai * br], axis=0).astype(BF16)
 
 
-def grad_stored(local_ref, rate_ref, scale_ref, carry_ref):
-    rate = row(rate_ref)
+def grad_stored(step, local_ref, rate_ref, scale_ref, carry_ref):
+    rate = row(rate_ref, step)
     rank = lax.broadcasted_iota(jnp.int32, (8, WIDTH), 0)
-    power = jnp.exp(-rate * (8 - rank).astype(F32)) * row(carry_ref)
+    power = jnp.exp(-rate * (8 - rank).astype(F32)) * row(carry_ref, step)
     groups = []
     for group in range(ROWS // 8):
         far = power * jnp.exp(-rate * float(ROWS - 8 - 8 * group))
         groups.append(local_ref[group * 8 : group * 8 + 8, :] + far)
-    return jnp.concatenate(groups, axis=0) * row(scale_ref)
+    return jnp.concatenate(groups, axis=0) * row(scale_ref, step)
 
 
 def filter_kernel(
-    place_ref, fwd_ref, lag_ref, product_ref, rim_ref, local_ref, query_ref, rate_ref, scale_ref, carry_ref,
+    step, place_ref, fwd_ref, lag_ref, product_ref, rim_ref, local_ref, query_ref, rate_ref, scale_ref, carry_ref,
     keep_ref, send_ref, mixed_grad_ref, head_ref,
 ):
     ext = jnp.concatenate([rim_ref[...].astype(BF16), product_ref[...]], axis=0)
     product = dot(fwd_ref[...], ext)
-    grad_mixed = query_ref[...].astype(F32) * grad_stored(local_ref, rate_ref, scale_ref, carry_ref)
+    grad_mixed = query_ref[...].astype(F32) * grad_stored(step, local_ref, rate_ref, scale_ref, carry_ref)
     head_ref[...] = grad_mixed[:TAPS]
     grad_mixed = grad_mixed.astype(BF16)
     mixed_grad_ref[...] = grad_mixed
@@ -252,64 +279,74 @@
 
 
 def query_kernel(
-    fwd_ref, inv_ref, product_ref, rim_ref, local_ref, filter_ref, rate_ref, scale_ref, carry_ref, grad_ref, token_ref
+    step, fwd_ref, inv_ref, product_ref, rim_ref, local_ref, filter_ref, rate_ref, scale_ref, carry_ref, grad_ref, token_ref
 ):
     ext = jnp.concatenate([rim_ref[...].astype(BF16), product_ref[...]], axis=0)
     product = dot(fwd_ref[...], ext)
     taps = dot(fwd_ref[:, :TAPS], filter_ref[...].astype(BF16))
     mixed = dot(inv_ref[TAPS:, :], mul(product, taps)) * (2.0 / POINTS)
-    grad_ref[...] = (mixed * grad_stored(local_ref, rate_ref, scale_ref, carry_ref)).astype(BF16)
-    token_ref[...] = carry_ref[...]
+    grad_ref[...] = (mixed * grad_stored(step, local_ref, rate_ref, scale_ref, carry_ref)).astype(BF16)
+    if step == STEPS - 1:
+        token_ref[...] = carry_ref[...]
 
 
 def weighted_kernel(
-    fwd_ref, inv_ref, grad_ref, after_ref, filter_ref, key_ref, stream_ref, gain_ref, weighted_ref, dots_ref, acc_ref
+    step, later_ref, fwd_ref, inv_ref, grad_ref, after_ref, filter_ref, key_ref, stream_ref, gain_ref, weighted_ref, dots_ref, acc_ref
 ):
-    step = pl.program_id(0)
     ext = jnp.concatenate([grad_ref[...], after_ref[...].astype(BF16)], axis=0)
     grad = dot(fwd_ref[...], ext)
     taps = dot(fwd_ref[:, :TAPS], filter_ref[...].astype(BF16))
     back = dot(inv_ref[:ROWS, :], mul_conj(taps, grad)) * (2.0 / POINTS)
-    weighted = row(gain_ref) * key_ref[...].astype(F32) * back
+    weighted = row(gain_ref, step) * key_ref[...].astype(F32) * back
     weighted_ref[...] = weighted
     dots = fold(weighted * stream_ref[...].astype(F32))
 
-    @pl.when(step == 0)
-    def _():
+    if step == 0:
         acc_ref[...] = dots
-
-    @pl.when(step > 0)
-    def _():
+    else:
         acc_ref[...] += dots
 
-    @pl.when(step == STEPS - 1)
-    def _():
-        spread_rows(acc_ref[...], dots_ref)
-
-
-def stream_kernel(inv_ref, dots_ref, weighted_ref, stream_ref, out_ref, token_ref, factor_ref):
+    if step == STEPS - 1:
+        pack_rows(acc_ref[...], dots_ref)
+
+
+def stream_kernel(step, inv_ref, dots_ref, weighted_ref, stream_ref, out_ref, factor_ref):
     inv = inv_ref[...]
 
-    @pl.when(pl.program_id(0) == 0)
-    def _():
+    if step == 0:
         factor_ref[...] = inv * inv * row_mean(dots_ref)
 
     value = weighted_ref[...] - stream_ref[...].astype(F32) * widen(factor_ref[...])
     out_ref[...] = (widen(inv) * value).astype(BF16)
-    token_ref[...] = factor_ref[0:8, :]
+
+
+def fence_kernel(value_ref, after_ref, out_ref):
+    pass
+
+
+def after_all(value, *others):
+    return pl.pallas_call(
+        fence_kernel,
+        out_shape=shape(value.shape, value.dtype),
+        in_specs=[ANY] * (1 + len(others)),
+        out_specs=ANY,
+        input_output_aliases={0: 0},
+        compiler_params=pltpu.CompilerParams(vmem_limit_bytes=LARGE),
+    )(value, *others)
+
+
+def gate_kernel(value_ref, after_ref, out_ref):
+    out_ref[...] = value_ref[...]
 
 
 def add_kernel(a_ref, b_ref, out_ref):
     out_ref[...] = a_ref[...] + b_ref[...]
 
 
-def spread_sum_kernel(parts_ref, after_ref, spread_ref):
+def spread_sum_kernel(parts_ref, *refs):
+    spread_ref = refs[-1]
     total = jnp.sum(parts_ref[...], axis=0)
     spread_ref[...] = jnp.broadcast_to(total, spread_ref.shape)
-
-
-def fence_kernel(value_ref, after_ref, out_ref):
-    out_ref[...] = value_ref[...]
 
 
 def finish_kernel(place_ref, own_ref, other_ref, filter_ref, residue_ref, filter_out, residue_out):
@@ -343,24 +380,23 @@
     swap = [(0, 1), (1, 0)]
     seq = ("y", "zh", "zl", "core")
     count = 2 * PLANE
-    dense, table = (whole(*DENSE), whole(POINTS, POINTS))
-
-    shares = (X,) + DENSE
-    squares, spread, local = large(
-        start_kernel, [shape(shares), shape((Z,) + DENSE), shape(FULL)],
-        [whole(*shares), whole(Z, *DENSE), cols(ROWS)],
-        (stream, gate_out, cotangent, rate), [cols(ROWS)] * 3 + [dense],
-        scratch=[pltpu.VMEM((ROWS, LANES), F32), pltpu.VMEM(DENSE, F32)],
-    )
-    squares = lax.all_to_all(squares, "chan", 0, 0, tiled=True)
+
+    packed = (ROWS // LANES, LANES)
+    spread, local = large(
+        scan_kernel, [shape((Z,) + DENSE), shape(FULL)], [None, cols], (gate_out, cotangent, rate),
+        [cols, cols, None], scratch=[pltpu.VMEM(DENSE, F32)],
+    )
     column = lax.all_to_all(spread, ("zh", "zl"), 0, 0, tiled=True)
-    thin = whole(ROWS, LANES)
-    (inv,) = small(norm_kernel, [shape((ROWS, LANES))], squares, column)
-    product, rim = large(
-        product_kernel, [shape(FULL, BF16), shape((TAPS, CHANS))], [cols(ROWS), cols(TAPS)],
-        (inv, stream, gate_key, gain), [thin, cols(ROWS), cols(ROWS), dense],
-    )
-    before = lax.ppermute(rim, seq, [(i, i + 1) for i in range(count - 1)])
+    (squares,) = large(
+        squares_kernel, [shape(packed)], [None], (stream,), [cols], scratch=[pltpu.VMEM((ROWS, LANES), F32)]
+    )
+    squares = lax.psum(squares, "chan")
+    product, rim, inv = large(
+        product_kernel, [shape(FULL, BF16), shape((TAPS, CHANS)), shape((ROWS, LANES))],
+        [cols, cols, None],
+        (squares, stream, gate_key, gain), [None, cols, cols, None],
+    )
+    before = lax.ppermute(after_all(rim, column), seq, [(i, i + 1) for i in range(count - 1)])
     (sums,) = small(
         column_kernel, [shape((2 * Y, 3) + DENSE)], place, column, spread, rate, specs=[SMEM] + [VMEM] * 3
     )
@@ -368,12 +404,11 @@
     (carry,) = small(carry_kernel, [shape(DENSE)], place, sums, rate, specs=[SMEM] + [VMEM] * 2)
 
     half = (GROUPS // 2, TILES, 8, LANES)
-    blocks = pl.BlockSpec((GROUPS // 2, PER, 8, LANES), lambda j: (0, j, 0, 0))
     keep, send, grad_mixed, head = large(
         filter_kernel, [shape(half), shape(half), shape(FULL, BF16), shape((TAPS, CHANS))],
-        [blocks, blocks, cols(ROWS), cols(TAPS)],
+        [blocks, blocks, cols, cols],
         (place, forward, lags, product, before, local, gate_query, rate, scale, carry),
-        [SMEM, table, whole(TAPS, POINTS), cols(ROWS), cols(TAPS), cols(ROWS), cols(ROWS), dense, dense, dense],
+        [SMEM, None, None, cols, cols, cols, cols, None, None, None],
         flops=2 * CHANS * POINTS * (POINTS + ROWS + TAPS),
     )
 
@@ -382,32 +417,34 @@
     after = lax.ppermute(head, seq, [(i + 1, i) for i in range(count - 1)])
     parts = lax.all_to_all(chip_sum.reshape(PLANE, 8, LANES), ("y", "zl"), 0, 0, tiled=True)
     grad_query, token = large(
-        query_kernel, [shape(FULL, BF16), shape(DENSE)], [cols(ROWS), dense],
+        query_kernel, [shape(FULL, BF16), shape(DENSE)], [cols, None],
         (forward, inverse, product, before, local, medium_filter, rate, scale, carry),
-        [table, table, cols(ROWS), cols(TAPS), cols(ROWS), cols(TAPS), dense, dense, dense],
+        [None, None, cols, cols, cols, cols, None, None, None],
         flops=2 * CHANS * POINTS * (POINTS + ROWS + TAPS),
     )
     mine = (ZH, 8, LANES)
     (spread,) = small(
-        spread_sum_kernel, [shape((ZH,) + mine)], parts.reshape((Y * ZL,) + mine), token
+        spread_sum_kernel, [shape((ZH,) + mine)], parts.reshape((Y * ZL,) + mine), token, specs=[VMEM, ANY]
     )
     parts = lax.all_to_all(spread, "zh", 0, 0, tiled=True)
     weighted, dots = large(
-        weighted_kernel, [shape(FULL), shape(shares)], [cols(ROWS), whole(*shares)],
-        (forward, inverse, grad_mixed, after, medium_filter, gate_key, stream, gain),
-        [table, table, cols(ROWS), cols(TAPS), cols(TAPS), cols(ROWS), cols(ROWS), dense],
+        weighted_kernel, [shape(FULL), shape(packed)], [cols, None],
+        (spread, forward, inverse, grad_mixed, after, medium_filter, gate_key, stream, gain),
+        [ANY, None, None, cols, cols, cols, cols, cols, None],
         scratch=[pltpu.VMEM((ROWS, LANES), F32)],
         flops=2 * CHANS * POINTS * (POINTS + ROWS + TAPS),
     )
-    (spread,) = small(spread_sum_kernel, [shape((Y * ZL,) + mine)], parts, dots)
-    dots = lax.all_to_all(dots, "chan", 0, 0, tiled=True)
+    (spread,) = small(
+        spread_sum_kernel, [shape((Y * ZL,) + mine)], parts, dots, specs=[VMEM, ANY]
+    )
+    dots = lax.psum(dots, "chan")
     own_half = lax.all_to_all(spread, ("y", "zl"), 0, 0, tiled=True).reshape(PLANE, 8, LANES)
-    grad_stream, token = large(
-        stream_kernel, [shape(FULL, BF16), shape(DENSE)], [cols(ROWS), dense],
-        (inv, dots, weighted, stream), [thin, whole(*shares)] + [cols(ROWS)] * 2,
+    (grad_stream,) = large(
+        stream_kernel, [shape(FULL, BF16)], [cols],
+        (inv, dots, weighted, stream), [None, None] + [cols] * 2,
         scratch=[pltpu.VMEM((ROWS, LANES), F32)],
     )
-    (own_half,) = small(fence_kernel, [shape(own_half.shape)], own_half, token)
+    (own_half,) = small(gate_kernel, [shape(own_half.shape)], own_half, dots, specs=[VMEM, ANY])
     other_half = lax.ppermute(own_half, "core", swap)
     grad_filter, grad_residue = small(
         finish_kernel, [shape((TAPS, CHANS)), shape(DENSE)], place, own_half, other_half, medium_filter,

time: 140 us -> 124 us (0.89)
  blocking collectives: 35.6 us -> 15 us
  starting transfers between devices: 37.7 us -> 55.1 us
  Pallas kernels: 32.7 us -> 20.6 us
  local copies, waits for them, and re-layouts: 6.36 us -> 13.2 us
  waiting for transfers between devices: 24.2 us -> 17.7 us
    all_to_all x2 -> x0, blocking collectives: 35.6 us -> none  [the longest x1 26.6 us: body(): column = lax.all_to_all(spread, ('zh', 'zl'), 0, 0, tiled=True)]
    psum x0 -> x2, blocking collectives: none -> 15 us  [the longest x1 8.99 us: body(): squares = lax.psum(squares, 'chan')]
    all_to_all x1, starting transfers between devices: 3.37 us -> 15.9 us  [body(): column = lax.all_to_all(spread, ('zh', 'zl'), 0, 0, tiled=True)]
    pallas_call x6 -> x8, Pallas kernels: 27.3 us -> 15.4 us  [the longest x7 15.4 us: large(): pl.pallas_call(stepped, out_shape=tuple(outs), in_specs=specs[:len(args)]...]
    unnamed x32 -> x60, local copies, waits for them, and re-layouts: 6.36 us -> 13.2 us
    all_to_all x1, starting transfers between devices: 4 us -> 8.27 us  [body(): parts = lax.all_to_all(spread, 'zh', 0, 0, tiled=True)]
    all_to_all x1, waiting for transfers between devices: 3.43 us -> 0.81 us  [body(): column = lax.all_to_all(spread, ('zh', 'zl'), 0, 0, tiled=True)]
    all_to_all x1, waiting for transfers between devices: 4.37 us -> 1.98 us  [body(): lax.all_to_all(spread, ('y', 'zl'), 0, 0, tiled=True)]
  transfers between devices with their start and end apart: 9 -> 9, of which waited for: 7 -> 6; matrix products, arithmetic and copies ran while one was open for 0% -> 0% of each run, Pallas kernels for 13% -> 11%
where the time goes in v3:
time: 124 us; the launch traced here: 123 us
  starting transfers between devices  55.1 us (44%)
  Pallas kernels  20.6 us (17%)
  waiting for transfers between devices  17.7 us (14%)
  blocking collectives  15 us (12%)
  local copies, waits for them, and re-layouts  13.2 us (11%)
    all_to_all x1, starting transfers between devices, body(): column = lax.all_to_all(spread, ('zh', 'zl'), 0, 0, tiled=True)  15.9 us
    pallas_call x7, Pallas kernels, large(): pl.pallas_call(stepped, out_shape=tuple(outs), in_specs=specs[:len(args)]...  15.4 us
    unnamed x60, local copies, waits for them, and re-layouts  13.2 us
    psum x1, blocking collectives, body(): squares = lax.psum(squares, 'chan')  8.99 us
    all_to_all x1, starting transfers between devices, body(): parts = lax.all_to_all(spread, 'zh', 0, 0, tiled=True)  8.27 us
    all_to_all x1, waiting for transfers between devices, body(): sums = lax.all_to_all(sums, ('y', 'core'), 0, 0, tiled=True)  6.52 us
    psum x1, blocking collectives, body(): dots = lax.psum(dots, 'chan')  6.01 us
    ppermute x1, starting transfers between devices, body(): other_half = lax.ppermute(own_half, 'core', swap)  5.76 us
  transfers between devices with their start and end apart: 9, of which 6 were waited for; matrix products, arithmetic and copies ran while one was open for 0% of the time, Pallas kernels for 11%

profile of v3, /device:TPU:1, one launch (start us, length us, event | category | flops | bytes accessed | tf_op | source)
XLA Modules:
  0.0 122.8 jit_solution(7027680053853004308)
XLA Ops:
  3.4 1.6 %shard_map.149 = (f32[16,8,128]{2,1,0:T(8,128)}, f32[256,1024]{1,0:T(8,128)S(1)}) custom-call(bf16[256,1024]{1,0:T(8,128)(2,1)S(1)} %copy-done.14, bf16[256,1024]{1,0:T(8,128)(2,1)S(1)} %copy-done.15, f32[8,128]{1,0:T(8,128)S(1)} %bitcast.14), custom_call_target="tpu_custom_call" | custom-call | bytes 1024 | tf_op jit(solution)/shard_map/pallas_call | solution.py:114
  5.0 15.9 %all-to-all-start = ((f32[16,8,128]{2,1,0:T(8,128)}), f32[16,8,128]{2,1,0:T(8,128)S(1)}, u32[]{:S(2)}, u32[]{:S(2)}) async-start(f32[16,8,128]{2,1,0:T(8,128)} %get-tuple-element.21.first_ref), calls=%async_computation | async-start | bytes 131072 | tf_op jit(solution)/shard_map/all_to_all | solution.py:389
  21.3 9.0 %psum.14.refs_0_ = f32[2,128]{1,0:T(2,128)S(1)} all-reduce(f32[2,128]{1,0:T(2,128)S(1)} %shard_map.147), channel_id=1, replica_groups=mesh['y'=4,'zh'=4,'zl'=4,'core'=2,'chan'=4] {'chan'}, use_global_device_ids=true, to_apply=%region_0.0 | all-reduce | flops 256 | bytes 2048 | tf_op jit(solution)/shard_map/psum | solution.py:393
  33.3 5.2 %collective-permute-start = (f32[128,1024]{1,0:T(8,128)}, f32[128,1024]{1,0:T(8,128)S(1)}, u32[]{:S(2)}, u32[]{:S(2)}) collective-permute-start(f32[128,1024]{1,0:T(8,128)} %copy-done.16), channel_id=1, source_target_pairs={{0,4},{4,8},{8,12},{12,16},{16,20},{20,24},{24,28},{28,32},{32,36}... | collective-permute-start | bytes 1572872 | tf_op jit(solution)/shard_map/ppermute | solution.py:399
  40.2 4.7 %all-to-all-start.1 = ((f32[8,3,8,128]{3,2,1,0:T(8,128)}), f32[8,3,8,128]{3,2,1,0:T(8,128)S(1)}, u32[]{:S(2)}, u32[]{:S(2)}) async-start(f32[8,3,8,128]{3,2,1,0:T(8,128)} %copy-done.17), calls=%async_computation.1 | async-start | bytes 196608 | tf_op jit(solution)/shard_map/all_to_all | solution.py:403
  44.9 6.5 %all-to-all-done.1.parts_ref = f32[8,3,8,128]{3,2,1,0:T(8,128)S(1)} async-done(((f32[8,3,8,128]{3,2,1,0:T(8,128)}), f32[8,3,8,128]{3,2,1,0:T(8,128)S(1)}, u32[]{:S(2)}, u32[]{:S(2)}) %all-to-all-start.1) | async-done | bytes 98336 | tf_op jit(solution)/shard_map/all_to_all | solution.py:403
  54.4 3.7 %shard_map.154 = (f32[8,8,8,128]{3,2,1,0:T(8,128)S(1)}, f32[8,8,8,128]{3,2,1,0:T(8,128)S(1)}, bf16[256,1024]{1,0:T(8,128)(2,1)S(1)}, f32[128,1024]{1,0:T(8,128)S(1)}) custom-call(s32[3]{0:T(128)S(1)} %copy-done.28, bf16[384,384]{1,0:T(8,128)(2,1)S(1)} %copy-done.2, bf16[128,384]{1,0:T(8,128)(2,1)S(1)} %copy-done.22, ...), custom_call_target="tpu_custom_call" | custom-call | flops 603979776 | bytes 1024 | tf_op jit(solution)/shard_map/pallas_call | solution.py:114
  58.1 2.4 %collective-permute-start.1 = (f32[8,8,8,128]{3,2,1,0:T(8,128)S(1)}, f32[8,8,8,128]{3,2,1,0:T(8,128)S(1)}, u32[]{:S(2)}, u32[]{:S(2)}) collective-permute-start(f32[8,8,8,128]{3,2,1,0:T(8,128)S(1)} %get-tuple-element.26), channel_id=1, source_target_pairs={{0,4},{4,0},{1,5},{5,1},{2,6},{6,2},{3,7},{7,3},{8,12},{12,8},{9,1... | collective-permute-start | bytes 786440 | tf_op jit(solution)/shard_map/ppermute | solution.py:415
  60.5 1.1 collective-permute-done.1.b_ref
  62.4 5.1 %all-to-all-start.2 = ((f32[64,8,128]{2,1,0:T(8,128)}), f32[64,8,128]{2,1,0:T(8,128)}, u32[]{:S(2)}, u32[]{:S(2)}) async-start(f32[64,8,128]{2,1,0:T(8,128)} %bitcast.12), calls=%async_computation.2 | async-start | bytes 524288 | tf_op jit(solution)/shard_map/all_to_all | solution.py:418
  67.5 2.6 %collective-permute-start.2 = (f32[128,1024]{1,0:T(8,128)}, f32[128,1024]{1,0:T(8,128)}, u32[]{:S(2)}, u32[]{:S(2)}) collective-permute-start(f32[128,1024]{1,0:T(8,128)} %copy-done.29), channel_id=1, source_target_pairs={{4,0},{8,4},{12,8},{16,12},{20,16},{24,20},{28,24},{32,28},{36,32}... | collective-permute-start | bytes 1572872 | tf_op jit(solution)/shard_map/ppermute | solution.py:417
  72.1 3.8 %shard_map.153 = (bf16[256,1024]{1,0:T(8,128)(2,1)}, f32[8,128]{1,0:T(8,128)S(1)}) custom-call(bf16[384,384]{1,0:T(8,128)(2,1)S(1)} %copy-done.2, bf16[384,384]{1,0:T(8,128)(2,1)S(1)} %copy-done.6, bf16[256,1024]{1,0:T(8,128)(2,1)S(1)} %get-tuple-element.19.refs_2_.refs_3_, f32[128,1024]{1,0:T(8,128)S(1)} %copy-done.5, ...), custom_call_target="tpu_custom_call" | custom-call | flops 603979776 | bytes 1024 | tf_op jit(solution)/shard_map/pallas_call | solution.py:114
  75.9 1.5 %all-to-all-done.2 = f32[64,8,128]{2,1,0:T(8,128)} async-done(((f32[64,8,128]{2,1,0:T(8,128)}), f32[64,8,128]{2,1,0:T(8,128)}, u32[]{:S(2)}, u32[]{:S(2)}) %all-to-all-start.2) | async-done | bytes 262176 | tf_op jit(solution)/shard_map/all_to_all | solution.py:418
  77.4 1.6 %shard_map.156.refs_0_ = f32[4,4,8,128]{3,2,1,0:T(8,128)} custom-call(f32[16,4,8,128]{3,2,1,0:T(8,128)} %bitcast.7.parts_ref, f32[8,128]{1,0:T(8,128)S(1)} %get-tuple-element.27.refs_0_), custom_call_target="tpu_custom_call" | custom-call | bytes 331776 | tf_op jit(solution)/shard_map/pallas_call | solution.py:69
  79.0 8.3 %all-to-all-start.3 = ((f32[4,4,8,128]{3,2,1,0:T(8,128)}), f32[4,4,8,128]{3,2,1,0:T(8,128)S(1)}, u32[]{:S(2)}, u32[]{:S(2)}) async-start(f32[4,4,8,128]{3,2,1,0:T(8,128)} %shard_map.156.refs_0_), calls=%async_computation.3 | async-start | bytes 131072 | tf_op jit(solution)/shard_map/all_to_all | solution.py:429
  88.4 4.0 %shard_map.157 = (f32[256,1024]{1,0:T(8,128)S(1)}, f32[2,128]{1,0:T(2,128)S(1)}) custom-call(f32[4,4,8,128]{3,2,1,0:T(8,128)} %shard_map.156.refs_0_, bf16[384,384]{1,0:T(8,128)(2,1)S(1)} %copy-done.2, bf16[384,384]{1,0:T(8,128)(2,1)S(1)} %copy-done.7, bf16[256,1024]{1,0:T(8,128)(2,1)S(1)} %copy-done.13, f32[128,1024]{1,0:T(8,128)} %collective-permute-done.2.refs_4_, ...), custom_call_target="tpu_custom_call" | custom-call | flops 603979776 | bytes 1024 | tf_op jit(solution)/shard_map/pallas_call | solution.py:114
  93.3 5.7 %all-to-all-done.3.parts_ref = f32[4,4,8,128]{3,2,1,0:T(8,128)S(1)} async-done(((f32[4,4,8,128]{3,2,1,0:T(8,128)}), f32[4,4,8,128]{3,2,1,0:T(8,128)S(1)}, u32[]{:S(2)}, u32[]{:S(2)}) %all-to-all-start.3) | async-done | bytes 65568 | tf_op jit(solution)/shard_map/all_to_all | solution.py:429
  99.7 5.3 %all-to-all-start.4 = ((f32[16,4,8,128]{3,2,1,0:T(8,128)}), f32[16,4,8,128]{3,2,1,0:T(8,128)S(1)}, u32[]{:S(2)}, u32[]{:S(2)}) async-start(f32[16,4,8,128]{3,2,1,0:T(8,128)} %shard_map.159), calls=%async_computation.4 | async-start | bytes 524288 | tf_op jit(solution)/shard_map/all_to_all | solution.py:441
  105.1 6.0 %psum.15.refs_1_.after_ref = f32[2,128]{1,0:T(2,128)S(1)} all-reduce(f32[2,128]{1,0:T(2,128)S(1)} %get-tuple-element.30.refs_0_), channel_id=1, replica_groups=mesh['y'=4,'zh'=4,'zl'=4,'core'=2,'chan'=4] {'chan'}, use_global_device_ids=true, to_apply=%region_1.0 | all-reduce | flops 256 | bytes 2048 | tf_op jit(solution)/shard_map/psum | solution.py:440
  111.1 2.0 %all-to-all-done.4 = f32[16,4,8,128]{3,2,1,0:T(8,128)S(1)} async-done(((f32[16,4,8,128]{3,2,1,0:T(8,128)}), f32[16,4,8,128]{3,2,1,0:T(8,128)S(1)}, u32[]{:S(2)}, u32[]{:S(2)}) %all-to-all-start.4) | async-done | bytes 262176 | tf_op jit(solution)/shard_map/all_to_all | solution.py:441
  113.1 5.8 %collective-permute-start.3 = (f32[64,8,128]{2,1,0:T(8,128)S(1)}, f32[64,8,128]{2,1,0:T(8,128)S(1)}, u32[]{:S(2)}, u32[]{:S(2)}) collective-permute-start(f32[64,8,128]{2,1,0:T(8,128)S(1)} %shard_map.160.own_ref), channel_id=1, source_target_pairs={{0,4},{4,0},{1,5},{5,1},{2,6},{6,2},{3,7},{7,3},{8,12},{12,8},{9,1... | collective-permute-start | bytes 786440 | tf_op jit(solution)/shard_map/ppermute | solution.py:448
  118.9 1.2 copy-done.10
  120.1 1.2 shard_map.158
  121.3 1.4 %shard_map.161 = (f32[128,1024]{1,0:T(8,128)}, f32[8,128]{1,0:T(8,128)}) custom-call(s32[3]{0:T(128)S(1)} %copy-done.28, f32[64,8,128]{2,1,0:T(8,128)S(1)} %shard_map.160.own_ref, f32[64,8,128]{2,1,0:T(8,128)S(1)} %collective-permute-done.3.other_ref, f32[128,1024]{1,0:T(8,128)S(1)} %copy-done.1, f32[8,128]{1,0:T(8,128)S(1)} %bitcast.21), custom_call_target="tpu_custom_call" | custom-call | bytes 1581068 | tf_op jit(solution)/shard_map/pallas_call | solution.py:69
  (73 shorter events, 16.2 us)
Async XLA Ops:
  3.4 17.5 %copy-start = (bf16[256,1024]{1,0:T(8,128)(2,1)S(1)}, bf16[256,1024]{1,0:T(8,128)(2,1)}, u32[]{:S(2)}) copy-start(bf16[256,1024]{1,0:T(8,128)(2,1)} %refs_3_.1) | copy-start | bytes 1572868
  5.0 25.3 %copy-start.3 = (bf16[256,1024]{1,0:T(8,128)(2,1)S(1)}, bf16[256,1024]{1,0:T(8,128)(2,1)}, u32[]{:S(2)}) copy-start(bf16[256,1024]{1,0:T(8,128)(2,1)} %refs_6_.3) | copy-start | bytes 1572868
  5.0 27.5 %all-to-all-start = ((f32[16,8,128]{2,1,0:T(8,128)}), f32[16,8,128]{2,1,0:T(8,128)S(1)}, u32[]{:S(2)}, u32[]{:S(2)}) async-start(f32[16,8,128]{2,1,0:T(8,128)} %get-tuple-element.21.first_ref), calls=%async_computation | async-start | bytes 131072 | tf_op jit(solution)/shard_map/all_to_all | solution.py:389
  20.9 9.4 %copy-start.23 = (f32[1024]{0:T(1024)S(1)}, f32[1024]{0:T(1024)}, u32[]{:S(2)}) copy-start(f32[1024]{0:T(1024)} %param.13) | copy-start | bytes 12292
  32.5 6.1 %copy-start.19 = (f32[1024]{0:T(1024)S(1)}, f32[1024]{0:T(1024)}, u32[]{:S(2)}) copy-start(f32[1024]{0:T(1024)} %param.20) | copy-start | bytes 12292
  33.3 19.4 %copy-start.2 = (bf16[384,384]{1,0:T(8,128)(2,1)S(1)}, bf16[384,384]{1,0:T(8,128)(2,1)}, u32[]{:S(2)}) copy-start(bf16[384,384]{1,0:T(8,128)(2,1)} %constant.28.clone.refs_0_.refs_1_) | copy-start | bytes 884740
  33.3 19.3 %collective-permute-start = (f32[128,1024]{1,0:T(8,128)}, f32[128,1024]{1,0:T(8,128)S(1)}, u32[]{:S(2)}, u32[]{:S(2)}) collective-permute-start(f32[128,1024]{1,0:T(8,128)} %copy-done.16), channel_id=1, source_target_pairs={{0,4},{4,8},{8,12},{12,16},{16,20},{20,24},{24,28},{28,32},{32,36}... | collective-permute-start | bytes 1572872 | tf_op jit(solution)/shard_map/ppermute | solution.py:399
  40.2 4.7 %copy-start.24 = (f32[1024]{0:T(1024)S(1)}, f32[1024]{0:T(1024)}, u32[]{:S(2)}) copy-start(f32[1024]{0:T(1024)} %param.19) | copy-start | bytes 12292
  40.2 11.2 %all-to-all-start.1 = ((f32[8,3,8,128]{3,2,1,0:T(8,128)}), f32[8,3,8,128]{3,2,1,0:T(8,128)S(1)}, u32[]{:S(2)}, u32[]{:S(2)}) async-start(f32[8,3,8,128]{3,2,1,0:T(8,128)} %copy-done.17), calls=%async_computation.1 | async-start | bytes 196608 | tf_op jit(solution)/shard_map/all_to_all | solution.py:403
  52.7 5.4 %copy-start.4 = (f32[128,1024]{1,0:T(8,128)}, f32[128,1024]{1,0:T(8,128)S(1)}, u32[]{:S(2)}) copy-start(f32[128,1024]{1,0:T(8,128)S(1)} %collective-permute-done.refs_3_.refs_4_) | copy-start | bytes 1572868
  58.1 3.6 %copy-start.12 = (bf16[256,1024]{1,0:T(8,128)(2,1)}, bf16[256,1024]{1,0:T(8,128)(2,1)S(1)}, u32[]{:S(2)}) copy-start(bf16[256,1024]{1,0:T(8,128)(2,1)S(1)} %get-tuple-element.28.refs_3_) | copy-start | bytes 1572868
  58.1 3.6 %copy-start.29 = (f32[128,1024]{1,0:T(8,128)}, f32[128,1024]{1,0:T(8,128)S(1)}, u32[]{:S(2)}) copy-start(f32[128,1024]{1,0:T(8,128)S(1)} %get-tuple-element.29) | copy-start | bytes 1572868
  58.1 3.5 %collective-permute-start.1 = (f32[8,8,8,128]{3,2,1,0:T(8,128)S(1)}, f32[8,8,8,128]{3,2,1,0:T(8,128)S(1)}, u32[]{:S(2)}, u32[]{:S(2)}) collective-permute-start(f32[8,8,8,128]{3,2,1,0:T(8,128)S(1)} %get-tuple-element.26), channel_id=1, source_target_pairs={{0,4},{4,0},{1,5},{5,1},{2,6},{6,2},{3,7},{7,3},{8,12},{12,8},{9,1... | collective-permute-start | bytes 786440 | tf_op jit(solution)/shard_map/ppermute | solution.py:415
  61.6 8.4 %copy-start.1 = (f32[128,1024]{1,0:T(8,128)S(1)}, f32[128,1024]{1,0:T(8,128)}, u32[]{:S(2)}) copy-start(f32[128,1024]{1,0:T(8,128)} %filter_ref.1) | copy-start | bytes 1572868
  62.4 15.0 %all-to-all-start.2 = ((f32[64,8,128]{2,1,0:T(8,128)}), f32[64,8,128]{2,1,0:T(8,128)}, u32[]{:S(2)}, u32[]{:S(2)}) async-start(f32[64,8,128]{2,1,0:T(8,128)} %bitcast.12), calls=%async_computation.2 | async-start | bytes 524288 | tf_op jit(solution)/shard_map/all_to_all | solution.py:418
  67.5 19.8 %collective-permute-start.2 = (f32[128,1024]{1,0:T(8,128)}, f32[128,1024]{1,0:T(8,128)}, u32[]{:S(2)}, u32[]{:S(2)}) collective-permute-start(f32[128,1024]{1,0:T(8,128)} %copy-done.29), channel_id=1, source_target_pairs={{4,0},{8,4},{12,8},{16,12},{20,16},{24,20},{28,24},{32,28},{36,32}... | collective-permute-start | bytes 1572872 | tf_op jit(solution)/shard_map/ppermute | solution.py:417
  70.1 1.0 copy-start.5
  75.9 11.4 %copy-start.7 = (bf16[384,384]{1,0:T(8,128)(2,1)S(1)}, bf16[384,384]{1,0:T(8,128)(2,1)}, u32[]{:S(2)}) copy-start(bf16[384,384]{1,0:T(8,128)(2,1)} %constant.29.clone.refs_1_.refs_2_) | copy-start | bytes 884740
  79.0 20.0 %all-to-all-start.3 = ((f32[4,4,8,128]{3,2,1,0:T(8,128)}), f32[4,4,8,128]{3,2,1,0:T(8,128)S(1)}, u32[]{:S(2)}, u32[]{:S(2)}) async-start(f32[4,4,8,128]{3,2,1,0:T(8,128)} %shard_map.156.refs_0_), calls=%async_computation.3 | async-start | bytes 131072 | tf_op jit(solution)/shard_map/all_to_all | solution.py:429
  99.7 13.3 %all-to-all-start.4 = ((f32[16,4,8,128]{3,2,1,0:T(8,128)}), f32[16,4,8,128]{3,2,1,0:T(8,128)S(1)}, u32[]{:S(2)}, u32[]{:S(2)}) async-start(f32[16,4,8,128]{3,2,1,0:T(8,128)} %shard_map.159), calls=%async_computation.4 | async-start | bytes 524288 | tf_op jit(solution)/shard_map/all_to_all | solution.py:441
  113.1 5.8 %copy-start.21 = (f32[256,128]{1,0:T(8,128)S(1)}, f32[256,128]{1,0:T(8,128)}, u32[]{:S(2)}) copy-start(f32[256,128]{1,0:T(8,128)} %copy-done.20) | copy-start | bytes 393220
  113.1 8.2 %collective-permute-start.3 = (f32[64,8,128]{2,1,0:T(8,128)S(1)}, f32[64,8,128]{2,1,0:T(8,128)S(1)}, u32[]{:S(2)}, u32[]{:S(2)}) collective-permute-start(f32[64,8,128]{2,1,0:T(8,128)S(1)} %shard_map.160.own_ref), channel_id=1, source_target_pairs={{0,4},{4,0},{1,5},{5,1},{2,6},{6,2},{3,7},{7,3},{8,12},{12,8},{9,1... | collective-permute-start | bytes 786440 | tf_op jit(solution)/shard_map/ppermute | solution.py:448
  118.9 1.2 copy-start.10
  120.1 1.2 copy-start.25
  (15 other events, 12.8 us)

commit v4 on v3

--- a/solution.py
+++ b/solution.py
@@ -43,7 +43,6 @@
 
 
 ANY = pl.BlockSpec(memory_space=pl.ANY)
-SMEM = pl.BlockSpec(memory_space=pltpu.SMEM)
 VMEM = pl.BlockSpec(memory_space=pltpu.VMEM)
 
 
@@ -76,50 +75,23 @@
     )(*args)
 
 
-def large(kernel, outs, out_cuts, args, in_cuts, scratch=(), flops=0):
+def large(kernel, outs, out_cuts, args, in_cuts, scratch=(), flops=0, grant=LARGE):
     cuts = list(in_cuts) + list(out_cuts)
-    cut_at = [i for i, cut in enumerate(cuts) if cut in (cols, blocks)]
-    like = list(args) + list(outs)
 
     def stepped(*refs):
-        count = len(cuts)
-        far = list(refs[:count])
-        extra = refs[count : count + len(scratch)]
-        near = dict(zip(cut_at, refs[count + len(scratch) :]))
-        sems = refs[-1]
-
-        def copy(i, step):
-            ends = [cuts[i](ref, step) for ref in (far[i], near[i])]
-            if i >= len(args):
-                ends.reverse()
-            return pltpu.make_async_copy(*ends, sems.at[cut_at.index(i) * STEPS + step])
-
-        loads = [[copy(i, step) for i in cut_at if i < len(args)] for step in range(STEPS)]
-        stores = [[copy(i, step) for i in cut_at if i >= len(args)] for step in range(STEPS)]
+        arrays, extra = (refs[: len(cuts)], refs[len(cuts) :])
         for step in range(STEPS):
-            for load in loads[step]:
-                load.start()
-        for step in range(STEPS):
-            for load in loads[step]:
-                load.wait()
-            views = [cuts[i](near[i], step) if i in near else far[i] for i in range(count)]
+            views = [cut(ref, step) if cut in (cols, blocks) else ref for cut, ref in zip(cuts, arrays)]
             kernel(step, *views, *extra)
-            for store in stores[step]:
-                store.start()
-        for step in range(STEPS):
-            for store in stores[step]:
-                store.wait()
-
-    specs = [ANY if i in cut_at else (VMEM if cuts[i] is None else cuts[i]) for i in range(len(cuts))]
+
+    specs = [VMEM if cut in (cols, blocks, None) else cut for cut in cuts]
     return pl.pallas_call(
         stepped,
         out_shape=tuple(outs),
         in_specs=specs[: len(args)],
         out_specs=tuple(specs[len(args) :]),
-        scratch_shapes=list(scratch)
-        + [pltpu.VMEM(like[i].shape, like[i].dtype) for i in cut_at]
-        + [pltpu.SemaphoreType.DMA((len(cut_at) * STEPS,))],
-        compiler_params=pltpu.CompilerParams(vmem_limit_bytes=LARGE),
+        scratch_shapes=list(scratch),
+        compiler_params=pltpu.CompilerParams(vmem_limit_bytes=grant),
         cost_estimate=pl.CostEstimate(flops=flops, bytes_accessed=1024, transcendentals=0),
     )(*args)
 
@@ -188,8 +160,8 @@
         spread_ref[...] = jnp.broadcast_to(first_ref[...], spread_ref.shape)
 
 
-def column_kernel(place_ref, parts_ref, first_ref, rate_ref, out_ref):
-    z = place_ref[1]
+def column_kernel(parts_ref, first_ref, rate_ref, after_ref, out_ref):
+    z = lax.axis_index(("zh", "zl"))
     pace = rate_ref[...] * (-2.0 * ROWS)
     ahead = jnp.zeros(DENSE, F32)
     total = jnp.zeros(DENSE, F32)
@@ -205,8 +177,8 @@
     out_ref[:, 2] = jnp.broadcast_to(first_ref[0], (count,) + DENSE)
 
 
-def carry_kernel(place_ref, parts_ref, rate_ref, carry_ref):
-    y, z, core = (place_ref[0], place_ref[1], place_ref[2])
+def carry_kernel(parts_ref, rate_ref, carry_ref):
+    y, z, core = (lax.axis_index("y"), lax.axis_index(("zh", "zl")), lax.axis_index("core"))
     rate = rate_ref[...]
     decay = jnp.exp(-ROWS * rate)
     rest = jnp.exp(rate * (-2.0 * ROWS) * (Z - 1 - z).astype(F32))
@@ -222,7 +194,7 @@
     carry_ref[...] = jnp.where(core == 0, parts_ref[y * 2 + 1, 2] + decay * last, last)
 
 
-def product_kernel(step, total_ref, stream_ref, key_ref, gain_ref, product_ref, rim_ref, inv_ref):
+def product_kernel(step, after_ref, total_ref, stream_ref, key_ref, gain_ref, product_ref, rim_ref, inv_ref):
     if step == 0:
         inv_ref[...] = lax.rsqrt(row_mean(total_ref) + EPSILON)
 
@@ -256,7 +228,7 @@
 
 
 def filter_kernel(
-    step, place_ref, fwd_ref, lag_ref, product_ref, rim_ref, local_ref, query_ref, rate_ref, scale_ref, carry_ref,
+    step, fwd_ref, lag_ref, product_ref, rim_ref, local_ref, query_ref, rate_ref, scale_ref, carry_ref,
     keep_ref, send_ref, mixed_grad_ref, head_ref,
 ):
     ext = jnp.concatenate([rim_ref[...].astype(BF16), product_ref[...]], axis=0)
@@ -267,7 +239,7 @@
     mixed_grad_ref[...] = grad_mixed
     spectrum = dot(fwd_ref[:, :ROWS], grad_mixed)
     taps = dot(lag_ref[...], mul_conj(spectrum, product))
-    is_first = place_ref[2] == 0
+    is_first = lax.axis_index("core") == 0
     for group in range(GROUPS // 2):
         low = taps[group * 8 : group * 8 + 8, :]
         high = taps[TAPS // 2 + group * 8 : TAPS // 2 + group * 8 + 8, :]
@@ -310,29 +282,13 @@
         pack_rows(acc_ref[...], dots_ref)
 
 
-def stream_kernel(step, inv_ref, dots_ref, weighted_ref, stream_ref, out_ref, factor_ref):
-    inv = inv_ref[...]
-
+def stream_kernel(step, total_ref, dots_ref, weighted_ref, stream_ref, out_ref, inv_ref, factor_ref):
     if step == 0:
-        factor_ref[...] = inv * inv * row_mean(dots_ref)
+        inv_ref[...] = lax.rsqrt(row_mean(total_ref) + EPSILON)
+        factor_ref[...] = inv_ref[...] * inv_ref[...] * row_mean(dots_ref)
 
     value = weighted_ref[...] - stream_ref[...].astype(F32) * widen(factor_ref[...])
-    out_ref[...] = (widen(inv) * value).astype(BF16)
-
-
-def fence_kernel(value_ref, after_ref, out_ref):
-    pass
-
-
-def after_all(value, *others):
-    return pl.pallas_call(
-        fence_kernel,
-        out_shape=shape(value.shape, value.dtype),
-        in_specs=[ANY] * (1 + len(others)),
-        out_specs=ANY,
-        input_output_aliases={0: 0},
-        compiler_params=pltpu.CompilerParams(vmem_limit_bytes=LARGE),
-    )(value, *others)
+    out_ref[...] = (widen(inv_ref[...]) * value).astype(BF16)
 
 
 def gate_kernel(value_ref, after_ref, out_ref):
@@ -349,10 +305,10 @@
     spread_ref[...] = jnp.broadcast_to(total, spread_ref.shape)
 
 
-def finish_kernel(place_ref, own_ref, other_ref, filter_ref, residue_ref, filter_out, residue_out):
+def finish_kernel(own_ref, other_ref, filter_ref, residue_ref, filter_out, residue_out):
     scale = TOKENS ** (-0.5) * 2.0 / POINTS
     count = own_ref.shape[0]
-    is_first = place_ref[2] == 0
+    is_first = lax.axis_index("core") == 0
     for tile in range(TILES):
         lanes = slice(tile * LANES, (tile + 1) * LANES)
         total = jnp.zeros((8, LANES), F32)
@@ -375,8 +331,6 @@
     forward, inverse, lags = (jnp.asarray(t) for t in transform_tables())
     gain, rate, residue = (v.reshape(DENSE) for v in (norm_gain, long_rate, long_residue))
     scale = residue * jnp.sqrt(-jnp.expm1(-2.0 * rate))
-    z_at = lax.axis_index(("zh", "zl"))
-    place = jnp.stack([lax.axis_index("y"), z_at, lax.axis_index("core")]).astype(jnp.int32)
     swap = [(0, 1), (1, 0)]
     seq = ("y", "zh", "zl", "core")
     count = 2 * PLANE
@@ -384,31 +338,31 @@
     packed = (ROWS // LANES, LANES)
     spread, local = large(
         scan_kernel, [shape((Z,) + DENSE), shape(FULL)], [None, cols], (gate_out, cotangent, rate),
-        [cols, cols, None], scratch=[pltpu.VMEM(DENSE, F32)],
+        [cols, cols, None], scratch=[pltpu.VMEM(DENSE, F32)], grant=60 * 1024 * 1024,
     )
     column = lax.all_to_all(spread, ("zh", "zl"), 0, 0, tiled=True)
     (squares,) = large(
         squares_kernel, [shape(packed)], [None], (stream,), [cols], scratch=[pltpu.VMEM((ROWS, LANES), F32)]
     )
     squares = lax.psum(squares, "chan")
-    product, rim, inv = large(
-        product_kernel, [shape(FULL, BF16), shape((TAPS, CHANS)), shape((ROWS, LANES))],
-        [cols, cols, None],
-        (squares, stream, gate_key, gain), [None, cols, cols, None],
-    )
-    before = lax.ppermute(after_all(rim, column), seq, [(i, i + 1) for i in range(count - 1)])
+    product, rim = large(
+        product_kernel, [shape(FULL, BF16), shape((TAPS, CHANS))], [cols, cols],
+        (column, squares, stream, gate_key, gain), [ANY, None, cols, cols, None],
+        scratch=[pltpu.VMEM((ROWS, LANES), F32)],
+    )
+    before = lax.ppermute(rim, seq, [(i, i + 1) for i in range(count - 1)])
     (sums,) = small(
-        column_kernel, [shape((2 * Y, 3) + DENSE)], place, column, spread, rate, specs=[SMEM] + [VMEM] * 3
+        column_kernel, [shape((2 * Y, 3) + DENSE)], column, spread, rate, scale
     )
     sums = lax.all_to_all(sums, ("y", "core"), 0, 0, tiled=True)
-    (carry,) = small(carry_kernel, [shape(DENSE)], place, sums, rate, specs=[SMEM] + [VMEM] * 2)
+    (carry,) = small(carry_kernel, [shape(DENSE)], sums, rate)
 
     half = (GROUPS // 2, TILES, 8, LANES)
     keep, send, grad_mixed, head = large(
         filter_kernel, [shape(half), shape(half), shape(FULL, BF16), shape((TAPS, CHANS))],
         [blocks, blocks, cols, cols],
-        (place, forward, lags, product, before, local, gate_query, rate, scale, carry),
-        [SMEM, None, None, cols, cols, cols, cols, None, None, None],
+        (forward, lags, product, before, local, gate_query, rate, scale, carry),
+        [None, None, cols, cols, cols, cols, None, None, None],
         flops=2 * CHANS * POINTS * (POINTS + ROWS + TAPS),
     )
 
@@ -441,14 +395,14 @@
     own_half = lax.all_to_all(spread, ("y", "zl"), 0, 0, tiled=True).reshape(PLANE, 8, LANES)
     (grad_stream,) = large(
         stream_kernel, [shape(FULL, BF16)], [cols],
-        (inv, dots, weighted, stream), [None, None] + [cols] * 2,
-        scratch=[pltpu.VMEM((ROWS, LANES), F32)],
+        (squares, dots, weighted, stream), [None, None] + [cols] * 2,
+        scratch=[pltpu.VMEM((ROWS, LANES), F32)] * 2,
     )
     (own_half,) = small(gate_kernel, [shape(own_half.shape)], own_half, dots, specs=[VMEM, ANY])
     other_half = lax.ppermute(own_half, "core", swap)
     grad_filter, grad_residue = small(
-        finish_kernel, [shape((TAPS, CHANS)), shape(DENSE)], place, own_half, other_half, medium_filter,
-        residue, specs=[SMEM] + [VMEM] * 4,
+        finish_kernel, [shape((TAPS, CHANS)), shape(DENSE)], own_half, other_half, medium_filter,
+        residue,
     )
     return (grad_query, grad_stream, grad_filter, grad_residue.reshape(CHANS))
 

time: 124 us -> 113 us (0.911)
  blocking collectives: 15 us -> 28.5 us
  starting transfers between devices: 55.1 us -> 45.3 us
  local copies, waits for them, and re-layouts: 13.2 us -> 7.41 us
  Pallas kernels: 20.6 us -> 15.2 us
  waiting for transfers between devices: 17.7 us -> 15.2 us
    all_to_all x0 -> x1, blocking collectives: none -> 13.3 us  [body(): sums = lax.all_to_all(sums, ('y', 'core'), 0, 0, tiled=True)]
    all_to_all x1 -> x0, waiting for transfers between devices: 6.52 us -> none  [body(): sums = lax.all_to_all(sums, ('y', 'core'), 0, 0, tiled=True)]
    unnamed x60 -> x42, local copies, waits for them, and re-layouts: 13.2 us -> 7.41 us
    all_to_all x1 -> x0, starting transfers between devices: 4.71 us -> none  [body(): sums = lax.all_to_all(sums, ('y', 'core'), 0, 0, tiled=True)]
    pallas_call x7, Pallas kernels: 15.4 us -> 11.8 us  [large(): pl.pallas_call(stepped, out_shape=tuple(outs), in_specs=specs[:len(args)]...]
    all_to_all x1, starting transfers between devices: 8.27 us -> 6.01 us  [body(): parts = lax.all_to_all(spread, 'zh', 0, 0, tiled=True)]
    pallas_call x7, Pallas kernels: 5.27 us -> 3.37 us  [small(): pl.pallas_call(kernel, out_shape=tuple(outs), in_specs=[VMEM] * len(args)...]
    all_to_all x1, waiting for transfers between devices: 1.52 us -> 3.04 us  [body(): lax.all_to_all(chip_sum.reshape(PLANE, 8, LANES), ('y', 'zl'), 0, 0, tile...]
  transfers between devices with their start and end apart: 9 -> 8, of which waited for: 6 -> 6; matrix products, arithmetic and copies ran while one was open for 0% -> 0% of each run, Pallas kernels for 11% -> 8%
where the time goes in v4:
time: 113 us
  starting transfers between devices  45.3 us (40%)
  blocking collectives  28.5 us (25%)
  Pallas kernels  15.2 us (13%)
  waiting for transfers between devices  15.2 us (13%)
  local copies, waits for them, and re-layouts  7.41 us (7%)
    all_to_all x1, starting transfers between devices, body(): column = lax.all_to_all(spread, ('zh', 'zl'), 0, 0, tiled=True)  15.9 us
    all_to_all x1, blocking collectives, body(): sums = lax.all_to_all(sums, ('y', 'core'), 0, 0, tiled=True)  13.3 us
    pallas_call x7, Pallas kernels, large(): pl.pallas_call(stepped, out_shape=tuple(outs), in_specs=specs[:len(args)]...  11.8 us
    psum x1, blocking collectives, body(): squares = lax.psum(squares, 'chan')  9.17 us
    unnamed x42, local copies, waits for them, and re-layouts  7.41 us
    all_to_all x1, waiting for transfers between devices, body(): parts = lax.all_to_all(spread, 'zh', 0, 0, tiled=True)  6.69 us
    all_to_all x1, starting transfers between devices, body(): parts = lax.all_to_all(spread, 'zh', 0, 0, tiled=True)  6.01 us
    psum x1, blocking collectives, body(): dots = lax.psum(dots, 'chan')  6.01 us
  transfers between devices with their start and end apart: 8, of which 6 were waited for; matrix products, arithmetic and copies ran while one was open for 0% of the time, Pallas kernels for 8%

profile of v4, /device:TPU:1, one launch (start us, length us, event | category | flops | bytes accessed | tf_op | source)
XLA Modules:
  0.0 112.5 jit_solution(16664266975771117937)
XLA Ops:
  0.6 2.9 %shard_map.147 = (f32[16,8,128]{2,1,0:T(8,128)}, f32[256,1024]{1,0:T(8,128)}) custom-call(bf16[256,1024]{1,0:T(8,128)(2,1)} %refs_0_.4, bf16[256,1024]{1,0:T(8,128)(2,1)} %refs_1_.4, f32[8,128]{1,0:T(8,128)} %bitcast.11), custom_call_target="tpu_custom_call" | custom-call | bytes 1024 | tf_op jit(solution)/shard_map/pallas_call | solution.py:88
  3.5 15.9 %all-to-all-start = ((f32[16,8,128]{2,1,0:T(8,128)}), f32[16,8,128]{2,1,0:T(8,128)S(1)}, u32[]{:S(2)}, u32[]{:S(2)}) async-start(f32[16,8,128]{2,1,0:T(8,128)} %get-tuple-element.18.first_ref), calls=%async_computation | async-start | bytes 131072 | tf_op jit(solution)/shard_map/all_to_all | solution.py:343
  19.6 9.2 %psum.14.refs_1_.refs_0_ = f32[2,128]{1,0:T(2,128)S(1)} all-reduce(f32[2,128]{1,0:T(2,128)S(1)} %shard_map.148), channel_id=1, replica_groups=mesh['y'=4,'zh'=4,'zl'=4,'core'=2,'chan'=4] {'chan'}, use_global_device_ids=true, to_apply=%region_0.0 | all-reduce | flops 256 | bytes 2048 | tf_op jit(solution)/shard_map/psum | solution.py:347
  28.7 2.2 %all-to-all-done.refs_0_.parts_ref = f32[16,8,128]{2,1,0:T(8,128)S(1)} async-done(((f32[16,8,128]{2,1,0:T(8,128)}), f32[16,8,128]{2,1,0:T(8,128)S(1)}, u32[]{:S(2)}, u32[]{:S(2)}) %all-to-all-start) | async-done | bytes 65568 | tf_op jit(solution)/shard_map/all_to_all | solution.py:343
  31.3 4.5 %collective-permute-start = (f32[128,1024]{1,0:T(8,128)S(1)}, f32[128,1024]{1,0:T(8,128)S(1)}, u32[]{:S(2)}, u32[]{:S(2)}) collective-permute-start(f32[128,1024]{1,0:T(8,128)S(1)} %get-tuple-element.20), channel_id=1, source_target_pairs={{0,4},{4,8},{8,12},{12,16},{16,20},{20,24},{24,28},{28,32},{32,36}... | collective-permute-start | bytes 1572872 | tf_op jit(solution)/shard_map/ppermute | solution.py:353
  35.9 13.3 %all_to_all.25.parts_ref = f32[8,3,8,128]{3,2,1,0:T(8,128)S(1)} all-to-all(f32[8,3,8,128]{3,2,1,0:T(8,128)S(1)} %shard_map.150), channel_id=1, replica_groups=mesh['y'=4,'zh'=4,'zl'=4,'core'=2,'chan'=4] {'y','core'}, dimensions={0} | all-to-all | bytes 196608 | tf_op jit(solution)/shard_map/all_to_all | solution.py:357
  50.1 1.0 copy-done.14
  51.1 1.8 %shard_map.153 = (f32[8,8,8,128]{3,2,1,0:T(8,128)S(1)}, f32[8,8,8,128]{3,2,1,0:T(8,128)S(1)}, bf16[256,1024]{1,0:T(8,128)(2,1)S(1)}, f32[128,1024]{1,0:T(8,128)S(1)}) custom-call(bf16[384,384]{1,0:T(8,128)(2,1)S(1)} %copy-done.3, bf16[128,384]{1,0:T(8,128)(2,1)S(1)} %copy-done.17, bf16[256,1024]{1,0:T(8,128)(2,1)S(1)} %get-tuple-element.19.refs_2_, ...), custom_call_target="tpu_custom_call" | custom-call | flops 603979776 | bytes 1024 | tf_op jit(solution)/shard_map/pallas_call | solution.py:88
  53.7 2.3 %collective-permute-start.1 = (f32[8,8,8,128]{3,2,1,0:T(8,128)S(1)}, f32[8,8,8,128]{3,2,1,0:T(8,128)S(1)}, u32[]{:S(2)}, u32[]{:S(2)}) collective-permute-start(f32[8,8,8,128]{3,2,1,0:T(8,128)S(1)} %get-tuple-element.24), channel_id=1, source_target_pairs={{0,4},{4,0},{1,5},{5,1},{2,6},{6,2},{3,7},{7,3},{8,12},{12,8},{9,1... | collective-permute-start | bytes 786440 | tf_op jit(solution)/shard_map/ppermute | solution.py:369
  56.1 1.1 %collective-permute-done.1.b_ref = f32[8,8,8,128]{3,2,1,0:T(8,128)S(1)} collective-permute-done((f32[8,8,8,128]{3,2,1,0:T(8,128)S(1)}, f32[8,8,8,128]{3,2,1,0:T(8,128)S(1)}, u32[]{:S(2)}, u32[]{:S(2)}) %collective-permute-start.1) | collective-permute-done | bytes 262176 | tf_op jit(solution)/shard_map/ppermute | solution.py:369
  58.0 4.2 %all-to-all-start.2 = ((f32[64,8,128]{2,1,0:T(8,128)}), f32[64,8,128]{2,1,0:T(8,128)}, u32[]{:S(2)}, u32[]{:S(2)}) async-start(f32[64,8,128]{2,1,0:T(8,128)} %bitcast.9), calls=%async_computation.2 | async-start | bytes 524288 | tf_op jit(solution)/shard_map/all_to_all | solution.py:372
  62.2 2.3 %collective-permute-start.2 = (f32[128,1024]{1,0:T(8,128)}, f32[128,1024]{1,0:T(8,128)}, u32[]{:S(2)}, u32[]{:S(2)}) collective-permute-start(f32[128,1024]{1,0:T(8,128)} %copy-done.20), channel_id=1, source_target_pairs={{4,0},{8,4},{12,8},{16,12},{20,16},{24,20},{28,24},{32,28},{36,32}... | collective-permute-start | bytes 1572872 | tf_op jit(solution)/shard_map/ppermute | solution.py:371
  66.5 2.6 %shard_map.152 = (bf16[256,1024]{1,0:T(8,128)(2,1)}, f32[8,128]{1,0:T(8,128)S(1)}) custom-call(bf16[384,384]{1,0:T(8,128)(2,1)S(1)} %copy-done.3, bf16[384,384]{1,0:T(8,128)(2,1)S(1)} %copy-done.7, bf16[256,1024]{1,0:T(8,128)(2,1)S(1)} %get-tuple-element.19.refs_2_, f32[128,1024]{1,0:T(8,128)S(1)} %copy-done.6, f32[256,1024]{1,0:T(8,128)S(1)} %copy-done.2, ...), custom_call_target="tpu_custom_call" | custom-call | flops 603979776 | bytes 1024 | tf_op jit(solution)/shard_map/pallas_call | solution.py:88
  69.1 3.0 %all-to-all-done.2 = f32[64,8,128]{2,1,0:T(8,128)} async-done(((f32[64,8,128]{2,1,0:T(8,128)}), f32[64,8,128]{2,1,0:T(8,128)}, u32[]{:S(2)}, u32[]{:S(2)}) %all-to-all-start.2) | async-done | bytes 262176 | tf_op jit(solution)/shard_map/all_to_all | solution.py:372
  72.2 1.6 %shard_map.155.refs_0_ = f32[4,4,8,128]{3,2,1,0:T(8,128)} custom-call(f32[16,4,8,128]{3,2,1,0:T(8,128)} %bitcast.4.parts_ref, f32[8,128]{1,0:T(8,128)S(1)} %get-tuple-element.25.refs_0_), custom_call_target="tpu_custom_call" | custom-call | bytes 331776 | tf_op jit(solution)/shard_map/pallas_call | solution.py:68
  73.8 6.0 %all-to-all-start.3 = ((f32[4,4,8,128]{3,2,1,0:T(8,128)}), f32[4,4,8,128]{3,2,1,0:T(8,128)S(1)}, u32[]{:S(2)}, u32[]{:S(2)}) async-start(f32[4,4,8,128]{3,2,1,0:T(8,128)} %shard_map.155.refs_0_), calls=%async_computation.3 | async-start | bytes 131072 | tf_op jit(solution)/shard_map/all_to_all | solution.py:383
  79.8 1.0 copy-done.13
  80.8 3.0 %shard_map.156 = (f32[256,1024]{1,0:T(8,128)S(1)}, f32[2,128]{1,0:T(2,128)S(1)}) custom-call(f32[4,4,8,128]{3,2,1,0:T(8,128)} %shard_map.155.refs_0_, bf16[384,384]{1,0:T(8,128)(2,1)S(1)} %copy-done.3, bf16[384,384]{1,0:T(8,128)(2,1)S(1)} %copy-done.8, bf16[256,1024]{1,0:T(8,128)(2,1)S(1)} %copy-done.13, f32[128,1024]{1,0:T(8,128)} %collective-permute-done.2.refs_4_, ...), custom_call_target="tpu_custom_call" | custom-call | flops 603979776 | bytes 1024 | tf_op jit(solution)/shard_map/pallas_call | solution.py:88
  84.8 6.7 %all-to-all-done.3.parts_ref = f32[4,4,8,128]{3,2,1,0:T(8,128)S(1)} async-done(((f32[4,4,8,128]{3,2,1,0:T(8,128)}), f32[4,4,8,128]{3,2,1,0:T(8,128)S(1)}, u32[]{:S(2)}, u32[]{:S(2)}) %all-to-all-start.3) | async-done | bytes 65568 | tf_op jit(solution)/shard_map/all_to_all | solution.py:383
  92.2 4.1 %all-to-all-start.4 = ((f32[16,4,8,128]{3,2,1,0:T(8,128)}), f32[16,4,8,128]{3,2,1,0:T(8,128)S(1)}, u32[]{:S(2)}, u32[]{:S(2)}) async-start(f32[16,4,8,128]{3,2,1,0:T(8,128)} %shard_map.158), calls=%async_computation.4 | async-start | bytes 524288 | tf_op jit(solution)/shard_map/all_to_all | solution.py:395
  96.3 6.0 %psum.15.refs_1_.after_ref = f32[2,128]{1,0:T(2,128)S(1)} all-reduce(f32[2,128]{1,0:T(2,128)S(1)} %get-tuple-element.28.refs_0_), channel_id=1, replica_groups=mesh['y'=4,'zh'=4,'zl'=4,'core'=2,'chan'=4] {'chan'}, use_global_device_ids=true, to_apply=%region_1.0 | all-reduce | flops 256 | bytes 2048 | tf_op jit(solution)/shard_map/psum | solution.py:394
  102.3 2.1 %all-to-all-done.4 = f32[16,4,8,128]{3,2,1,0:T(8,128)S(1)} async-done(((f32[16,4,8,128]{3,2,1,0:T(8,128)}), f32[16,4,8,128]{3,2,1,0:T(8,128)S(1)}, u32[]{:S(2)}, u32[]{:S(2)}) %all-to-all-start.4) | async-done | bytes 262176 | tf_op jit(solution)/shard_map/all_to_all | solution.py:395
  104.5 6.0 %collective-permute-start.3 = (f32[64,8,128]{2,1,0:T(8,128)S(1)}, f32[64,8,128]{2,1,0:T(8,128)S(1)}, u32[]{:S(2)}, u32[]{:S(2)}) collective-permute-start(f32[64,8,128]{2,1,0:T(8,128)S(1)} %shard_map.159.own_ref), channel_id=1, source_target_pairs={{0,4},{4,0},{1,5},{5,1},{2,6},{6,2},{3,7},{7,3},{8,12},{12,8},{9,1... | collective-permute-start | bytes 786440 | tf_op jit(solution)/shard_map/ppermute | solution.py:402
  110.5 1.1 shard_map.157
  (52 shorter events, 7.6 us)
Async XLA Ops:
  0.6 18.8 %copy-start = (bf16[256,1024]{1,0:T(8,128)(2,1)S(1)}, bf16[256,1024]{1,0:T(8,128)(2,1)}, u32[]{:S(2)}) copy-start(bf16[256,1024]{1,0:T(8,128)(2,1)} %refs_3_.3) | copy-start | bytes 1572868
  3.5 27.5 %copy-start.4 = (bf16[256,1024]{1,0:T(8,128)(2,1)S(1)}, bf16[256,1024]{1,0:T(8,128)(2,1)}, u32[]{:S(2)}) copy-start(bf16[256,1024]{1,0:T(8,128)(2,1)} %refs_6_.1) | copy-start | bytes 1572868
  3.5 27.5 %copy-start.18 = (f32[1024]{0:T(1024)S(1)}, f32[1024]{0:T(1024)}, u32[]{:S(2)}) copy-start(f32[1024]{0:T(1024)} %param.13) | copy-start | bytes 12292
  3.5 27.5 %all-to-all-start = ((f32[16,8,128]{2,1,0:T(8,128)}), f32[16,8,128]{2,1,0:T(8,128)S(1)}, u32[]{:S(2)}, u32[]{:S(2)}) async-start(f32[16,8,128]{2,1,0:T(8,128)} %get-tuple-element.18.first_ref), calls=%async_computation | async-start | bytes 131072 | tf_op jit(solution)/shard_map/all_to_all | solution.py:343
  19.4 29.9 %copy-start.2 = (f32[256,1024]{1,0:T(8,128)S(1)}, f32[256,1024]{1,0:T(8,128)}, u32[]{:S(2)}) copy-start(f32[256,1024]{1,0:T(8,128)} %get-tuple-element.21.refs_4_) | copy-start | bytes 3145732
  31.0 4.8 %copy-start.16 = (f32[1024]{0:T(1024)S(1)}, f32[1024]{0:T(1024)}, u32[]{:S(2)}) copy-start(f32[1024]{0:T(1024)} %param.20) | copy-start | bytes 12292
  31.0 4.8 %copy-start.19 = (f32[1024]{0:T(1024)S(1)}, f32[1024]{0:T(1024)}, u32[]{:S(2)}) copy-start(f32[1024]{0:T(1024)} %param.19) | copy-start | bytes 12292
  31.0 4.9 %copy-start.15 = (f32[16,8,128]{2,1,0:T(8,128)S(1)}, f32[16,8,128]{2,1,0:T(8,128)}, u32[]{:S(2)}) copy-start(f32[16,8,128]{2,1,0:T(8,128)} %get-tuple-element.18.first_ref) | copy-start | bytes 196612
  31.3 18.0 %copy-start.3 = (bf16[384,384]{1,0:T(8,128)(2,1)S(1)}, bf16[384,384]{1,0:T(8,128)(2,1)}, u32[]{:S(2)}) copy-start(bf16[384,384]{1,0:T(8,128)(2,1)} %constant.8.clone.refs_0_.refs_1_) | copy-start | bytes 884740
  31.3 17.9 %collective-permute-start = (f32[128,1024]{1,0:T(8,128)S(1)}, f32[128,1024]{1,0:T(8,128)S(1)}, u32[]{:S(2)}, u32[]{:S(2)}) collective-permute-start(f32[128,1024]{1,0:T(8,128)S(1)} %get-tuple-element.20), channel_id=1, source_target_pairs={{0,4},{4,8},{8,12},{12,16},{16,20},{20,24},{24,28},{28,32},{32,36}... | collective-permute-start | bytes 1572872 | tf_op jit(solution)/shard_map/ppermute | solution.py:353
  49.2 3.7 %copy-start.5 = (f32[128,1024]{1,0:T(8,128)}, f32[128,1024]{1,0:T(8,128)S(1)}, u32[]{:S(2)}) copy-start(f32[128,1024]{1,0:T(8,128)S(1)} %collective-permute-done.refs_3_) | copy-start | bytes 1572868
  50.1 1.0 copy-start.14
  53.7 3.5 %copy-start.12 = (bf16[256,1024]{1,0:T(8,128)(2,1)}, bf16[256,1024]{1,0:T(8,128)(2,1)S(1)}, u32[]{:S(2)}) copy-start(bf16[256,1024]{1,0:T(8,128)(2,1)S(1)} %get-tuple-element.26.refs_3_) | copy-start | bytes 1572868
  53.7 3.5 %collective-permute-start.1 = (f32[8,8,8,128]{3,2,1,0:T(8,128)S(1)}, f32[8,8,8,128]{3,2,1,0:T(8,128)S(1)}, u32[]{:S(2)}, u32[]{:S(2)}) collective-permute-start(f32[8,8,8,128]{3,2,1,0:T(8,128)S(1)} %get-tuple-element.24), channel_id=1, source_target_pairs={{0,4},{4,0},{1,5},{5,1},{2,6},{6,2},{3,7},{7,3},{8,12},{12,8},{9,1... | collective-permute-start | bytes 786440 | tf_op jit(solution)/shard_map/ppermute | solution.py:369
  57.2 7.2 %copy-start.1 = (f32[128,1024]{1,0:T(8,128)S(1)}, f32[128,1024]{1,0:T(8,128)}, u32[]{:S(2)}) copy-start(f32[128,1024]{1,0:T(8,128)} %filter_ref.1) | copy-start | bytes 1572868
  58.0 14.2 %all-to-all-start.2 = ((f32[64,8,128]{2,1,0:T(8,128)}), f32[64,8,128]{2,1,0:T(8,128)}, u32[]{:S(2)}, u32[]{:S(2)}) async-start(f32[64,8,128]{2,1,0:T(8,128)} %bitcast.9), calls=%async_computation.2 | async-start | bytes 524288 | tf_op jit(solution)/shard_map/all_to_all | solution.py:372
  62.2 17.6 %collective-permute-start.2 = (f32[128,1024]{1,0:T(8,128)}, f32[128,1024]{1,0:T(8,128)}, u32[]{:S(2)}, u32[]{:S(2)}) collective-permute-start(f32[128,1024]{1,0:T(8,128)} %copy-done.20), channel_id=1, source_target_pairs={{4,0},{8,4},{12,8},{16,12},{20,16},{24,20},{28,24},{32,28},{36,32}... | collective-permute-start | bytes 1572872 | tf_op jit(solution)/shard_map/ppermute | solution.py:371
  64.5 1.0 copy-start.6
  69.1 10.7 %copy-start.8 = (bf16[384,384]{1,0:T(8,128)(2,1)S(1)}, bf16[384,384]{1,0:T(8,128)(2,1)}, u32[]{:S(2)}) copy-start(bf16[384,384]{1,0:T(8,128)(2,1)} %constant.9.clone.refs_1_.refs_2_) | copy-start | bytes 884740
  73.8 17.7 %all-to-all-start.3 = ((f32[4,4,8,128]{3,2,1,0:T(8,128)}), f32[4,4,8,128]{3,2,1,0:T(8,128)S(1)}, u32[]{:S(2)}, u32[]{:S(2)}) async-start(f32[4,4,8,128]{3,2,1,0:T(8,128)} %shard_map.155.refs_0_), calls=%async_computation.3 | async-start | bytes 131072 | tf_op jit(solution)/shard_map/all_to_all | solution.py:383
  79.8 1.0 copy-start.13
  91.5 19.0 %copy-start.10 = (f32[256,1024]{1,0:T(8,128)S(1)}, f32[256,1024]{1,0:T(8,128)}, u32[]{:S(2)}) copy-start(f32[256,1024]{1,0:T(8,128)} %copy-done.9) | copy-start | bytes 3145732
  92.2 12.2 %all-to-all-start.4 = ((f32[16,4,8,128]{3,2,1,0:T(8,128)}), f32[16,4,8,128]{3,2,1,0:T(8,128)S(1)}, u32[]{:S(2)}, u32[]{:S(2)}) async-start(f32[16,4,8,128]{3,2,1,0:T(8,128)} %shard_map.158), calls=%async_computation.4 | async-start | bytes 524288 | tf_op jit(solution)/shard_map/all_to_all | solution.py:395
  104.5 7.2 %collective-permute-start.3 = (f32[64,8,128]{2,1,0:T(8,128)S(1)}, f32[64,8,128]{2,1,0:T(8,128)S(1)}, u32[]{:S(2)}, u32[]{:S(2)}) collective-permute-start(f32[64,8,128]{2,1,0:T(8,128)S(1)} %shard_map.159.own_ref), channel_id=1, source_target_pairs={{0,4},{4,0},{1,5},{5,1},{2,6},{6,2},{3,7},{7,3},{8,12},{12,8},{9,1... | collective-permute-start | bytes 786440 | tf_op jit(solution)/shard_map/ppermute | solution.py:402
  (5 other events, 4.3 us)

commit v5 on v4

--- a/solution.py
+++ b/solution.py
@@ -31,15 +31,12 @@
 FULL = (ROWS, CHANS)
 
 
-def transform_tables():
+def transform_table():
     k = np.arange(HALF, dtype=np.int64)[:, None]
     n = np.arange(POINTS, dtype=np.int64)[None, :]
     angle = np.pi * (((2 * k + 1) * n) % (2 * POINTS)).astype(np.float64) / POINTS
     table = np.concatenate([np.cos(angle), -np.sin(angle)], axis=0)
-    forward = table.astype(BF16)
-    inverse = np.ascontiguousarray(table.T).astype(BF16)
-    lags = np.ascontiguousarray(table.T[TAPS:0:-1]).astype(BF16)
-    return forward, inverse, lags
+    return table.astype(BF16)
 
 
 ANY = pl.BlockSpec(memory_space=pl.ANY)
@@ -99,6 +96,12 @@
 def dot(a, b):
     return lax.dot_general(
         a, b, (((1,), (0,)), ((), ())), preferred_element_type=F32
+    )
+
+
+def dot_back(table, b):
+    return lax.dot_general(
+        table, b, (((0,), (0,)), ((), ())), preferred_element_type=F32
     )
 
 
@@ -160,7 +163,7 @@
         spread_ref[...] = jnp.broadcast_to(first_ref[...], spread_ref.shape)
 
 
-def column_kernel(parts_ref, first_ref, rate_ref, after_ref, out_ref):
+def column_kernel(parts_ref, rate_ref, after_ref, out_ref):
     z = lax.axis_index(("zh", "zl"))
     pace = rate_ref[...] * (-2.0 * ROWS)
     ahead = jnp.zeros(DENSE, F32)
@@ -174,7 +177,7 @@
     count = out_ref.shape[0]
     out_ref[:, 0] = jnp.broadcast_to(total, (count,) + DENSE)
     out_ref[:, 1] = jnp.broadcast_to(ahead, (count,) + DENSE)
-    out_ref[:, 2] = jnp.broadcast_to(first_ref[0], (count,) + DENSE)
+    out_ref[:, 2] = jnp.broadcast_to(parts_ref[z], (count,) + DENSE)
 
 
 def carry_kernel(parts_ref, rate_ref, carry_ref):
@@ -228,7 +231,7 @@
 
 
 def filter_kernel(
-    step, fwd_ref, lag_ref, product_ref, rim_ref, local_ref, query_ref, rate_ref, scale_ref, carry_ref,
+    step, fwd_ref, product_ref, rim_ref, local_ref, query_ref, rate_ref, scale_ref, carry_ref,
     keep_ref, send_ref, mixed_grad_ref, head_ref,
 ):
     ext = jnp.concatenate([rim_ref[...].astype(BF16), product_ref[...]], axis=0)
@@ -238,7 +241,7 @@
     grad_mixed = grad_mixed.astype(BF16)
     mixed_grad_ref[...] = grad_mixed
     spectrum = dot(fwd_ref[:, :ROWS], grad_mixed)
-    taps = dot(lag_ref[...], mul_conj(spectrum, product))
+    taps = -dot_back(fwd_ref[:, ROWS:], mul_conj(product, spectrum))
     is_first = lax.axis_index("core") == 0
     for group in range(GROUPS // 2):
         low = taps[group * 8 : group * 8 + 8, :]
@@ -251,24 +254,24 @@
 
 
 def query_kernel(
-    step, fwd_ref, inv_ref, product_ref, rim_ref, local_ref, filter_ref, rate_ref, scale_ref, carry_ref, grad_ref, token_ref
+    step, fwd_ref, product_ref, rim_ref, local_ref, filter_ref, rate_ref, scale_ref, carry_ref, grad_ref, token_ref
 ):
     ext = jnp.concatenate([rim_ref[...].astype(BF16), product_ref[...]], axis=0)
     product = dot(fwd_ref[...], ext)
     taps = dot(fwd_ref[:, :TAPS], filter_ref[...].astype(BF16))
-    mixed = dot(inv_ref[TAPS:, :], mul(product, taps)) * (2.0 / POINTS)
+    mixed = dot_back(fwd_ref[:, TAPS:], mul(product, taps)) * (2.0 / POINTS)
     grad_ref[...] = (mixed * grad_stored(step, local_ref, rate_ref, scale_ref, carry_ref)).astype(BF16)
     if step == STEPS - 1:
         token_ref[...] = carry_ref[...]
 
 
 def weighted_kernel(
-    step, later_ref, fwd_ref, inv_ref, grad_ref, after_ref, filter_ref, key_ref, stream_ref, gain_ref, weighted_ref, dots_ref, acc_ref
+    step, later_ref, fwd_ref, grad_ref, after_ref, filter_ref, key_ref, stream_ref, gain_ref, weighted_ref, dots_ref, acc_ref
 ):
     ext = jnp.concatenate([grad_ref[...], after_ref[...].astype(BF16)], axis=0)
     grad = dot(fwd_ref[...], ext)
     taps = dot(fwd_ref[:, :TAPS], filter_ref[...].astype(BF16))
-    back = dot(inv_ref[:ROWS, :], mul_conj(taps, grad)) * (2.0 / POINTS)
+    back = dot_back(fwd_ref[:, :ROWS], mul_conj(taps, grad)) * (2.0 / POINTS)
     weighted = row(gain_ref, step) * key_ref[...].astype(F32) * back
     weighted_ref[...] = weighted
     dots = fold(weighted * stream_ref[...].astype(F32))
@@ -328,7 +331,7 @@
 def body(
     stream, norm_gain, gate_query, gate_key, gate_out, cotangent, medium_filter, long_residue, long_rate
 ):
-    forward, inverse, lags = (jnp.asarray(t) for t in transform_tables())
+    forward = jnp.asarray(transform_table())
     gain, rate, residue = (v.reshape(DENSE) for v in (norm_gain, long_rate, long_residue))
     scale = residue * jnp.sqrt(-jnp.expm1(-2.0 * rate))
     swap = [(0, 1), (1, 0)]
@@ -347,12 +350,12 @@
     squares = lax.psum(squares, "chan")
     product, rim = large(
         product_kernel, [shape(FULL, BF16), shape((TAPS, CHANS))], [cols, cols],
-        (column, squares, stream, gate_key, gain), [ANY, None, cols, cols, None],
+        (column, squares, stream, gate_key, gain), [None, None, cols, cols, None],
         scratch=[pltpu.VMEM((ROWS, LANES), F32)],
     )
     before = lax.ppermute(rim, seq, [(i, i + 1) for i in range(count - 1)])
     (sums,) = small(
-        column_kernel, [shape((2 * Y, 3) + DENSE)], column, spread, rate, scale
+        column_kernel, [shape((2 * Y, 3) + DENSE)], column, rate, scale
     )
     sums = lax.all_to_all(sums, ("y", "core"), 0, 0, tiled=True)
     (carry,) = small(carry_kernel, [shape(DENSE)], sums, rate)
@@ -361,8 +364,8 @@
     keep, send, grad_mixed, head = large(
         filter_kernel, [shape(half), shape(half), shape(FULL, BF16), shape((TAPS, CHANS))],
         [blocks, blocks, cols, cols],
-        (forward, lags, product, before, local, gate_query, rate, scale, carry),
-        [None, None, cols, cols, cols, cols, None, None, None],
+        (forward, product, before, local, gate_query, rate, scale, carry),
+        [None, cols, cols, cols, cols, None, None, None],
         flops=2 * CHANS * POINTS * (POINTS + ROWS + TAPS),
     )
 
@@ -372,8 +375,8 @@
     parts = lax.all_to_all(chip_sum.reshape(PLANE, 8, LANES), ("y", "zl"), 0, 0, tiled=True)
     grad_query, token = large(
         query_kernel, [shape(FULL, BF16), shape(DENSE)], [cols, None],
-        (forward, inverse, product, before, local, medium_filter, rate, scale, carry),
-        [None, None, cols, cols, cols, cols, None, None, None],
+        (forward, product, before, local, medium_filter, rate, scale, carry),
+        [None, cols, cols, cols, cols, None, None, None],
         flops=2 * CHANS * POINTS * (POINTS + ROWS + TAPS),
     )
     mine = (ZH, 8, LANES)
@@ -383,8 +386,8 @@
     parts = lax.all_to_all(spread, "zh", 0, 0, tiled=True)
     weighted, dots = large(
         weighted_kernel, [shape(FULL), shape(packed)], [cols, None],
-        (spread, forward, inverse, grad_mixed, after, medium_filter, gate_key, stream, gain),
-        [ANY, None, None, cols, cols, cols, cols, cols, None],
+        (spread, forward, grad_mixed, after, medium_filter, gate_key, stream, gain),
+        [ANY, None, cols, cols, cols, cols, cols, None],
         scratch=[pltpu.VMEM((ROWS, LANES), F32)],
         flops=2 * CHANS * POINTS * (POINTS + ROWS + TAPS),
     )

time: 113 us -> 113 us (level)
  local copies, waits for them, and re-layouts: 7.41 us -> 4.84 us
  waiting for transfers between devices: 15.2 us -> 17.1 us
    unnamed x42 -> x30, local copies, waits for them, and re-layouts: 7.41 us -> 4.84 us
where the time goes in v5:
time: 113 us; the launch traced here: 112 us
  starting transfers between devices  45.2 us (40%)
  blocking collectives  28.5 us (25%)
  waiting for transfers between devices  17.1 us (15%)
  Pallas kernels  15.2 us (13%)
  local copies, waits for them, and re-layouts  4.84 us (4%)
    all_to_all x1, starting transfers between devices, body(): column = lax.all_to_all(spread, ('zh', 'zl'), 0, 0, tiled=True)  15.9 us
    all_to_all x1, blocking collectives, body(): sums = lax.all_to_all(sums, ('y', 'core'), 0, 0, tiled=True)  13.3 us
    pallas_call x7, Pallas kernels, large(): pl.pallas_call(stepped, out_shape=tuple(outs), in_specs=specs[:len(args)]...  11.8 us
    psum x1, blocking collectives, body(): squares = lax.psum(squares, 'chan')  9.17 us
    all_to_all x1, waiting for transfers between devices, body(): parts = lax.all_to_all(spread, 'zh', 0, 0, tiled=True)  7.68 us
    ppermute x1, starting transfers between devices, body(): other_half = lax.ppermute(own_half, 'core', swap)  6.26 us
    psum x1, blocking collectives, body(): dots = lax.psum(dots, 'chan')  6.01 us
    all_to_all x1, starting transfers between devices, body(): parts = lax.all_to_all(spread, 'zh', 0, 0, tiled=True)  6 us
  transfers between devices with their start and end apart: 8, of which 6 were waited for; matrix products, arithmetic and copies ran while one was open for 0% of the time, Pallas kernels for 8%

profile of v5, /device:TPU:1, one launch (start us, length us, event | category | flops | bytes accessed | tf_op | source)
XLA Modules:
  0.0 111.8 jit_solution(742827623440796167)
XLA Ops:
  0.6 2.9 %shard_map.129 = (f32[16,8,128]{2,1,0:T(8,128)}, f32[256,1024]{1,0:T(8,128)}) custom-call(bf16[256,1024]{1,0:T(8,128)(2,1)} %refs_0_.4, bf16[256,1024]{1,0:T(8,128)(2,1)} %refs_1_.2, f32[8,128]{1,0:T(8,128)} %bitcast.11), custom_call_target="tpu_custom_call" | custom-call | bytes 1024 | tf_op jit(solution)/shard_map/pallas_call | solution.py:85
  3.5 15.9 %all-to-all-start = ((f32[16,8,128]{2,1,0:T(8,128)}), f32[16,8,128]{2,1,0:T(8,128)S(1)}, u32[]{:S(2)}, u32[]{:S(2)}) async-start(f32[16,8,128]{2,1,0:T(8,128)} %get-tuple-element.18), calls=%async_computation | async-start | bytes 131072 | tf_op jit(solution)/shard_map/all_to_all | solution.py:346
  19.6 9.2 %psum.14.refs_1_.refs_0_ = f32[2,128]{1,0:T(2,128)S(1)} all-reduce(f32[2,128]{1,0:T(2,128)S(1)} %shard_map.130), channel_id=1, replica_groups=mesh['y'=4,'zh'=4,'zl'=4,'core'=2,'chan'=4] {'chan'}, use_global_device_ids=true, to_apply=%region_0.0 | all-reduce | flops 256 | bytes 2048 | tf_op jit(solution)/shard_map/psum | solution.py:350
  28.8 2.2 %all-to-all-done.refs_0_.parts_ref = f32[16,8,128]{2,1,0:T(8,128)S(1)} async-done(((f32[16,8,128]{2,1,0:T(8,128)}), f32[16,8,128]{2,1,0:T(8,128)S(1)}, u32[]{:S(2)}, u32[]{:S(2)}) %all-to-all-start) | async-done | bytes 65568 | tf_op jit(solution)/shard_map/all_to_all | solution.py:346
  31.3 4.5 %collective-permute-start = (f32[128,1024]{1,0:T(8,128)S(1)}, f32[128,1024]{1,0:T(8,128)S(1)}, u32[]{:S(2)}, u32[]{:S(2)}) collective-permute-start(f32[128,1024]{1,0:T(8,128)S(1)} %get-tuple-element.20), channel_id=1, source_target_pairs={{0,4},{4,8},{8,12},{12,16},{16,20},{20,24},{24,28},{28,32},{32,36}... | collective-permute-start | bytes 1572872 | tf_op jit(solution)/shard_map/ppermute | solution.py:356
  35.9 13.3 %all_to_all.25.parts_ref = f32[8,3,8,128]{3,2,1,0:T(8,128)S(1)} all-to-all(f32[8,3,8,128]{3,2,1,0:T(8,128)S(1)} %shard_map.132), channel_id=1, replica_groups=mesh['y'=4,'zh'=4,'zl'=4,'core'=2,'chan'=4] {'y','core'}, dimensions={0} | all-to-all | bytes 196608 | tf_op jit(solution)/shard_map/all_to_all | solution.py:360
  49.3 1.2 %copy-done.8 = bf16[256,1024]{1,0:T(8,128)(2,1)S(1)} copy-done((bf16[256,1024]{1,0:T(8,128)(2,1)S(1)}, bf16[256,1024]{1,0:T(8,128)(2,1)}, u32[]{:S(2)}) %copy-start.8) | copy-done | bytes 524312
  50.5 1.8 %shard_map.135 = (f32[8,8,8,128]{3,2,1,0:T(8,128)S(1)}, f32[8,8,8,128]{3,2,1,0:T(8,128)S(1)}, bf16[256,1024]{1,0:T(8,128)(2,1)S(1)}, f32[128,1024]{1,0:T(8,128)S(1)}) custom-call(bf16[384,384]{1,0:T(8,128)(2,1)S(1)} %copy-done.3, bf16[256,1024]{1,0:T(8,128)(2,1)S(1)} %get-tuple-element.19.refs_1_, f32[128,1024]{1,0:T(8,128)S(1)} %collective-permute-done.refs_2_, ...), custom_call_target="tpu_custom_call" | custom-call | flops 603979776 | bytes 1024 | tf_op jit(solution)/shard_map/pallas_call | solution.py:85
  53.1 2.3 %collective-permute-start.1 = (f32[8,8,8,128]{3,2,1,0:T(8,128)S(1)}, f32[8,8,8,128]{3,2,1,0:T(8,128)S(1)}, u32[]{:S(2)}, u32[]{:S(2)}) collective-permute-start(f32[8,8,8,128]{3,2,1,0:T(8,128)S(1)} %get-tuple-element.24), channel_id=1, source_target_pairs={{0,4},{4,0},{1,5},{5,1},{2,6},{6,2},{3,7},{7,3},{8,12},{12,8},{9,1... | collective-permute-start | bytes 786440 | tf_op jit(solution)/shard_map/ppermute | solution.py:372
  55.5 1.1 %collective-permute-done.1.b_ref = f32[8,8,8,128]{3,2,1,0:T(8,128)S(1)} collective-permute-done((f32[8,8,8,128]{3,2,1,0:T(8,128)S(1)}, f32[8,8,8,128]{3,2,1,0:T(8,128)S(1)}, u32[]{:S(2)}, u32[]{:S(2)}) %collective-permute-start.1) | collective-permute-done | bytes 262176 | tf_op jit(solution)/shard_map/ppermute | solution.py:372
  57.4 4.2 %all-to-all-start.2 = ((f32[64,8,128]{2,1,0:T(8,128)}), f32[64,8,128]{2,1,0:T(8,128)}, u32[]{:S(2)}, u32[]{:S(2)}) async-start(f32[64,8,128]{2,1,0:T(8,128)} %bitcast.9), calls=%async_computation.2 | async-start | bytes 524288 | tf_op jit(solution)/shard_map/all_to_all | solution.py:375
  61.6 2.3 %collective-permute-start.2 = (f32[128,1024]{1,0:T(8,128)}, f32[128,1024]{1,0:T(8,128)}, u32[]{:S(2)}, u32[]{:S(2)}) collective-permute-start(f32[128,1024]{1,0:T(8,128)} %copy-done.14), channel_id=1, source_target_pairs={{4,0},{8,4},{12,8},{16,12},{20,16},{24,20},{28,24},{32,28},{36,32}... | collective-permute-start | bytes 1572872 | tf_op jit(solution)/shard_map/ppermute | solution.py:374
  64.9 2.6 %shard_map.134 = (bf16[256,1024]{1,0:T(8,128)(2,1)}, f32[8,128]{1,0:T(8,128)S(1)}) custom-call(bf16[384,384]{1,0:T(8,128)(2,1)S(1)} %copy-done.3, bf16[256,1024]{1,0:T(8,128)(2,1)S(1)} %get-tuple-element.19.refs_1_, f32[128,1024]{1,0:T(8,128)S(1)} %copy-done.6, f32[256,1024]{1,0:T(8,128)S(1)} %copy-done.2, f32[128,1024]{1,0:T(8,128)S(1)} %copy-done.1, ...), custom_call_target="tpu_custom_call" | custom-call | flops 603979776 | bytes 1024 | tf_op jit(solution)/shard_map/pallas_call | solution.py:85
  67.6 4.0 %all-to-all-done.2 = f32[64,8,128]{2,1,0:T(8,128)} async-done(((f32[64,8,128]{2,1,0:T(8,128)}), f32[64,8,128]{2,1,0:T(8,128)}, u32[]{:S(2)}, u32[]{:S(2)}) %all-to-all-start.2) | async-done | bytes 262176 | tf_op jit(solution)/shard_map/all_to_all | solution.py:375
  71.6 1.6 %shard_map.137.refs_0_ = f32[4,4,8,128]{3,2,1,0:T(8,128)} custom-call(f32[16,4,8,128]{3,2,1,0:T(8,128)} %bitcast.4.parts_ref, f32[8,128]{1,0:T(8,128)S(1)} %get-tuple-element.25.refs_0_), custom_call_target="tpu_custom_call" | custom-call | bytes 331776 | tf_op jit(solution)/shard_map/pallas_call | solution.py:65
  73.2 6.0 %all-to-all-start.3 = ((f32[4,4,8,128]{3,2,1,0:T(8,128)}), f32[4,4,8,128]{3,2,1,0:T(8,128)S(1)}, u32[]{:S(2)}, u32[]{:S(2)}) async-start(f32[4,4,8,128]{3,2,1,0:T(8,128)} %shard_map.137.refs_0_), calls=%async_computation.3 | async-start | bytes 131072 | tf_op jit(solution)/shard_map/all_to_all | solution.py:386
  79.2 1.0 copy-done.10
  80.2 3.0 %shard_map.138 = (f32[256,1024]{1,0:T(8,128)S(1)}, f32[2,128]{1,0:T(2,128)S(1)}) custom-call(f32[4,4,8,128]{3,2,1,0:T(8,128)} %shard_map.137.refs_0_, bf16[384,384]{1,0:T(8,128)(2,1)S(1)} %copy-done.3, bf16[256,1024]{1,0:T(8,128)(2,1)S(1)} %copy-done.10, f32[128,1024]{1,0:T(8,128)} %collective-permute-done.2.refs_3_, f32[128,1024]{1,0:T(8,128)S(1)} %copy-done.1, ...), custom_call_target="tpu_custom_call" | custom-call | flops 603979776 | bytes 1024 | tf_op jit(solution)/shard_map/pallas_call | solution.py:85
  83.2 7.7 %all-to-all-done.3.parts_ref = f32[4,4,8,128]{3,2,1,0:T(8,128)S(1)} async-done(((f32[4,4,8,128]{3,2,1,0:T(8,128)}), f32[4,4,8,128]{3,2,1,0:T(8,128)S(1)}, u32[]{:S(2)}, u32[]{:S(2)}) %all-to-all-start.3) | async-done | bytes 65568 | tf_op jit(solution)/shard_map/all_to_all | solution.py:386
  91.6 3.8 %all-to-all-start.4 = ((f32[16,4,8,128]{3,2,1,0:T(8,128)}), f32[16,4,8,128]{3,2,1,0:T(8,128)S(1)}, u32[]{:S(2)}, u32[]{:S(2)}) async-start(f32[16,4,8,128]{3,2,1,0:T(8,128)} %shard_map.140), calls=%async_computation.4 | async-start | bytes 524288 | tf_op jit(solution)/shard_map/all_to_all | solution.py:398
  95.4 6.0 %psum.15.refs_1_.after_ref = f32[2,128]{1,0:T(2,128)S(1)} all-reduce(f32[2,128]{1,0:T(2,128)S(1)} %get-tuple-element.28.refs_0_), channel_id=1, replica_groups=mesh['y'=4,'zh'=4,'zl'=4,'core'=2,'chan'=4] {'chan'}, use_global_device_ids=true, to_apply=%region_1.0 | all-reduce | flops 256 | bytes 2048 | tf_op jit(solution)/shard_map/psum | solution.py:397
  101.4 2.0 %all-to-all-done.4 = f32[16,4,8,128]{3,2,1,0:T(8,128)S(1)} async-done(((f32[16,4,8,128]{3,2,1,0:T(8,128)}), f32[16,4,8,128]{3,2,1,0:T(8,128)S(1)}, u32[]{:S(2)}, u32[]{:S(2)}) %all-to-all-start.4) | async-done | bytes 262176 | tf_op jit(solution)/shard_map/all_to_all | solution.py:398
  103.5 6.3 %collective-permute-start.3 = (f32[64,8,128]{2,1,0:T(8,128)S(1)}, f32[64,8,128]{2,1,0:T(8,128)S(1)}, u32[]{:S(2)}, u32[]{:S(2)}) collective-permute-start(f32[64,8,128]{2,1,0:T(8,128)S(1)} %shard_map.141.own_ref), channel_id=1, source_target_pairs={{0,4},{4,0},{1,5},{5,1},{2,6},{6,2},{3,7},{7,3},{8,12},{12,8},{9,1... | collective-permute-start | bytes 786440 | tf_op jit(solution)/shard_map/ppermute | solution.py:405
  109.7 1.1 shard_map.139
  (40 shorter events, 4.9 us)
Async XLA Ops:
  0.6 18.8 %copy-start = (bf16[256,1024]{1,0:T(8,128)(2,1)S(1)}, bf16[256,1024]{1,0:T(8,128)(2,1)}, u32[]{:S(2)}) copy-start(bf16[256,1024]{1,0:T(8,128)(2,1)} %refs_3_.3) | copy-start | bytes 1572868
  3.5 27.5 %copy-start.4 = (bf16[256,1024]{1,0:T(8,128)(2,1)S(1)}, bf16[256,1024]{1,0:T(8,128)(2,1)}, u32[]{:S(2)}) copy-start(bf16[256,1024]{1,0:T(8,128)(2,1)} %refs_5_.1) | copy-start | bytes 1572868
  3.5 27.5 %copy-start.12 = (f32[1024]{0:T(1024)S(1)}, f32[1024]{0:T(1024)}, u32[]{:S(2)}) copy-start(f32[1024]{0:T(1024)} %param.11) | copy-start | bytes 12292
  3.5 27.5 %all-to-all-start = ((f32[16,8,128]{2,1,0:T(8,128)}), f32[16,8,128]{2,1,0:T(8,128)S(1)}, u32[]{:S(2)}, u32[]{:S(2)}) async-start(f32[16,8,128]{2,1,0:T(8,128)} %get-tuple-element.18), calls=%async_computation | async-start | bytes 131072 | tf_op jit(solution)/shard_map/all_to_all | solution.py:346
  19.4 29.8 %copy-start.2 = (f32[256,1024]{1,0:T(8,128)S(1)}, f32[256,1024]{1,0:T(8,128)}, u32[]{:S(2)}) copy-start(f32[256,1024]{1,0:T(8,128)} %get-tuple-element.21.refs_3_) | copy-start | bytes 3145732
  31.0 4.8 %copy-start.11 = (f32[1024]{0:T(1024)S(1)}, f32[1024]{0:T(1024)}, u32[]{:S(2)}) copy-start(f32[1024]{0:T(1024)} %param.18) | copy-start | bytes 12292
  31.0 4.8 %copy-start.13 = (f32[1024]{0:T(1024)S(1)}, f32[1024]{0:T(1024)}, u32[]{:S(2)}) copy-start(f32[1024]{0:T(1024)} %param.17) | copy-start | bytes 12292
  31.3 18.0 %copy-start.3 = (bf16[384,384]{1,0:T(8,128)(2,1)S(1)}, bf16[384,384]{1,0:T(8,128)(2,1)}, u32[]{:S(2)}) copy-start(bf16[384,384]{1,0:T(8,128)(2,1)} %constant.4.clone.refs_0_.refs_1_) | copy-start | bytes 884740
  31.3 17.9 %collective-permute-start = (f32[128,1024]{1,0:T(8,128)S(1)}, f32[128,1024]{1,0:T(8,128)S(1)}, u32[]{:S(2)}, u32[]{:S(2)}) collective-permute-start(f32[128,1024]{1,0:T(8,128)S(1)} %get-tuple-element.20), channel_id=1, source_target_pairs={{0,4},{4,8},{8,12},{12,16},{16,20},{20,24},{24,28},{28,32},{32,36}... | collective-permute-start | bytes 1572872 | tf_op jit(solution)/shard_map/ppermute | solution.py:356
  49.3 3.0 %copy-start.5 = (f32[128,1024]{1,0:T(8,128)}, f32[128,1024]{1,0:T(8,128)S(1)}, u32[]{:S(2)}) copy-start(f32[128,1024]{1,0:T(8,128)S(1)} %collective-permute-done.refs_2_) | copy-start | bytes 1572868
  49.3 1.2 %copy-start.8 = (bf16[256,1024]{1,0:T(8,128)(2,1)S(1)}, bf16[256,1024]{1,0:T(8,128)(2,1)}, u32[]{:S(2)}) copy-start(bf16[256,1024]{1,0:T(8,128)(2,1)} %refs_4_.4) | copy-start | bytes 1572868
  52.3 0.8 copy-start.14
  53.1 3.5 %copy-start.9 = (bf16[256,1024]{1,0:T(8,128)(2,1)}, bf16[256,1024]{1,0:T(8,128)(2,1)S(1)}, u32[]{:S(2)}) copy-start(bf16[256,1024]{1,0:T(8,128)(2,1)S(1)} %get-tuple-element.26.refs_2_) | copy-start | bytes 1572868
  53.1 3.5 %collective-permute-start.1 = (f32[8,8,8,128]{3,2,1,0:T(8,128)S(1)}, f32[8,8,8,128]{3,2,1,0:T(8,128)S(1)}, u32[]{:S(2)}, u32[]{:S(2)}) collective-permute-start(f32[8,8,8,128]{3,2,1,0:T(8,128)S(1)} %get-tuple-element.24), channel_id=1, source_target_pairs={{0,4},{4,0},{1,5},{5,1},{2,6},{6,2},{3,7},{7,3},{8,12},{12,8},{9,1... | collective-permute-start | bytes 786440 | tf_op jit(solution)/shard_map/ppermute | solution.py:372
  56.6 7.2 %copy-start.1 = (f32[128,1024]{1,0:T(8,128)S(1)}, f32[128,1024]{1,0:T(8,128)}, u32[]{:S(2)}) copy-start(f32[128,1024]{1,0:T(8,128)} %filter_ref.1) | copy-start | bytes 1572868
  56.7 0.7 copy-start.7
  57.4 14.2 %all-to-all-start.2 = ((f32[64,8,128]{2,1,0:T(8,128)}), f32[64,8,128]{2,1,0:T(8,128)}, u32[]{:S(2)}, u32[]{:S(2)}) async-start(f32[64,8,128]{2,1,0:T(8,128)} %bitcast.9), calls=%async_computation.2 | async-start | bytes 524288 | tf_op jit(solution)/shard_map/all_to_all | solution.py:375
  61.6 17.6 %collective-permute-start.2 = (f32[128,1024]{1,0:T(8,128)}, f32[128,1024]{1,0:T(8,128)}, u32[]{:S(2)}, u32[]{:S(2)}) collective-permute-start(f32[128,1024]{1,0:T(8,128)} %copy-done.14), channel_id=1, source_target_pairs={{4,0},{8,4},{12,8},{16,12},{20,16},{24,20},{28,24},{32,28},{36,32}... | collective-permute-start | bytes 1572872 | tf_op jit(solution)/shard_map/ppermute | solution.py:374
  63.9 1.0 copy-start.6
  73.2 17.7 %all-to-all-start.3 = ((f32[4,4,8,128]{3,2,1,0:T(8,128)}), f32[4,4,8,128]{3,2,1,0:T(8,128)S(1)}, u32[]{:S(2)}, u32[]{:S(2)}) async-start(f32[4,4,8,128]{3,2,1,0:T(8,128)} %shard_map.137.refs_0_), calls=%async_computation.3 | async-start | bytes 131072 | tf_op jit(solution)/shard_map/all_to_all | solution.py:386
  79.2 1.0 copy-start.10
  91.6 11.8 %all-to-all-start.4 = ((f32[16,4,8,128]{3,2,1,0:T(8,128)}), f32[16,4,8,128]{3,2,1,0:T(8,128)S(1)}, u32[]{:S(2)}, u32[]{:S(2)}) async-start(f32[16,4,8,128]{3,2,1,0:T(8,128)} %shard_map.140), calls=%async_computation.4 | async-start | bytes 524288 | tf_op jit(solution)/shard_map/all_to_all | solution.py:398
  103.5 7.4 %collective-permute-start.3 = (f32[64,8,128]{2,1,0:T(8,128)S(1)}, f32[64,8,128]{2,1,0:T(8,128)S(1)}, u32[]{:S(2)}, u32[]{:S(2)}) collective-permute-start(f32[64,8,128]{2,1,0:T(8,128)S(1)} %shard_map.141.own_ref), channel_id=1, source_target_pairs={{0,4},{4,0},{1,5},{5,1},{2,6},{6,2},{3,7},{7,3},{8,12},{12,8},{9,1... | collective-permute-start | bytes 786440 | tf_op jit(solution)/shard_map/ppermute | solution.py:405

commit v6 on v5

--- a/solution.py
+++ b/solution.py
@@ -180,7 +180,7 @@
     out_ref[:, 2] = jnp.broadcast_to(parts_ref[z], (count,) + DENSE)
 
 
-def carry_kernel(parts_ref, rate_ref, carry_ref):
+def find_carry(parts_ref, rate_ref, carry_ref):
     y, z, core = (lax.axis_index("y"), lax.axis_index(("zh", "zl")), lax.axis_index("core"))
     rate = rate_ref[...]
     decay = jnp.exp(-ROWS * rate)
@@ -231,9 +231,11 @@
 
 
 def filter_kernel(
-    step, fwd_ref, product_ref, rim_ref, local_ref, query_ref, rate_ref, scale_ref, carry_ref,
-    keep_ref, send_ref, mixed_grad_ref, head_ref,
+    step, fwd_ref, product_ref, rim_ref, local_ref, query_ref, rate_ref, scale_ref, sums_ref,
+    keep_ref, send_ref, mixed_grad_ref, head_ref, carry_ref,
 ):
+    if step == 0:
+        find_carry(sums_ref, rate_ref, carry_ref)
     ext = jnp.concatenate([rim_ref[...].astype(BF16), product_ref[...]], axis=0)
     product = dot(fwd_ref[...], ext)
     grad_mixed = query_ref[...].astype(F32) * grad_stored(step, local_ref, rate_ref, scale_ref, carry_ref)
@@ -358,13 +360,12 @@
         column_kernel, [shape((2 * Y, 3) + DENSE)], column, rate, scale
     )
     sums = lax.all_to_all(sums, ("y", "core"), 0, 0, tiled=True)
-    (carry,) = small(carry_kernel, [shape(DENSE)], sums, rate)
 
     half = (GROUPS // 2, TILES, 8, LANES)
-    keep, send, grad_mixed, head = large(
-        filter_kernel, [shape(half), shape(half), shape(FULL, BF16), shape((TAPS, CHANS))],
-        [blocks, blocks, cols, cols],
-        (forward, product, before, local, gate_query, rate, scale, carry),
+    keep, send, grad_mixed, head, carry = large(
+        filter_kernel, [shape(half), shape(half), shape(FULL, BF16), shape((TAPS, CHANS)), shape(DENSE)],
+        [blocks, blocks, cols, cols, None],
+        (forward, product, before, local, gate_query, rate, scale, sums),
         [None, cols, cols, cols, cols, None, None, None],
         flops=2 * CHANS * POINTS * (POINTS + ROWS + TAPS),
     )

time: 113 us -> 113 us (level)
    pallas_call x7 -> x6, Pallas kernels: 3.39 us -> 3.36 us  [small(): pl.pallas_call(kernel, out_shape=tuple(outs), in_specs=[VMEM] * len(args)...]
where the time goes in v6:
time: 113 us; the launch traced here: 112 us
  starting transfers between devices  45.2 us (40%)
  blocking collectives  28.5 us (25%)
  waiting for transfers between devices  17.1 us (15%)
  Pallas kernels  15.2 us (13%)
  local copies, waits for them, and re-layouts  4.84 us (4%)
    all_to_all x1, starting transfers between devices, body(): column = lax.all_to_all(spread, ('zh', 'zl'), 0, 0, tiled=True)  15.9 us
    all_to_all x1, blocking collectives, body(): sums = lax.all_to_all(sums, ('y', 'core'), 0, 0, tiled=True)  13.3 us
    pallas_call x7, Pallas kernels, large(): pl.pallas_call(stepped, out_shape=tuple(outs), in_specs=specs[:len(args)]...  11.8 us
    psum x1, blocking collectives, body(): squares = lax.psum(squares, 'chan')  9.17 us
    all_to_all x1, waiting for transfers between devices, body(): parts = lax.all_to_all(spread, 'zh', 0, 0, tiled=True)  7.68 us
    ppermute x1, starting transfers between devices, body(): other_half = lax.ppermute(own_half, 'core', swap)  6.26 us
    psum x1, blocking collectives, body(): dots = lax.psum(dots, 'chan')  6.01 us
    all_to_all x1, starting transfers between devices, body(): parts = lax.all_to_all(spread, 'zh', 0, 0, tiled=True)  6 us
  transfers between devices with their start and end apart: 8, of which 6 were waited for; matrix products, arithmetic and copies ran while one was open for 0% of the time, Pallas kernels for 8%

profile of v6, /device:TPU:1, one launch (start us, length us, event | category | flops | bytes accessed | tf_op | source)
XLA Modules:
  0.0 111.8 jit_solution(3985680722019375220)
XLA Ops:
  0.6 2.9 %shard_map.129 = (f32[16,8,128]{2,1,0:T(8,128)}, f32[256,1024]{1,0:T(8,128)}) custom-call(bf16[256,1024]{1,0:T(8,128)(2,1)} %refs_0_.4, bf16[256,1024]{1,0:T(8,128)(2,1)} %refs_1_.2, f32[8,128]{1,0:T(8,128)} %bitcast.11), custom_call_target="tpu_custom_call" | custom-call | bytes 1024 | tf_op jit(solution)/shard_map/pallas_call | solution.py:85
  3.5 15.9 %all-to-all-start = ((f32[16,8,128]{2,1,0:T(8,128)}), f32[16,8,128]{2,1,0:T(8,128)S(1)}, u32[]{:S(2)}, u32[]{:S(2)}) async-start(f32[16,8,128]{2,1,0:T(8,128)} %get-tuple-element.19), calls=%async_computation | async-start | bytes 131072 | tf_op jit(solution)/shard_map/all_to_all | solution.py:348
  19.6 9.2 %psum.14.refs_1_.refs_0_ = f32[2,128]{1,0:T(2,128)S(1)} all-reduce(f32[2,128]{1,0:T(2,128)S(1)} %shard_map.130), channel_id=1, replica_groups=mesh['y'=4,'zh'=4,'zl'=4,'core'=2,'chan'=4] {'chan'}, use_global_device_ids=true, to_apply=%region_0.0 | all-reduce | flops 256 | bytes 2048 | tf_op jit(solution)/shard_map/psum | solution.py:352
  28.8 2.2 %all-to-all-done.refs_0_.parts_ref = f32[16,8,128]{2,1,0:T(8,128)S(1)} async-done(((f32[16,8,128]{2,1,0:T(8,128)}), f32[16,8,128]{2,1,0:T(8,128)S(1)}, u32[]{:S(2)}, u32[]{:S(2)}) %all-to-all-start) | async-done | bytes 65568 | tf_op jit(solution)/shard_map/all_to_all | solution.py:348
  31.3 4.5 %collective-permute-start = (f32[128,1024]{1,0:T(8,128)S(1)}, f32[128,1024]{1,0:T(8,128)S(1)}, u32[]{:S(2)}, u32[]{:S(2)}) collective-permute-start(f32[128,1024]{1,0:T(8,128)S(1)} %get-tuple-element.21), channel_id=1, source_target_pairs={{0,4},{4,8},{8,12},{12,16},{16,20},{20,24},{24,28},{28,32},{32,36}... | collective-permute-start | bytes 1572872 | tf_op jit(solution)/shard_map/ppermute | solution.py:358
  35.9 13.3 %all_to_all.25.refs_7_ = f32[8,3,8,128]{3,2,1,0:T(8,128)S(1)} all-to-all(f32[8,3,8,128]{3,2,1,0:T(8,128)S(1)} %shard_map.132), channel_id=1, replica_groups=mesh['y'=4,'zh'=4,'zl'=4,'core'=2,'chan'=4] {'y','core'}, dimensions={0} | all-to-all | bytes 196608 | tf_op jit(solution)/shard_map/all_to_all | solution.py:362
  49.3 1.2 %copy-done.8 = bf16[256,1024]{1,0:T(8,128)(2,1)S(1)} copy-done((bf16[256,1024]{1,0:T(8,128)(2,1)S(1)}, bf16[256,1024]{1,0:T(8,128)(2,1)}, u32[]{:S(2)}) %copy-start.8) | copy-done | bytes 524312
  50.5 1.8 %shard_map.133 = (f32[8,8,8,128]{3,2,1,0:T(8,128)S(1)}, f32[8,8,8,128]{3,2,1,0:T(8,128)S(1)}, bf16[256,1024]{1,0:T(8,128)(2,1)S(1)}, f32[128,1024]{1,0:T(8,128)S(1)}, f32[8,128]{1,0:T(8,128)S(1)}) custom-call(bf16[384,384]{1,0:T(8,128)(2,1)S(1)} %copy-done.3, bf16[256,1024]{1,0:T(8,128)(2,1)S(1)} %get-tuple-element.20.refs_1_, ...), custom_call_target="tpu_custom_call" | custom-call | flops 603979776 | bytes 1024 | tf_op jit(solution)/shard_map/pallas_call | solution.py:85
  53.1 2.3 %collective-permute-start.1 = (f32[8,8,8,128]{3,2,1,0:T(8,128)S(1)}, f32[8,8,8,128]{3,2,1,0:T(8,128)S(1)}, u32[]{:S(2)}, u32[]{:S(2)}) collective-permute-start(f32[8,8,8,128]{3,2,1,0:T(8,128)S(1)} %get-tuple-element.26), channel_id=1, source_target_pairs={{0,4},{4,0},{1,5},{5,1},{2,6},{6,2},{3,7},{7,3},{8,12},{12,8},{9,1... | collective-permute-start | bytes 786440 | tf_op jit(solution)/shard_map/ppermute | solution.py:373
  55.5 1.1 %collective-permute-done.1.b_ref = f32[8,8,8,128]{3,2,1,0:T(8,128)S(1)} collective-permute-done((f32[8,8,8,128]{3,2,1,0:T(8,128)S(1)}, f32[8,8,8,128]{3,2,1,0:T(8,128)S(1)}, u32[]{:S(2)}, u32[]{:S(2)}) %collective-permute-start.1) | collective-permute-done | bytes 262176 | tf_op jit(solution)/shard_map/ppermute | solution.py:373
  57.3 4.2 %all-to-all-start.2 = ((f32[64,8,128]{2,1,0:T(8,128)}), f32[64,8,128]{2,1,0:T(8,128)}, u32[]{:S(2)}, u32[]{:S(2)}) async-start(f32[64,8,128]{2,1,0:T(8,128)} %bitcast.9), calls=%async_computation.2 | async-start | bytes 524288 | tf_op jit(solution)/shard_map/all_to_all | solution.py:376
  61.5 2.3 %collective-permute-start.2 = (f32[128,1024]{1,0:T(8,128)}, f32[128,1024]{1,0:T(8,128)}, u32[]{:S(2)}, u32[]{:S(2)}) collective-permute-start(f32[128,1024]{1,0:T(8,128)} %copy-done.14), channel_id=1, source_target_pairs={{4,0},{8,4},{12,8},{16,12},{20,16},{24,20},{28,24},{32,28},{36,32}... | collective-permute-start | bytes 1572872 | tf_op jit(solution)/shard_map/ppermute | solution.py:375
  64.9 2.6 %shard_map.134 = (bf16[256,1024]{1,0:T(8,128)(2,1)}, f32[8,128]{1,0:T(8,128)S(1)}) custom-call(bf16[384,384]{1,0:T(8,128)(2,1)S(1)} %copy-done.3, bf16[256,1024]{1,0:T(8,128)(2,1)S(1)} %get-tuple-element.20.refs_1_, f32[128,1024]{1,0:T(8,128)S(1)} %copy-done.6, f32[256,1024]{1,0:T(8,128)S(1)} %copy-done.2, f32[128,1024]{1,0:T(8,128)S(1)} %copy-done.1, ...), custom_call_target="tpu_custom_call" | custom-call | flops 603979776 | bytes 1024 | tf_op jit(solution)/shard_map/pallas_call | solution.py:85
  67.5 4.0 %all-to-all-done.2 = f32[64,8,128]{2,1,0:T(8,128)} async-done(((f32[64,8,128]{2,1,0:T(8,128)}), f32[64,8,128]{2,1,0:T(8,128)}, u32[]{:S(2)}, u32[]{:S(2)}) %all-to-all-start.2) | async-done | bytes 262176 | tf_op jit(solution)/shard_map/all_to_all | solution.py:376
  71.5 1.6 %shard_map.136.refs_0_ = f32[4,4,8,128]{3,2,1,0:T(8,128)} custom-call(f32[16,4,8,128]{3,2,1,0:T(8,128)} %bitcast.4.parts_ref, f32[8,128]{1,0:T(8,128)S(1)} %get-tuple-element.27.refs_0_), custom_call_target="tpu_custom_call" | custom-call | bytes 331776 | tf_op jit(solution)/shard_map/pallas_call | solution.py:65
  73.1 6.0 %all-to-all-start.3 = ((f32[4,4,8,128]{3,2,1,0:T(8,128)}), f32[4,4,8,128]{3,2,1,0:T(8,128)S(1)}, u32[]{:S(2)}, u32[]{:S(2)}) async-start(f32[4,4,8,128]{3,2,1,0:T(8,128)} %shard_map.136.refs_0_), calls=%async_computation.3 | async-start | bytes 131072 | tf_op jit(solution)/shard_map/all_to_all | solution.py:387
  79.1 1.0 copy-done.10
  80.2 3.0 %shard_map.137 = (f32[256,1024]{1,0:T(8,128)S(1)}, f32[2,128]{1,0:T(2,128)S(1)}) custom-call(f32[4,4,8,128]{3,2,1,0:T(8,128)} %shard_map.136.refs_0_, bf16[384,384]{1,0:T(8,128)(2,1)S(1)} %copy-done.3, bf16[256,1024]{1,0:T(8,128)(2,1)S(1)} %copy-done.10, f32[128,1024]{1,0:T(8,128)} %collective-permute-done.2.refs_3_, f32[128,1024]{1,0:T(8,128)S(1)} %copy-done.1, ...), custom_call_target="tpu_custom_call" | custom-call | flops 603979776 | bytes 1024 | tf_op jit(solution)/shard_map/pallas_call | solution.py:85
  83.2 7.7 %all-to-all-done.3.parts_ref = f32[4,4,8,128]{3,2,1,0:T(8,128)S(1)} async-done(((f32[4,4,8,128]{3,2,1,0:T(8,128)}), f32[4,4,8,128]{3,2,1,0:T(8,128)S(1)}, u32[]{:S(2)}, u32[]{:S(2)}) %all-to-all-start.3) | async-done | bytes 65568 | tf_op jit(solution)/shard_map/all_to_all | solution.py:387
  91.6 3.8 %all-to-all-start.4 = ((f32[16,4,8,128]{3,2,1,0:T(8,128)}), f32[16,4,8,128]{3,2,1,0:T(8,128)S(1)}, u32[]{:S(2)}, u32[]{:S(2)}) async-start(f32[16,4,8,128]{3,2,1,0:T(8,128)} %shard_map.139), calls=%async_computation.4 | async-start | bytes 524288 | tf_op jit(solution)/shard_map/all_to_all | solution.py:399
  95.4 6.0 %psum.15.refs_1_.after_ref = f32[2,128]{1,0:T(2,128)S(1)} all-reduce(f32[2,128]{1,0:T(2,128)S(1)} %get-tuple-element.30.refs_0_), channel_id=1, replica_groups=mesh['y'=4,'zh'=4,'zl'=4,'core'=2,'chan'=4] {'chan'}, use_global_device_ids=true, to_apply=%region_1.0 | all-reduce | flops 256 | bytes 2048 | tf_op jit(solution)/shard_map/psum | solution.py:398
  101.4 2.0 %all-to-all-done.4 = f32[16,4,8,128]{3,2,1,0:T(8,128)S(1)} async-done(((f32[16,4,8,128]{3,2,1,0:T(8,128)}), f32[16,4,8,128]{3,2,1,0:T(8,128)S(1)}, u32[]{:S(2)}, u32[]{:S(2)}) %all-to-all-start.4) | async-done | bytes 262176 | tf_op jit(solution)/shard_map/all_to_all | solution.py:399
  103.4 6.3 %collective-permute-start.3 = (f32[64,8,128]{2,1,0:T(8,128)S(1)}, f32[64,8,128]{2,1,0:T(8,128)S(1)}, u32[]{:S(2)}, u32[]{:S(2)}) collective-permute-start(f32[64,8,128]{2,1,0:T(8,128)S(1)} %shard_map.140.own_ref), channel_id=1, source_target_pairs={{0,4},{4,0},{1,5},{5,1},{2,6},{6,2},{3,7},{7,3},{8,12},{12,8},{9,1... | collective-permute-start | bytes 786440 | tf_op jit(solution)/shard_map/ppermute | solution.py:406
  109.7 1.1 shard_map.138
  (39 shorter events, 4.9 us)
Async XLA Ops:
  0.6 18.8 %copy-start = (bf16[256,1024]{1,0:T(8,128)(2,1)S(1)}, bf16[256,1024]{1,0:T(8,128)(2,1)}, u32[]{:S(2)}) copy-start(bf16[256,1024]{1,0:T(8,128)(2,1)} %refs_3_.3) | copy-start | bytes 1572868
  3.5 27.5 %copy-start.4 = (bf16[256,1024]{1,0:T(8,128)(2,1)S(1)}, bf16[256,1024]{1,0:T(8,128)(2,1)}, u32[]{:S(2)}) copy-start(bf16[256,1024]{1,0:T(8,128)(2,1)} %refs_5_.1) | copy-start | bytes 1572868
  3.5 27.5 %copy-start.12 = (f32[1024]{0:T(1024)S(1)}, f32[1024]{0:T(1024)}, u32[]{:S(2)}) copy-start(f32[1024]{0:T(1024)} %param.11) | copy-start | bytes 12292
  3.5 27.5 %all-to-all-start = ((f32[16,8,128]{2,1,0:T(8,128)}), f32[16,8,128]{2,1,0:T(8,128)S(1)}, u32[]{:S(2)}, u32[]{:S(2)}) async-start(f32[16,8,128]{2,1,0:T(8,128)} %get-tuple-element.19), calls=%async_computation | async-start | bytes 131072 | tf_op jit(solution)/shard_map/all_to_all | solution.py:348
  19.4 29.8 %copy-start.2 = (f32[256,1024]{1,0:T(8,128)S(1)}, f32[256,1024]{1,0:T(8,128)}, u32[]{:S(2)}) copy-start(f32[256,1024]{1,0:T(8,128)} %get-tuple-element.22.refs_3_) | copy-start | bytes 3145732
  31.0 4.8 %copy-start.11 = (f32[1024]{0:T(1024)S(1)}, f32[1024]{0:T(1024)}, u32[]{:S(2)}) copy-start(f32[1024]{0:T(1024)} %param.18) | copy-start | bytes 12292
  31.0 4.8 %copy-start.13 = (f32[1024]{0:T(1024)S(1)}, f32[1024]{0:T(1024)}, u32[]{:S(2)}) copy-start(f32[1024]{0:T(1024)} %param.17) | copy-start | bytes 12292
  31.3 17.9 %copy-start.3 = (bf16[384,384]{1,0:T(8,128)(2,1)S(1)}, bf16[384,384]{1,0:T(8,128)(2,1)}, u32[]{:S(2)}) copy-start(bf16[384,384]{1,0:T(8,128)(2,1)} %constant.4.clone.refs_0_.refs_1_) | copy-start | bytes 884740
  31.3 17.9 %collective-permute-start = (f32[128,1024]{1,0:T(8,128)S(1)}, f32[128,1024]{1,0:T(8,128)S(1)}, u32[]{:S(2)}, u32[]{:S(2)}) collective-permute-start(f32[128,1024]{1,0:T(8,128)S(1)} %get-tuple-element.21), channel_id=1, source_target_pairs={{0,4},{4,8},{8,12},{12,16},{16,20},{20,24},{24,28},{28,32},{32,36}... | collective-permute-start | bytes 1572872 | tf_op jit(solution)/shard_map/ppermute | solution.py:358
  49.2 3.1 %copy-start.5 = (f32[128,1024]{1,0:T(8,128)}, f32[128,1024]{1,0:T(8,128)S(1)}, u32[]{:S(2)}) copy-start(f32[128,1024]{1,0:T(8,128)S(1)} %collective-permute-done.refs_2_) | copy-start | bytes 1572868
  49.2 1.2 %copy-start.8 = (bf16[256,1024]{1,0:T(8,128)(2,1)S(1)}, bf16[256,1024]{1,0:T(8,128)(2,1)}, u32[]{:S(2)}) copy-start(bf16[256,1024]{1,0:T(8,128)(2,1)} %refs_4_.3) | copy-start | bytes 1572868
  52.3 0.8 copy-start.14
  53.1 3.5 %copy-start.9 = (bf16[256,1024]{1,0:T(8,128)(2,1)}, bf16[256,1024]{1,0:T(8,128)(2,1)S(1)}, u32[]{:S(2)}) copy-start(bf16[256,1024]{1,0:T(8,128)(2,1)S(1)} %get-tuple-element.28.refs_2_) | copy-start | bytes 1572868
  53.1 3.5 %collective-permute-start.1 = (f32[8,8,8,128]{3,2,1,0:T(8,128)S(1)}, f32[8,8,8,128]{3,2,1,0:T(8,128)S(1)}, u32[]{:S(2)}, u32[]{:S(2)}) collective-permute-start(f32[8,8,8,128]{3,2,1,0:T(8,128)S(1)} %get-tuple-element.26), channel_id=1, source_target_pairs={{0,4},{4,0},{1,5},{5,1},{2,6},{6,2},{3,7},{7,3},{8,12},{12,8},{9,1... | collective-permute-start | bytes 786440 | tf_op jit(solution)/shard_map/ppermute | solution.py:373
  56.6 7.2 %copy-start.1 = (f32[128,1024]{1,0:T(8,128)S(1)}, f32[128,1024]{1,0:T(8,128)}, u32[]{:S(2)}) copy-start(f32[128,1024]{1,0:T(8,128)} %filter_ref.1) | copy-start | bytes 1572868
  56.6 0.7 copy-start.7
  57.3 14.2 %all-to-all-start.2 = ((f32[64,8,128]{2,1,0:T(8,128)}), f32[64,8,128]{2,1,0:T(8,128)}, u32[]{:S(2)}, u32[]{:S(2)}) async-start(f32[64,8,128]{2,1,0:T(8,128)} %bitcast.9), calls=%async_computation.2 | async-start | bytes 524288 | tf_op jit(solution)/shard_map/all_to_all | solution.py:376
  61.5 17.6 %collective-permute-start.2 = (f32[128,1024]{1,0:T(8,128)}, f32[128,1024]{1,0:T(8,128)}, u32[]{:S(2)}, u32[]{:S(2)}) collective-permute-start(f32[128,1024]{1,0:T(8,128)} %copy-done.14), channel_id=1, source_target_pairs={{4,0},{8,4},{12,8},{16,12},{20,16},{24,20},{28,24},{32,28},{36,32}... | collective-permute-start | bytes 1572872 | tf_op jit(solution)/shard_map/ppermute | solution.py:375
  63.8 1.0 copy-start.6
  73.1 17.7 %all-to-all-start.3 = ((f32[4,4,8,128]{3,2,1,0:T(8,128)}), f32[4,4,8,128]{3,2,1,0:T(8,128)S(1)}, u32[]{:S(2)}, u32[]{:S(2)}) async-start(f32[4,4,8,128]{3,2,1,0:T(8,128)} %shard_map.136.refs_0_), calls=%async_computation.3 | async-start | bytes 131072 | tf_op jit(solution)/shard_map/all_to_all | solution.py:387
  79.1 1.0 copy-start.10
  91.6 11.8 %all-to-all-start.4 = ((f32[16,4,8,128]{3,2,1,0:T(8,128)}), f32[16,4,8,128]{3,2,1,0:T(8,128)S(1)}, u32[]{:S(2)}, u32[]{:S(2)}) async-start(f32[16,4,8,128]{3,2,1,0:T(8,128)} %shard_map.139), calls=%async_computation.4 | async-start | bytes 524288 | tf_op jit(solution)/shard_map/all_to_all | solution.py:399
  103.4 7.4 %collective-permute-start.3 = (f32[64,8,128]{2,1,0:T(8,128)S(1)}, f32[64,8,128]{2,1,0:T(8,128)S(1)}, u32[]{:S(2)}, u32[]{:S(2)}) collective-permute-start(f32[64,8,128]{2,1,0:T(8,128)S(1)} %shard_map.140.own_ref), channel_id=1, source_target_pairs={{0,4},{4,0},{1,5},{5,1},{2,6},{6,2},{3,7},{7,3},{8,12},{12,8},{9,1... | collective-permute-start | bytes 786440 | tf_op jit(solution)/shard_map/ppermute | solution.py:406

commit v7 on v6

--- a/solution.py
+++ b/solution.py
@@ -232,11 +232,13 @@
 
 def filter_kernel(
     step, fwd_ref, product_ref, rim_ref, local_ref, query_ref, rate_ref, scale_ref, sums_ref,
-    keep_ref, send_ref, mixed_grad_ref, head_ref, carry_ref,
+    keep_ref, send_ref, mixed_grad_ref, head_ref, carry_ref, edge_ref,
 ):
     if step == 0:
         find_carry(sums_ref, rate_ref, carry_ref)
-    ext = jnp.concatenate([rim_ref[...].astype(BF16), product_ref[...]], axis=0)
+    edge = rim_ref[...].astype(BF16)
+    edge_ref[...] = edge
+    ext = jnp.concatenate([edge, product_ref[...]], axis=0)
     product = dot(fwd_ref[...], ext)
     grad_mixed = query_ref[...].astype(F32) * grad_stored(step, local_ref, rate_ref, scale_ref, carry_ref)
     head_ref[...] = grad_mixed[:TAPS]
@@ -256,9 +258,9 @@
 
 
 def query_kernel(
-    step, fwd_ref, product_ref, rim_ref, local_ref, filter_ref, rate_ref, scale_ref, carry_ref, grad_ref, token_ref
+    step, fwd_ref, product_ref, edge_ref, local_ref, filter_ref, rate_ref, scale_ref, carry_ref, grad_ref, token_ref
 ):
-    ext = jnp.concatenate([rim_ref[...].astype(BF16), product_ref[...]], axis=0)
+    ext = jnp.concatenate([edge_ref[...], product_ref[...]], axis=0)
     product = dot(fwd_ref[...], ext)
     taps = dot(fwd_ref[:, :TAPS], filter_ref[...].astype(BF16))
     mixed = dot_back(fwd_ref[:, TAPS:], mul(product, taps)) * (2.0 / POINTS)
@@ -362,9 +364,10 @@
     sums = lax.all_to_all(sums, ("y", "core"), 0, 0, tiled=True)
 
     half = (GROUPS // 2, TILES, 8, LANES)
-    keep, send, grad_mixed, head, carry = large(
-        filter_kernel, [shape(half), shape(half), shape(FULL, BF16), shape((TAPS, CHANS)), shape(DENSE)],
-        [blocks, blocks, cols, cols, None],
+    keep, send, grad_mixed, head, carry, edge = large(
+        filter_kernel, [shape(half), shape(half), shape(FULL, BF16), shape((TAPS, CHANS)), shape(DENSE),
+         shape((TAPS, CHANS), BF16)],
+        [blocks, blocks, cols, cols, None, cols],
         (forward, product, before, local, gate_query, rate, scale, sums),
         [None, cols, cols, cols, cols, None, None, None],
         flops=2 * CHANS * POINTS * (POINTS + ROWS + TAPS),
@@ -376,7 +379,7 @@
     parts = lax.all_to_all(chip_sum.reshape(PLANE, 8, LANES), ("y", "zl"), 0, 0, tiled=True)
     grad_query, token = large(
         query_kernel, [shape(FULL, BF16), shape(DENSE)], [cols, None],
-        (forward, product, before, local, medium_filter, rate, scale, carry),
+        (forward, product, edge, local, medium_filter, rate, scale, carry),
         [None, cols, cols, cols, cols, None, None, None],
         flops=2 * CHANS * POINTS * (POINTS + ROWS + TAPS),
     )

time: 113 us -> 112 us (level)
  no operation moved by 1% of the time
where the time goes in v7:
time: 112 us
  starting transfers between devices  45.2 us (40%)
  blocking collectives  28.5 us (25%)
  waiting for transfers between devices  17.2 us (15%)
  Pallas kernels  15.2 us (14%)
  local copies, waits for them, and re-layouts  4.55 us (4%)
    all_to_all x1, starting transfers between devices, body(): column = lax.all_to_all(spread, ('zh', 'zl'), 0, 0, tiled=True)  15.9 us
    all_to_all x1, blocking collectives, body(): sums = lax.all_to_all(sums, ('y', 'core'), 0, 0, tiled=True)  13.3 us
    pallas_call x7, Pallas kernels, large(): pl.pallas_call(stepped, out_shape=tuple(outs), in_specs=specs[:len(args)]...  11.8 us
    psum x1, blocking collectives, body(): squares = lax.psum(squares, 'chan')  9.17 us
    all_to_all x1, waiting for transfers between devices, body(): parts = lax.all_to_all(spread, 'zh', 0, 0, tiled=True)  7.69 us
    ppermute x1, starting transfers between devices, body(): other_half = lax.ppermute(own_half, 'core', swap)  6.26 us
    psum x1, blocking collectives, body(): dots = lax.psum(dots, 'chan')  6.01 us
    all_to_all x1, starting transfers between devices, body(): parts = lax.all_to_all(spread, 'zh', 0, 0, tiled=True)  6 us
  transfers between devices with their start and end apart: 8, of which 6 were waited for; matrix products, arithmetic and copies ran while one was open for 0% of the time, Pallas kernels for 8%

profile of v7, /device:TPU:1, one launch (start us, length us, event | category | flops | bytes accessed | tf_op | source)
XLA Modules:
  0.0 111.5 jit_solution(15936728468907338801)
XLA Ops:
  0.6 2.9 %shard_map.129 = (f32[16,8,128]{2,1,0:T(8,128)}, f32[256,1024]{1,0:T(8,128)}) custom-call(bf16[256,1024]{1,0:T(8,128)(2,1)} %refs_0_.4, bf16[256,1024]{1,0:T(8,128)(2,1)} %refs_1_.2, f32[8,128]{1,0:T(8,128)} %bitcast.11), custom_call_target="tpu_custom_call" | custom-call | bytes 1024 | tf_op jit(solution)/shard_map/pallas_call | solution.py:85
  3.5 15.9 %all-to-all-start = ((f32[16,8,128]{2,1,0:T(8,128)}), f32[16,8,128]{2,1,0:T(8,128)S(1)}, u32[]{:S(2)}, u32[]{:S(2)}) async-start(f32[16,8,128]{2,1,0:T(8,128)} %get-tuple-element.20), calls=%async_computation | async-start | bytes 131072 | tf_op jit(solution)/shard_map/all_to_all | solution.py:350
  19.6 9.2 %psum.14.refs_1_.refs_0_ = f32[2,128]{1,0:T(2,128)S(1)} all-reduce(f32[2,128]{1,0:T(2,128)S(1)} %shard_map.130), channel_id=1, replica_groups=mesh['y'=4,'zh'=4,'zl'=4,'core'=2,'chan'=4] {'chan'}, use_global_device_ids=true, to_apply=%region_0.0 | all-reduce | flops 256 | bytes 2048 | tf_op jit(solution)/shard_map/psum | solution.py:354
  28.8 2.2 %all-to-all-done.refs_0_.parts_ref = f32[16,8,128]{2,1,0:T(8,128)S(1)} async-done(((f32[16,8,128]{2,1,0:T(8,128)}), f32[16,8,128]{2,1,0:T(8,128)S(1)}, u32[]{:S(2)}, u32[]{:S(2)}) %all-to-all-start) | async-done | bytes 65568 | tf_op jit(solution)/shard_map/all_to_all | solution.py:350
  31.3 4.5 %collective-permute-start = (f32[128,1024]{1,0:T(8,128)S(1)}, f32[128,1024]{1,0:T(8,128)S(1)}, u32[]{:S(2)}, u32[]{:S(2)}) collective-permute-start(f32[128,1024]{1,0:T(8,128)S(1)} %get-tuple-element.22), channel_id=1, source_target_pairs={{0,4},{4,8},{8,12},{12,16},{16,20},{20,24},{24,28},{28,32},{32,36}... | collective-permute-start | bytes 1572872 | tf_op jit(solution)/shard_map/ppermute | solution.py:360
  35.9 13.3 %all_to_all.25.refs_7_ = f32[8,3,8,128]{3,2,1,0:T(8,128)S(1)} all-to-all(f32[8,3,8,128]{3,2,1,0:T(8,128)S(1)} %shard_map.132), channel_id=1, replica_groups=mesh['y'=4,'zh'=4,'zl'=4,'core'=2,'chan'=4] {'y','core'}, dimensions={0} | all-to-all | bytes 196608 | tf_op jit(solution)/shard_map/all_to_all | solution.py:364
  49.2 1.0 copy-done.6
  50.3 1.8 %shard_map.133 = (f32[8,8,8,128]{3,2,1,0:T(8,128)S(1)}, f32[8,8,8,128]{3,2,1,0:T(8,128)S(1)}, bf16[256,1024]{1,0:T(8,128)(2,1)S(1)}, f32[128,1024]{1,0:T(8,128)S...) custom-call(bf16[384,384]{1,0:T(8,128)(2,1)S(1)} %copy-done.3, ...), custom_call_target="tpu_custom_call" | custom-call | flops 603979776 | bytes 1024 | tf_op jit(solution)/shard_map/pallas_call | solution.py:85
  52.9 2.3 %collective-permute-start.1 = (f32[8,8,8,128]{3,2,1,0:T(8,128)S(1)}, f32[8,8,8,128]{3,2,1,0:T(8,128)S(1)}, u32[]{:S(2)}, u32[]{:S(2)}) collective-permute-start(f32[8,8,8,128]{3,2,1,0:T(8,128)S(1)} %get-tuple-element.28), channel_id=1, source_target_pairs={{0,4},{4,0},{1,5},{5,1},{2,6},{6,2},{3,7},{7,3},{8,12},{12,8},{9,1... | collective-permute-start | bytes 786440 | tf_op jit(solution)/shard_map/ppermute | solution.py:376
  55.2 1.1 %collective-permute-done.1.b_ref = f32[8,8,8,128]{3,2,1,0:T(8,128)S(1)} collective-permute-done((f32[8,8,8,128]{3,2,1,0:T(8,128)S(1)}, f32[8,8,8,128]{3,2,1,0:T(8,128)S(1)}, u32[]{:S(2)}, u32[]{:S(2)}) %collective-permute-start.1) | collective-permute-done | bytes 262176 | tf_op jit(solution)/shard_map/ppermute | solution.py:376
  57.1 4.2 %all-to-all-start.2 = ((f32[64,8,128]{2,1,0:T(8,128)}), f32[64,8,128]{2,1,0:T(8,128)}, u32[]{:S(2)}, u32[]{:S(2)}) async-start(f32[64,8,128]{2,1,0:T(8,128)} %bitcast.9), calls=%async_computation.2 | async-start | bytes 524288 | tf_op jit(solution)/shard_map/all_to_all | solution.py:379
  61.3 2.3 %collective-permute-start.2 = (f32[128,1024]{1,0:T(8,128)}, f32[128,1024]{1,0:T(8,128)}, u32[]{:S(2)}, u32[]{:S(2)}) collective-permute-start(f32[128,1024]{1,0:T(8,128)} %copy-done.14), channel_id=1, source_target_pairs={{4,0},{8,4},{12,8},{16,12},{20,16},{24,20},{28,24},{32,28},{36,32}... | collective-permute-start | bytes 1572872 | tf_op jit(solution)/shard_map/ppermute | solution.py:378
  64.6 2.7 %shard_map.134 = (bf16[256,1024]{1,0:T(8,128)(2,1)}, f32[8,128]{1,0:T(8,128)S(1)}) custom-call(bf16[384,384]{1,0:T(8,128)(2,1)S(1)} %copy-done.3, bf16[256,1024]{1,0:T(8,128)(2,1)S(1)} %get-tuple-element.21.refs_1_, bf16[128,1024]{1,0:T(8,128)(2,1)S(1)} %copy-done.10, f32[256,1024]{1,0:T(8,128)S(1)} %copy-done.2, f32[128,1024]{1,0:T(8,128)S(1)} %copy-done.1, ...), custom_call_target="tpu_custom_call" | custom-call | flops 603979776 | bytes 1024 | tf_op jit(solution)/shard_map/pallas_call | solution.py:85
  67.2 4.1 %all-to-all-done.2 = f32[64,8,128]{2,1,0:T(8,128)} async-done(((f32[64,8,128]{2,1,0:T(8,128)}), f32[64,8,128]{2,1,0:T(8,128)}, u32[]{:S(2)}, u32[]{:S(2)}) %all-to-all-start.2) | async-done | bytes 262176 | tf_op jit(solution)/shard_map/all_to_all | solution.py:379
  71.3 1.6 %shard_map.136.refs_0_ = f32[4,4,8,128]{3,2,1,0:T(8,128)} custom-call(f32[16,4,8,128]{3,2,1,0:T(8,128)} %bitcast.4.parts_ref, f32[8,128]{1,0:T(8,128)S(1)} %get-tuple-element.29.refs_0_), custom_call_target="tpu_custom_call" | custom-call | bytes 331776 | tf_op jit(solution)/shard_map/pallas_call | solution.py:65
  72.9 6.0 %all-to-all-start.3 = ((f32[4,4,8,128]{3,2,1,0:T(8,128)}), f32[4,4,8,128]{3,2,1,0:T(8,128)S(1)}, u32[]{:S(2)}, u32[]{:S(2)}) async-start(f32[4,4,8,128]{3,2,1,0:T(8,128)} %shard_map.136.refs_0_), calls=%async_computation.3 | async-start | bytes 131072 | tf_op jit(solution)/shard_map/all_to_all | solution.py:390
  78.9 1.0 copy-done.8
  80.0 3.0 %shard_map.137 = (f32[256,1024]{1,0:T(8,128)S(1)}, f32[2,128]{1,0:T(2,128)S(1)}) custom-call(f32[4,4,8,128]{3,2,1,0:T(8,128)} %shard_map.136.refs_0_, bf16[384,384]{1,0:T(8,128)(2,1)S(1)} %copy-done.3, bf16[256,1024]{1,0:T(8,128)(2,1)S(1)} %copy-done.8, f32[128,1024]{1,0:T(8,128)} %collective-permute-done.2.refs_3_, f32[128,1024]{1,0:T(8,128)S(1)} %copy-done.1, ...), custom_call_target="tpu_custom_call" | custom-call | flops 603979776 | bytes 1024 | tf_op jit(solution)/shard_map/pallas_call | solution.py:85
  82.9 7.7 %all-to-all-done.3.parts_ref = f32[4,4,8,128]{3,2,1,0:T(8,128)S(1)} async-done(((f32[4,4,8,128]{3,2,1,0:T(8,128)}), f32[4,4,8,128]{3,2,1,0:T(8,128)S(1)}, u32[]{:S(2)}, u32[]{:S(2)}) %all-to-all-start.3) | async-done | bytes 65568 | tf_op jit(solution)/shard_map/all_to_all | solution.py:390
  91.4 3.8 %all-to-all-start.4 = ((f32[16,4,8,128]{3,2,1,0:T(8,128)}), f32[16,4,8,128]{3,2,1,0:T(8,128)S(1)}, u32[]{:S(2)}, u32[]{:S(2)}) async-start(f32[16,4,8,128]{3,2,1,0:T(8,128)} %shard_map.139), calls=%async_computation.4 | async-start | bytes 524288 | tf_op jit(solution)/shard_map/all_to_all | solution.py:402
  95.1 6.0 %psum.15.refs_1_.after_ref = f32[2,128]{1,0:T(2,128)S(1)} all-reduce(f32[2,128]{1,0:T(2,128)S(1)} %get-tuple-element.32.refs_0_), channel_id=1, replica_groups=mesh['y'=4,'zh'=4,'zl'=4,'core'=2,'chan'=4] {'chan'}, use_global_device_ids=true, to_apply=%region_1.0 | all-reduce | flops 256 | bytes 2048 | tf_op jit(solution)/shard_map/psum | solution.py:401
  101.2 2.0 %all-to-all-done.4 = f32[16,4,8,128]{3,2,1,0:T(8,128)S(1)} async-done(((f32[16,4,8,128]{3,2,1,0:T(8,128)}), f32[16,4,8,128]{3,2,1,0:T(8,128)S(1)}, u32[]{:S(2)}, u32[]{:S(2)}) %all-to-all-start.4) | async-done | bytes 262176 | tf_op jit(solution)/shard_map/all_to_all | solution.py:402
  103.2 6.3 %collective-permute-start.3 = (f32[64,8,128]{2,1,0:T(8,128)S(1)}, f32[64,8,128]{2,1,0:T(8,128)S(1)}, u32[]{:S(2)}, u32[]{:S(2)}) collective-permute-start(f32[64,8,128]{2,1,0:T(8,128)S(1)} %shard_map.140.own_ref), channel_id=1, source_target_pairs={{0,4},{4,0},{1,5},{5,1},{2,6},{6,2},{3,7},{7,3},{8,12},{12,8},{9,1... | collective-permute-start | bytes 786440 | tf_op jit(solution)/shard_map/ppermute | solution.py:409
  109.5 1.1 shard_map.138
  (39 shorter events, 4.8 us)
Async XLA Ops:
  0.6 18.8 %copy-start = (bf16[256,1024]{1,0:T(8,128)(2,1)S(1)}, bf16[256,1024]{1,0:T(8,128)(2,1)}, u32[]{:S(2)}) copy-start(bf16[256,1024]{1,0:T(8,128)(2,1)} %refs_3_.3) | copy-start | bytes 1572868
  3.5 27.5 %copy-start.4 = (bf16[256,1024]{1,0:T(8,128)(2,1)S(1)}, bf16[256,1024]{1,0:T(8,128)(2,1)}, u32[]{:S(2)}) copy-start(bf16[256,1024]{1,0:T(8,128)(2,1)} %refs_5_.1) | copy-start | bytes 1572868
  3.5 27.5 %copy-start.12 = (f32[1024]{0:T(1024)S(1)}, f32[1024]{0:T(1024)}, u32[]{:S(2)}) copy-start(f32[1024]{0:T(1024)} %param.11) | copy-start | bytes 12292
  3.5 27.5 %all-to-all-start = ((f32[16,8,128]{2,1,0:T(8,128)}), f32[16,8,128]{2,1,0:T(8,128)S(1)}, u32[]{:S(2)}, u32[]{:S(2)}) async-start(f32[16,8,128]{2,1,0:T(8,128)} %get-tuple-element.20), calls=%async_computation | async-start | bytes 131072 | tf_op jit(solution)/shard_map/all_to_all | solution.py:350
  19.4 29.8 %copy-start.2 = (f32[256,1024]{1,0:T(8,128)S(1)}, f32[256,1024]{1,0:T(8,128)}, u32[]{:S(2)}) copy-start(f32[256,1024]{1,0:T(8,128)} %get-tuple-element.23.refs_3_) | copy-start | bytes 3145732
  31.0 4.8 %copy-start.11 = (f32[1024]{0:T(1024)S(1)}, f32[1024]{0:T(1024)}, u32[]{:S(2)}) copy-start(f32[1024]{0:T(1024)} %param.18) | copy-start | bytes 12292
  31.0 4.8 %copy-start.13 = (f32[1024]{0:T(1024)S(1)}, f32[1024]{0:T(1024)}, u32[]{:S(2)}) copy-start(f32[1024]{0:T(1024)} %param.17) | copy-start | bytes 12292
  31.3 17.9 %copy-start.3 = (bf16[384,384]{1,0:T(8,128)(2,1)S(1)}, bf16[384,384]{1,0:T(8,128)(2,1)}, u32[]{:S(2)}) copy-start(bf16[384,384]{1,0:T(8,128)(2,1)} %constant.4.clone.refs_0_.refs_1_) | copy-start | bytes 884740
  31.3 17.9 %collective-permute-start = (f32[128,1024]{1,0:T(8,128)S(1)}, f32[128,1024]{1,0:T(8,128)S(1)}, u32[]{:S(2)}, u32[]{:S(2)}) collective-permute-start(f32[128,1024]{1,0:T(8,128)S(1)} %get-tuple-element.22), channel_id=1, source_target_pairs={{0,4},{4,8},{8,12},{12,16},{16,20},{20,24},{24,28},{28,32},{32,36}... | collective-permute-start | bytes 1572872 | tf_op jit(solution)/shard_map/ppermute | solution.py:360
  49.2 1.0 copy-start.6
  52.1 0.8 copy-start.14
  52.9 3.5 %copy-start.7 = (bf16[256,1024]{1,0:T(8,128)(2,1)}, bf16[256,1024]{1,0:T(8,128)(2,1)S(1)}, u32[]{:S(2)}) copy-start(bf16[256,1024]{1,0:T(8,128)(2,1)S(1)} %get-tuple-element.30.refs_2_) | copy-start | bytes 1572868
  52.9 3.5 %copy-start.9 = (bf16[128,1024]{1,0:T(8,128)(2,1)}, bf16[128,1024]{1,0:T(8,128)(2,1)S(1)}, u32[]{:S(2)}) copy-start(bf16[128,1024]{1,0:T(8,128)(2,1)S(1)} %get-tuple-element.24.refs_2_) | copy-start | bytes 786436
  52.9 3.5 %collective-permute-start.1 = (f32[8,8,8,128]{3,2,1,0:T(8,128)S(1)}, f32[8,8,8,128]{3,2,1,0:T(8,128)S(1)}, u32[]{:S(2)}, u32[]{:S(2)}) collective-permute-start(f32[8,8,8,128]{3,2,1,0:T(8,128)S(1)} %get-tuple-element.28), channel_id=1, source_target_pairs={{0,4},{4,0},{1,5},{5,1},{2,6},{6,2},{3,7},{7,3},{8,12},{12,8},{9,1... | collective-permute-start | bytes 786440 | tf_op jit(solution)/shard_map/ppermute | solution.py:376
  56.4 7.3 %copy-start.1 = (f32[128,1024]{1,0:T(8,128)S(1)}, f32[128,1024]{1,0:T(8,128)}, u32[]{:S(2)}) copy-start(f32[128,1024]{1,0:T(8,128)} %filter_ref.1) | copy-start | bytes 1572868
  56.4 0.7 copy-start.5
  57.1 14.2 %all-to-all-start.2 = ((f32[64,8,128]{2,1,0:T(8,128)}), f32[64,8,128]{2,1,0:T(8,128)}, u32[]{:S(2)}, u32[]{:S(2)}) async-start(f32[64,8,128]{2,1,0:T(8,128)} %bitcast.9), calls=%async_computation.2 | async-start | bytes 524288 | tf_op jit(solution)/shard_map/all_to_all | solution.py:379
  61.3 17.6 %collective-permute-start.2 = (f32[128,1024]{1,0:T(8,128)}, f32[128,1024]{1,0:T(8,128)}, u32[]{:S(2)}, u32[]{:S(2)}) collective-permute-start(f32[128,1024]{1,0:T(8,128)} %copy-done.14), channel_id=1, source_target_pairs={{4,0},{8,4},{12,8},{16,12},{20,16},{24,20},{28,24},{32,28},{36,32}... | collective-permute-start | bytes 1572872 | tf_op jit(solution)/shard_map/ppermute | solution.py:378
  63.6 1.0 copy-start.10
  72.9 17.7 %all-to-all-start.3 = ((f32[4,4,8,128]{3,2,1,0:T(8,128)}), f32[4,4,8,128]{3,2,1,0:T(8,128)S(1)}, u32[]{:S(2)}, u32[]{:S(2)}) async-start(f32[4,4,8,128]{3,2,1,0:T(8,128)} %shard_map.136.refs_0_), calls=%async_computation.3 | async-start | bytes 131072 | tf_op jit(solution)/shard_map/all_to_all | solution.py:390
  78.9 1.0 copy-start.8
  91.4 11.8 %all-to-all-start.4 = ((f32[16,4,8,128]{3,2,1,0:T(8,128)}), f32[16,4,8,128]{3,2,1,0:T(8,128)S(1)}, u32[]{:S(2)}, u32[]{:S(2)}) async-start(f32[16,4,8,128]{3,2,1,0:T(8,128)} %shard_map.139), calls=%async_computation.4 | async-start | bytes 524288 | tf_op jit(solution)/shard_map/all_to_all | solution.py:402
  103.2 7.4 %collective-permute-start.3 = (f32[64,8,128]{2,1,0:T(8,128)S(1)}, f32[64,8,128]{2,1,0:T(8,128)S(1)}, u32[]{:S(2)}, u32[]{:S(2)}) collective-permute-start(f32[64,8,128]{2,1,0:T(8,128)S(1)} %shard_map.140.own_ref), channel_id=1, source_target_pairs={{0,4},{4,0},{1,5},{5,1},{2,6},{6,2},{3,7},{7,3},{8,12},{12,8},{9,1... | collective-permute-start | bytes 786440 | tf_op jit(solution)/shard_map/ppermute | solution.py:409
